TPU v7x, 32 devices: a whole 2x2x4 slice. The times are simulated.
32 devices in a mesh: ctx: 16 (over z, y, x), fsdp: 2 (over core).
Axes of the slice: x: 2, y: 2, z: 4, core: 2. Of those that a mesh axis runs over, the one named last changes fastest.
Arguments:
- tokens: bfloat16 [2, 2048, 576], P('fsdp', 'ctx'), may hold values from -6 to 6
- cotangent: bfloat16 [2, 2048, 576], P('fsdp', 'ctx'), may hold values from -6 to 6
- norm_attn: bfloat16 [576], P('fsdp'), may hold values from 0.5 to 1.5
- w_query: bfloat16 [576, 576], P('fsdp'), may hold values from -0.25 to 0.25
- w_key: bfloat16 [576, 192], P('fsdp'), may hold values from -0.25 to 0.25
- w_value: bfloat16 [576, 192], P('fsdp'), may hold values from -0.25 to 0.25
- w_out: bfloat16 [576, 576], P('fsdp'), may hold values from -4 to 4
- norm_ffn: bfloat16 [576], P('fsdp'), may hold values from 0.5 to 1.5
- w_gate: bfloat16 [576, 1536], P('fsdp'), may hold values from -0.25 to 0.25
- w_up: bfloat16 [576, 1536], P('fsdp'), may hold values from -0.25 to 0.25
- w_down: bfloat16 [1536, 576], P('fsdp'), may hold values from -0.15625 to 0.15625
Outputs:
- output: bfloat16 [2, 2048, 576], P('fsdp', 'ctx')
- grad_tokens: float32 [2, 2048, 576], P('fsdp', 'ctx')
- grad_norm_attn: float32 [576], P('fsdp')
- grad_w_query: float32 [576, 576], P('fsdp')
- grad_w_key: float32 [576, 192], P('fsdp')
- grad_w_value: float32 [576, 192], P('fsdp')
- grad_w_out: float32 [576, 576], P('fsdp')
- grad_norm_ffn: float32 [576], P('fsdp')
- grad_w_gate: float32 [576, 1536], P('fsdp')
- grad_w_up: float32 [576, 1536], P('fsdp')
- grad_w_down: float32 [1536, 576], P('fsdp')
All inputs are finite; a program needn't handle non-finite values.
Results may differ from a plain program's by a relative error of at most 0.03.
Values may be sent and summed in bfloat16 or wider, within the bound.
A program may use at most 128 MiB of HBM per device.

v0:
```python
import jax
import jax.numpy as jnp
from jax import lax
from jax.sharding import PartitionSpec as P

HEADS = 9
KV_HEADS = 3
HEAD_DIM = 64


norm_eps = 1e-05
rope_base = 10000.0
masked_score = -1e30


def rope_tables(first_pos, length, head_width):
    halfway = head_width // 2
    inverse = rope_base ** (-(jnp.arange(halfway, dtype=jnp.float32) * 2.0 / head_width))
    places = (first_pos + jnp.arange(length, dtype=jnp.int32)).astype(jnp.float32)
    angles = places[:, None] * inverse[None, :]
    return (jnp.cos(angles)[:, None, :], jnp.sin(angles)[:, None, :])


def rotate(values, cosine_table, sine_table):
    halfway = values.shape[-1] // 2
    former = values[..., :halfway]
    latter = values[..., halfway:]
    return jnp.concatenate(
        [former * cosine_table - latter * sine_table, latter * cosine_table + former * sine_table],
        -1,
    )


def unrotate(values, cosine_table, sine_table):
    halfway = values.shape[-1] // 2
    former = values[..., :halfway]
    latter = values[..., halfway:]
    return jnp.concatenate(
        [former * cosine_table + latter * sine_table, latter * cosine_table - former * sine_table],
        -1,
    )


def norm_forward(values, gain):
    factor = lax.rsqrt(jnp.mean(values * values, -1, keepdims=True) + norm_eps)
    normed = values * factor
    return (normed * gain, normed, factor)


def norm_backward(incoming, gain, normed, factor):
    scaled = incoming * gain
    back = factor * (scaled - normed * jnp.mean(scaled * normed, -1, keepdims=True))
    return (back, jnp.sum(incoming * normed, 0))


def times_transposed(left, right):
    return lax.dot_general(
        left, right, (((1,), (1,)), ((), ())), preferred_element_type=jnp.float32
    )


def transposed_times(left, right):
    return lax.dot_general(
        left, right, (((0,), (0,)), ((), ())), preferred_element_type=jnp.float32
    )


def block_span(count_rows):
    span_rows = count_rows
    while span_rows > 1024 and span_rows % 2 == 0:
        span_rows = span_rows // 2
    return span_rows


def over_blocks(count_rows, block_step, initial):
    span_rows = block_span(count_rows)

    def advance(number, carried):
        return block_step(number * span_rows, span_rows, carried)

    return lax.fori_loop(0, count_rows // span_rows, advance, initial)


def split_pair(block_rows, kv_width, groups):
    rows_here = block_rows.shape[0]
    return (
        block_rows[:, :kv_width].reshape(rows_here, groups, -1),
        block_rows[:, kv_width:].reshape(rows_here, groups, -1),
    )


def query_scores(query_matrix, block_keys, positions, key_first, score_scale):
    scores = (
        jnp.einsum("ofxy,efy->fxoe", query_matrix, block_keys, preferred_element_type=jnp.float32)
        * score_scale
    )
    key_places = key_first + jnp.arange(block_keys.shape[0], dtype=jnp.int32)
    allowed = key_places[None, :] <= positions[:, None]
    return (scores, allowed)


def three_parts(values):
    upper = values.astype(jnp.bfloat16)
    rest = values - upper.astype(jnp.float32)
    middle = rest.astype(jnp.bfloat16)
    lower = (rest - middle.astype(jnp.float32)).astype(jnp.bfloat16)
    return jnp.concatenate([upper, middle, lower], 1)


def join_parts(parts, width):
    wide = parts.astype(jnp.float32)
    return wide[:, :width] + (wide[:, width : 2 * width] + wide[:, 2 * width :])


def body(
    tokens, cotangent, norm_attn, w_query, w_key, w_value, w_out, norm_ffn, w_gate, w_up, w_down
):
    gathered = (
        lax.all_gather(norm_attn, "fsdp", axis=0, tiled=True),
        lax.all_gather(w_query, "fsdp", axis=0, tiled=True),
        lax.all_gather(w_key, "fsdp", axis=0, tiled=True),
        lax.all_gather(w_value, "fsdp", axis=0, tiled=True),
        lax.all_gather(w_out, "fsdp", axis=0, tiled=True),
        lax.all_gather(norm_ffn, "fsdp", axis=0, tiled=True),
        lax.all_gather(w_gate, "fsdp", axis=0, tiled=True),
        lax.all_gather(w_up, "fsdp", axis=0, tiled=True),
        lax.all_gather(w_down, "fsdp", axis=0, tiled=True),
    )
    gain_attn, query_w, key_w, value_w, out_w, gain_ffn, gate_w, up_w, down_w = gathered
    gain_attn = gain_attn.astype(jnp.float32)
    gain_ffn = gain_ffn.astype(jnp.float32)
    local_rows = tokens.shape[1]
    model_width = tokens.shape[2]
    groups = KV_HEADS
    repeat = HEADS // KV_HEADS
    kv_width = KV_HEADS * HEAD_DIM
    score_scale = HEAD_DIM ** (-0.5)
    first_pos = lax.axis_index("ctx") * local_rows
    positions = first_pos + jnp.arange(local_rows, dtype=jnp.int32)
    inputs = tokens[0].astype(jnp.float32)
    grad_output = cotangent[0]
    attn_in, normed_one, factor_one = norm_forward(inputs, gain_attn)
    act_one = attn_in.astype(jnp.bfloat16)
    cosine_table, sine_table = rope_tables(first_pos, local_rows, HEAD_DIM)
    query_pre = jnp.dot(act_one, query_w, preferred_element_type=jnp.float32)
    key_pre = jnp.dot(act_one, key_w, preferred_element_type=jnp.float32)
    value_pre = jnp.dot(act_one, value_w, preferred_element_type=jnp.float32)
    query_matrix = rotate(
        query_pre.reshape(local_rows, HEADS, HEAD_DIM), cosine_table, sine_table
    ).astype(jnp.bfloat16)
    query_matrix = query_matrix.reshape(local_rows, groups, repeat, HEAD_DIM)
    keys_here = rotate(
        key_pre.reshape(local_rows, groups, HEAD_DIM), cosine_table, sine_table
    ).astype(jnp.bfloat16)
    values_here = value_pre.reshape(local_rows, groups, HEAD_DIM).astype(jnp.bfloat16)
    packed = jnp.concatenate(
        [keys_here.reshape(local_rows, kv_width), values_here.reshape(local_rows, kv_width)], 1
    )
    stat_start = (
        jnp.full((groups, repeat, local_rows), masked_score, jnp.float32),
        jnp.zeros((groups, repeat, local_rows), jnp.float32),
    )
    arriving = lax.all_gather(packed, "ctx", axis=0, tiled=True)

    def block_step(offset, span_rows, running):
        highest, totals = running
        block_keys, unused_values = split_pair(
            lax.dynamic_slice_in_dim(arriving, offset, span_rows, 0), kv_width, groups
        )
        scores, allowed = query_scores(query_matrix, block_keys, positions, offset, score_scale)
        masked = jnp.where(allowed, scores, masked_score)
        new_high = jnp.maximum(highest, jnp.max(masked, -1))
        weights = jnp.where(allowed, jnp.exp(masked - new_high[..., None]), 0.0)
        return (new_high, totals * jnp.exp(highest - new_high) + jnp.sum(weights, -1))

    highest, totals = over_blocks(arriving.shape[0], block_step, stat_start)
    log_totals = highest + jnp.log(totals)
    head_zeros = jnp.zeros((local_rows, groups, repeat, HEAD_DIM), jnp.float32)
    output_arriving = lax.all_gather(packed, "ctx", axis=0, tiled=True)

    def block_step(offset, span_rows, running):
        block_keys, block_values = split_pair(
            lax.dynamic_slice_in_dim(output_arriving, offset, span_rows, 0), kv_width, groups
        )
        scores, allowed = query_scores(query_matrix, block_keys, positions, offset, score_scale)
        share_portions = jnp.where(allowed, jnp.exp(scores - log_totals[..., None]), 0.0).astype(
            jnp.bfloat16
        )
        return running + jnp.einsum(
            "nmje,enx->jnmx", share_portions, block_values, preferred_element_type=jnp.float32
        )

    attended = over_blocks(output_arriving.shape[0], block_step, head_zeros)
    out_act = attended.reshape(local_rows, model_width).astype(jnp.bfloat16)
    residual = inputs + jnp.dot(out_act, out_w, preferred_element_type=jnp.float32)
    ffn_in, normed_two, factor_two = norm_forward(residual, gain_ffn)
    act_two = ffn_in.astype(jnp.bfloat16)
    gate_pre = jnp.dot(act_two, gate_w, preferred_element_type=jnp.float32)
    upward = jnp.dot(act_two, up_w, preferred_element_type=jnp.float32)
    silu_gate = jax.nn.silu(gate_pre)
    hidden = (silu_gate * upward).astype(jnp.bfloat16)
    result = (residual + jnp.dot(hidden, down_w, preferred_element_type=jnp.float32)).astype(
        jnp.bfloat16
    )
    grad_hidden = times_transposed(grad_output, down_w)
    grad_down_w = transposed_times(hidden, grad_output)
    sigmoid_gate = jax.nn.sigmoid(gate_pre)
    grad_gate = (
        grad_hidden * upward * sigmoid_gate * (1.0 + gate_pre * (1.0 - sigmoid_gate))
    ).astype(jnp.bfloat16)
    grad_upward = (grad_hidden * silu_gate).astype(jnp.bfloat16)
    grad_gate_w = transposed_times(act_two, grad_gate)
    grad_up_w = transposed_times(act_two, grad_upward)
    grad_act_two = times_transposed(grad_gate, gate_w) + times_transposed(grad_upward, up_w)
    back_two, grad_gain_ffn = norm_backward(grad_act_two, gain_ffn, normed_two, factor_two)
    grad_residual = grad_output.astype(jnp.float32) + back_two
    grad_attn = grad_residual.astype(jnp.bfloat16)
    grad_out_w = transposed_times(out_act, grad_attn)
    grad_flat = times_transposed(grad_attn, out_w).astype(jnp.bfloat16)
    head_gradient = grad_flat.reshape(local_rows, groups, repeat, HEAD_DIM)
    row_inner = jnp.sum(head_gradient.astype(jnp.float32) * attended, -1).transpose(1, 2, 0)
    query_arriving = lax.all_gather(packed, "ctx", axis=0, tiled=True)

    def block_step(offset, span_rows, running):
        block_keys, block_values = split_pair(
            lax.dynamic_slice_in_dim(query_arriving, offset, span_rows, 0), kv_width, groups
        )
        scores, allowed = query_scores(query_matrix, block_keys, positions, offset, score_scale)
        share_portions = jnp.where(allowed, jnp.exp(scores - log_totals[..., None]), 0.0)
        grad_shares = jnp.einsum(
            "ofxy,efy->fxoe", head_gradient, block_values, preferred_element_type=jnp.float32
        )
        score_gradient = (share_portions * (grad_shares - row_inner[..., None])).astype(
            jnp.bfloat16
        )
        return running + jnp.einsum(
            "nmje,enx->jnmx", score_gradient, block_keys, preferred_element_type=jnp.float32
        )

    grad_queries = over_blocks(query_arriving.shape[0], block_step, head_zeros) * score_scale
    total_parts = three_parts(log_totals.transpose(2, 0, 1).reshape(local_rows, HEADS))
    inner_parts = three_parts(row_inner.transpose(2, 0, 1).reshape(local_rows, HEADS))
    sent_rows = (query_matrix.reshape(local_rows, model_width), grad_flat, total_parts, inner_parts)
    key_zeros = jnp.zeros((local_rows, groups, HEAD_DIM), jnp.float32)
    query_rows = lax.all_gather(sent_rows[0], "ctx", axis=0, tiled=True)
    grad_rows = lax.all_gather(sent_rows[1], "ctx", axis=0, tiled=True)
    total_split = lax.all_gather(sent_rows[2], "ctx", axis=0, tiled=True)
    inner_split = lax.all_gather(sent_rows[3], "ctx", axis=0, tiled=True)
    arriving_count = query_rows.shape[0]
    overall_rows = join_parts(total_split, HEADS)
    inner_rows = join_parts(inner_split, HEADS)

    def block_step(offset, span_rows, running):
        grad_keys, grad_values = running
        query_block = lax.dynamic_slice_in_dim(query_rows, offset, span_rows, 0).reshape(
            span_rows, groups, repeat, HEAD_DIM
        )
        grad_block = lax.dynamic_slice_in_dim(grad_rows, offset, span_rows, 0).reshape(
            span_rows, groups, repeat, HEAD_DIM
        )
        total_block = (
            lax.dynamic_slice_in_dim(overall_rows, offset, span_rows, 0)
            .reshape(span_rows, groups, repeat)
            .transpose(1, 2, 0)
        )
        inner_block = (
            lax.dynamic_slice_in_dim(inner_rows, offset, span_rows, 0)
            .reshape(span_rows, groups, repeat)
            .transpose(1, 2, 0)
        )
        scores = (
            jnp.einsum("sgrd,tgd->grst", query_block, keys_here, preferred_element_type=jnp.float32)
            * score_scale
        )
        query_places = offset + jnp.arange(span_rows, dtype=jnp.int32)
        allowed = positions[None, :] <= query_places[:, None]
        share_portions = jnp.where(allowed, jnp.exp(scores - total_block[..., None]), 0.0)
        grad_values = grad_values + jnp.einsum(
            "grst,sgrd->tgd",
            share_portions.astype(jnp.bfloat16),
            grad_block,
            preferred_element_type=jnp.float32,
        )
        grad_shares = jnp.einsum(
            "sgrd,tgd->grst", grad_block, values_here, preferred_element_type=jnp.float32
        )
        score_gradient = (share_portions * (grad_shares - inner_block[..., None])).astype(
            jnp.bfloat16
        )
        grad_keys = grad_keys + jnp.einsum(
            "grst,sgrd->tgd", score_gradient, query_block, preferred_element_type=jnp.float32
        )
        return (grad_keys, grad_values)

    grad_keys, grad_values = over_blocks(arriving_count, block_step, (key_zeros, key_zeros))
    grad_keys = grad_keys * score_scale
    grad_query_pre = (
        unrotate(grad_queries.reshape(local_rows, HEADS, HEAD_DIM), cosine_table, sine_table)
        .reshape(local_rows, model_width)
        .astype(jnp.bfloat16)
    )
    grad_key_pre = (
        unrotate(grad_keys, cosine_table, sine_table)
        .reshape(local_rows, kv_width)
        .astype(jnp.bfloat16)
    )
    grad_value_pre = grad_values.reshape(local_rows, kv_width).astype(jnp.bfloat16)
    grad_query_w = transposed_times(act_one, grad_query_pre)
    grad_key_w = transposed_times(act_one, grad_key_pre)
    grad_value_w = transposed_times(act_one, grad_value_pre)
    grad_act_one = (
        times_transposed(grad_query_pre, query_w)
        + times_transposed(grad_key_pre, key_w)
        + times_transposed(grad_value_pre, value_w)
    )
    back_one, grad_gain_attn = norm_backward(grad_act_one, gain_attn, normed_one, factor_one)
    grad_input = grad_residual + back_one
    local_grads = (
        grad_gain_attn,
        grad_query_w,
        grad_key_w,
        grad_value_w,
        grad_out_w,
        grad_gain_ffn,
        grad_gate_w,
        grad_up_w,
        grad_down_w,
    )
    summed = lax.psum(
        (
            local_grads[0],
            local_grads[1],
            local_grads[2],
            local_grads[3],
            local_grads[4],
            local_grads[5],
            local_grads[6],
            local_grads[7],
            local_grads[8],
        ),
        ("ctx", "fsdp"),
    )
    own_index = lax.axis_index("fsdp")
    part_count = lax.axis_size("fsdp")
    shards = tuple(
        (
            lax.dynamic_slice_in_dim(
                summed_one,
                own_index * (summed_one.shape[0] // part_count),
                summed_one.shape[0] // part_count,
                0,
            )
            for summed_one in summed
        )
    )
    return (
        result[None],
        grad_input[None],
        shards[0],
        shards[1],
        shards[2],
        shards[3],
        shards[4],
        shards[5],
        shards[6],
        shards[7],
        shards[8],
    )


def solution(mesh):
    placed = (
        P("fsdp", "ctx", None),
        P("fsdp", "ctx", None),
        P("fsdp"),
        P("fsdp", None),
        P("fsdp", None),
        P("fsdp", None),
        P("fsdp", None),
        P("fsdp"),
        P("fsdp", None),
        P("fsdp", None),
        P("fsdp", None),
    )
    return jax.shard_map(
        body,
        mesh=mesh,
        in_specs=placed,
        out_specs=(
            P("fsdp", "ctx", None),
            P("fsdp", "ctx", None),
            P("fsdp"),
            P("fsdp", None),
            P("fsdp", None),
            P("fsdp", None),
            P("fsdp", None),
            P("fsdp"),
            P("fsdp", None),
            P("fsdp", None),
            P("fsdp", None),
        ),
        check_vma=False,
    )
```

profile of v0, /device:TPU:0, one launch (start us, length us, event | category | flops | bytes accessed | tf_op | source)
XLA Modules:
  0.0 581.1 jit_solution(1046841294438354179)
XLA Ops:
  7.3 1.0 fusion.96
  8.3 1.2 dynamic-slice
  12.0 2.6 all-reduce.4
  14.5 2.2 all_gather.45
  17.6 2.2 all_gather.46
  20.1 1.3 fusion.106
  21.4 1.2 convolution_convert_fusion.1
  25.6 2.3 all_gather.48
  30.4 2.3 all_gather.49
  33.0 50.9 %all-gather.7.cloned.1.call-done = bf16[2048,384]{0,1:T(8,128)(2,1)} async-done(((bf16[128,384]{0,1:T(8,128)(2,1)}), bf16[2048,384]{0,1:T(8,128)(2,1)}) %all-gather.7.cloned.1.call-update) | async-done | bytes 1572880 | tf_op jit(solution)/shard_map/all_gather | solution.py:179
  83.9 6.7 %while.60 = (s32[]{:T(128)}, f32[3,3,128]{2,1,0:T(4,128)S(1)}, f32[3,3,128]{2,1,0:T(4,128)S(1)}, bf16[2048,384]{0,1:T(8,128)(2,1)}, bf16[128,3,3,64]{0,3,2,1:T(8...) while((s32[]{:T(128)}, f32[3,3,128]{2,1,0:T(4,128)S(1)}, ...), condition=%wide.region_4.5_spmd.clone, body=%wide.region_1.4_spmd.clone.sunk | while | flops 160570112 | bytes 11226802 | solution.py:81
  84.1 1.0 constant_dynamic-slice_fusion.18
  85.2 0.9 fusion.210
  86.1 1.1 select_reduce_fusion.2
  87.5 1.0 constant_dynamic-slice_fusion.18
  88.5 0.9 fusion.210
  89.4 1.1 select_reduce_fusion.2
  91.2 7.5 %while.61 = (s32[]{:T(128)}, f32[128,3,3,64]{0,3,2,1:T(8,128)S(1)}, bf16[2048,384]{0,1:T(8,128)(2,1)}, bf16[128,3,3,64]{3,2,1,0:T(4,128)(2,1)S(1)}, f32[3,3,128]...) while((s32[]{:T(128)}, f32[128,3,3,64]{0,3,2,1:T(8,128)S(1)}, ...), condition=%wide.region_6.7_spmd.clone, body=%wide.region_5.6_spmd.clone.sunk | while | flops 306988160 | bytes 3372745 | solution.py:81
  91.4 1.3 constant_dynamic-slice_fusion.19
  92.6 2.3 fusion.216
  95.2 1.2 constant_dynamic-slice_fusion.19
  96.3 2.3 fusion.216
  99.6 2.9 fusion.131
  102.5 4.1 all-gather.9.cloned.1.call-done
  106.6 2.9 fusion.130
  109.5 9.8 %all-gather.13.cloned.1.call-done = bf16[1536,576]{0,1:T(8,128)(2,1)} async-done(((bf16[768,576]{0,1:T(8,128)(2,1)}), bf16[1536,576]{0,1:T(8,128)(2,1)}) %all-gather.13.cloned.1.call-update) | async-done | bytes 1769488 | tf_op jit(solution)/shard_map/all_gather | solution.py:127
  119.3 3.5 multiply_convert_fusion
  123.5 1.3 multiply_reduce_fusion
  125.4 1.0 copy.35
  126.3 1.6 multiply_reduce_fusion.1
  128.2 18.3 %while.62 = (s32[]{:T(128)}, f32[128,3,3,64]{0,3,2,1:T(8,128)}, bf16[2048,384]{0,1:T(8,128)(2,1)S(1)}, bf16[128,3,3,64]{3,2,1,0:T(4,128)(2,1)S(1)}, f32[3,3,128]...) while((s32[]{:T(128)}, f32[128,3,3,64]{0,3,2,1:T(8,128)}, ...), condition=%wide.region_11.12_spmd.clone, body=%wide.region_10.11_spmd.clone.sunk | while | flops 460342400 | bytes 13355225 | solution.py:81
  129.1 2.9 fusion.224
  132.0 5.3 fusion.225
  138.2 2.9 fusion.224
  141.1 5.4 fusion.225
  148.0 42.3 %all_gather.55 = bf16[2048,27]{0,1:T(8,128)(2,1)S(1)} all-gather(bf16[128,27]{0,1:T(8,128)(2,1)S(1)} %pad_maximum_fusion.3), channel_id=1, replica_groups=mesh['ctx'=16,'fsdp'=2] {'ctx'}, dimensions={0}, use_global_device_ids=true | all-gather | bytes 117504 | tf_op jit(solution)/shard_map/all_gather | solution.py:247
  190.4 36.3 %all_gather.57 = bf16[2048,27]{0,1:T(8,128)(2,1)S(1)} all-gather(bf16[128,27]{0,1:T(8,128)(2,1)S(1)} %pad_maximum_fusion.4), channel_id=1, replica_groups=mesh['ctx'=16,'fsdp'=2] {'ctx'}, dimensions={0}, use_global_device_ids=true | all-gather | bytes 117504 | tf_op jit(solution)/shard_map/all_gather | solution.py:248
  226.7 1.0 broadcast_multiply_fusion
  228.5 2.2 fusion.112
  230.8 1.5 fusion.116
  232.3 2.4 fusion.134
  234.6 2.4 fusion.133
  237.1 2.4 fusion.99
  240.1 19.5 %all-gather.17.cloned.1.call-done = bf16[2048,576]{0,1:T(8,128)(2,1)} async-done(((bf16[128,576]{0,1:T(8,128)(2,1)}), bf16[2048,576]{0,1:T(8,128)(2,1)}) %all-gather.17.cloned.1.call-update) | async-done | bytes 2359312 | tf_op jit(solution)/shard_map/all_gather | solution.py:246
  259.7 35.9 %while.63 = (s32[]{:T(128)}, f32[128,3,64]{0,2,1:T(8,128)}, f32[128,3,64]{0,2,1:T(8,128)}, bf16[2048,576]{0,1:T(8,128)(2,1)}, bf16[128,3,64]{0,2,1:T(8,128)(2,1)...) while((s32[]{:T(128)}, f32[128,3,64]{0,2,1:T(8,128)}, ...), condition=%wide.region_13.14_spmd.clone, body=%wide.region_12.13_spmd.clone.sunk | while | flops 616006784 | bytes 25040112 | solution.py:81
  261.4 1.8 constant_dynamic-slice_fusion.20
  263.3 3.1 fusion.234
  266.4 6.3 %fusion.235 = f32[128,3,64]{0,2,1:T(8,128)} fusion(bf16[1024,3,3,64]{0,3,2,1:T(8,128)(2,1)S(1)} %bitcast.325, f32[3,1024,3,128]{3,1,2,0:T(8,128)} %fusion.234, f32[3,3,1024]{2,1,0:T(4,128)S(1)} %bitcast.347, f32[3,3,1024]{2,1,0:T(4,128)S(1)} %bitcast.345, pred[1024,128]{1,0:T(8,128)(4,1)S(1)} %broadcast_compare_fusion.11, ...), kind=kOutput, calls=%fused_computation.65.clone.1 | convolution fusion | flops 309116928 | bytes 7528449 | tf_op jit(solution)/shard_map/while/body/eval_jaxpr/grst,sgrd->tgd/dot_general | solution.py:290
  272.7 4.9 fusion.236
  279.4 1.8 constant_dynamic-slice_fusion.20
  281.3 3.1 fusion.234
  284.3 6.3 %fusion.235 = f32[128,3,64]{0,2,1:T(8,128)} fusion(bf16[1024,3,3,64]{0,3,2,1:T(8,128)(2,1)S(1)} %bitcast.325, f32[3,1024,3,128]{3,1,2,0:T(8,128)} %fusion.234, f32[3,3,1024]{2,1,0:T(4,128)S(1)} %bitcast.347, f32[3,3,1024]{2,1,0:T(4,128)S(1)} %bitcast.345, pred[1024,128]{1,0:T(8,128)(4,1)S(1)} %broadcast_compare_fusion.11, ...), kind=kOutput, calls=%fused_computation.65.clone.1 | convolution fusion | flops 309116928 | bytes 7528449 | tf_op jit(solution)/shard_map/while/body/eval_jaxpr/grst,sgrd->tgd/dot_general | solution.py:290
  290.7 4.9 fusion.236
  295.6 0.9 convert_element_type.223
  298.2 1.8 fusion.110
  300.0 1.8 fusion.108
  301.8 0.9 copy-done.16
  302.7 2.8 fusion.83
  306.5 40.4 %all-reduce.2 = (f32[576]{0:T(1024)S(1)}, f32[576]{0:T(1024)S(1)}) all-reduce(f32[576]{0:T(1024)S(1)} %get-tuple-element.709, f32[576]{0:T(1024)S(1)} %copy-done.38), channel_id=1, replica_groups=mesh['ctx'=16,'fsdp'=2] {'ctx','fsdp'}, use_global_device_ids=true, to_apply=%region_16.17 | all-reduce | flops 1152 | bytes 9216 | tf_op jit(solution)/shard_map/psum | solution.py:329
  349.1 215.5 %all-reduce.7.cloned.1.call-done = (f32[576,576]{1,0:T(8,128)}, f32[576,192]{1,0:T(8,128)}, f32[576,192]{1,0:T(8,128)}, f32[576,576]{1,0:T(8,128)}, f32[576,1536...) async-done(((f32[576,576]{1,0:T(8,128)}, f32[576,192]{1,0:T(8,128)}, f32[576,192]{1,0:T(8,128)}, f32[576,576]{1,0:T(8,128)}, f32[576,1536]{1,0:T(8,128)}, ...) | async-done | bytes 14155792 | tf_op jit(solution)/shard_map/psum | solution.py:329
  564.6 2.7 constant_dynamic-slice_fusion.10
  567.3 1.9 constant_dynamic-slice_fusion.11
  569.2 3.8 constant_dynamic-slice_fusion.8
  573.0 1.3 constant_dynamic-slice_fusion.7
  (192 shorter events, 25.1 us)
Async XLA Ops:
  7.2 18.5 %copy-start.32 = (bf16[288,576]{1,0:T(8,128)(2,1)S(1)}, bf16[288,576]{1,0:T(8,128)(2,1)}, u32[]{:S(2)}) copy-start(bf16[288,576]{1,0:T(8,128)(2,1)} %param.22) | copy-start | bytes 995332
  7.2 76.7 %all-gather.7.cloned.1.call-start = ((), (), s32[]{:S(2)}) async-start(), calls=%async_computation | async-start | bytes 1671168 | tf_op jit(solution)/shard_map/all_gather | solution.py:179
  8.3 20.0 %copy-start.36 = (f32[128]{0:T(128)}, f32[128]{0:T(128)S(1)}, u32[]{:S(2)}) copy-start(f32[128]{0:T(128)S(1)} %add_rsqrt_fusion.1) | copy-start | bytes 1540
  14.5 13.8 %copy-start.34 = (f32[576]{0:T(1024)}, f32[576]{0:T(1024)S(1)}, u32[]{:S(2)}) copy-start(f32[576]{0:T(1024)S(1)} %convert_element_type.187) | copy-start | bytes 6916
  16.8 0.7 copy-start.12
  19.9 5.7 copy-start.10
  20.1 8.3 %copy-start.1 = (bf16[1,128,576]{1,2,0:T(8,128)(2,1)S(1)}, bf16[1,128,576]{1,2,0:T(8,128)(2,1)}, u32[]{:S(2)}) copy-start(bf16[1,128,576]{1,2,0:T(8,128)(2,1)} %param.19) | copy-start | bytes 442372
  22.8 6.1 %copy-start.31 = (f32[128,32]{0,1:T(8,128)}, f32[128,32]{0,1:T(8,128)S(1)}, u32[]{:S(2)}) copy-start(f32[128,32]{0,1:T(8,128)S(1)} %get-tuple-element.810) | copy-start | bytes 49156
  23.5 76.1 %all-gather.11.cloned.1.call-start = ((), (), s32[]{:S(2)}) async-start(), calls=%async_computation.2 | async-start | bytes 2654208 | tf_op jit(solution)/shard_map/all_gather | solution.py:126
  24.3 6.2 %copy-start.33 = (bf16[288,576]{1,0:T(8,128)(2,1)S(1)}, bf16[288,576]{1,0:T(8,128)(2,1)}, u32[]{:S(2)}) copy-start(bf16[288,576]{1,0:T(8,128)(2,1)} %param.25) | copy-start | bytes 995332
  24.3 82.3 %all-gather.9.cloned.1.call-start = ((), (), s32[]{:S(2)}) async-start(), calls=%async_computation.1 | async-start | bytes 2654208 | tf_op jit(solution)/shard_map/all_gather | solution.py:125
  25.0 94.3 %all-gather.13.cloned.1.call-start = ((), (), s32[]{:S(2)}) async-start(), calls=%async_computation.3 | async-start | bytes 2654208 | tf_op jit(solution)/shard_map/all_gather | solution.py:127
  25.6 214.6 %all-gather.15.cloned.1.call-start = ((), (), s32[]{:S(2)}) async-start(), calls=%async_computation.4 | async-start | bytes 2506752 | tf_op jit(solution)/shard_map/all_gather | solution.py:245
  28.0 4.8 copy-start.6
  29.6 230.1 %all-gather.17.cloned.1.call-start = ((), (), s32[]{:S(2)}) async-start(), calls=%async_computation.5 | async-start | bytes 2506752 | tf_op jit(solution)/shard_map/all_gather | solution.py:246
  32.8 66.0 %copy-start.4 = (bf16[576,576]{1,0:T(8,128)(2,1)}, bf16[576,576]{1,0:T(8,128)(2,1)S(1)}, u32[]{:S(2)}) copy-start(bf16[576,576]{1,0:T(8,128)(2,1)S(1)} %all_gather.49) | copy-start | bytes 1990660
  98.7 7.9 %copy-start.26 = (f32[128,3,3,64]{0,3,2,1:T(8,128)}, f32[128,3,3,64]{0,3,2,1:T(8,128)S(1)}, u32[]{:S(2)}) copy-start(f32[128,3,3,64]{0,3,2,1:T(8,128)S(1)} %get-tuple-element.541) | copy-start | bytes 884740
  98.7 0.7 copy-start.23
  98.8 20.6 %copy-start.29 = (bf16[1,128,576]{1,2,0:T(8,128)(2,1)S(1)}, bf16[1,128,576]{1,2,0:T(8,128)(2,1)}, u32[]{:S(2)}) copy-start(bf16[1,128,576]{1,2,0:T(8,128)(2,1)} %param.20) | copy-start | bytes 442372
  99.6 23.2 %copy-start.8 = (bf16[128,576]{0,1:T(8,128)(2,1)}, bf16[128,576]{0,1:T(8,128)(2,1)S(1)}, u32[]{:S(2)}) copy-start(bf16[128,576]{0,1:T(8,128)(2,1)S(1)} %multiply_convert_fusion.3) | copy-start | bytes 442372
  109.5 13.4 %copy-start.2 = (bf16[576,1536]{1,0:T(8,128)(2,1)S(1)}, bf16[576,1536]{1,0:T(8,128)(2,1)}, u32[]{:S(2)}) copy-start(bf16[576,1536]{1,0:T(8,128)(2,1)} %all-gather.9.cloned.1.call-done) | copy-start | bytes 5308420
  119.3 4.2 copy-start.3
  122.8 2.0 copy-start.19
  122.8 2.5 copy-start.17
  122.8 2.1 copy-start.5
  123.5 4.7 copy-start
  125.4 2.6 copy-start.14
  128.0 436.6 %all-reduce.7.cloned.1.call-start = ((), (), s32[]{:S(2)}) async-start(), calls=%async_computation.6 | async-start | bytes 29491200 | tf_op jit(solution)/shard_map/psum | solution.py:329
  146.5 84.3 %copy-start.24 = (bf16[128,3,3,64]{0,3,2,1:T(8,128)(2,1)S(1)}, bf16[128,3,3,64]{0,3,2,1:T(8,128)(2,1)}, u32[]{:S(2)}) copy-start(bf16[128,3,3,64]{0,3,2,1:T(8,128)(2,1)} %copy-done.23) | copy-start | bytes 442372
  146.5 85.7 %copy-start.9 = (bf16[128,576]{0,1:T(8,128)(2,1)S(1)}, bf16[128,576]{0,1:T(8,128)(2,1)}, u32[]{:S(2)}) copy-start(bf16[128,576]{0,1:T(8,128)(2,1)} %copy-done.8) | copy-start | bytes 442372
  146.5 85.7 %copy-start.20 = (bf16[128,1536]{1,0:T(8,128)(2,1)S(1)}, bf16[128,1536]{1,0:T(8,128)(2,1)}, u32[]{:S(2)}) copy-start(bf16[128,1536]{1,0:T(8,128)(2,1)} %copy-done.19) | copy-start | bytes 1179652
  228.5 6.1 %copy-start.21 = (bf16[128,9,64]{0,2,1:T(8,128)(2,1)}, bf16[128,9,64]{0,2,1:T(8,128)(2,1)S(1)}, u32[]{:S(2)}) copy-start(bf16[128,9,64]{0,2,1:T(8,128)(2,1)S(1)} %maximum_convert_fusion) | copy-start | bytes 442372
  228.5 6.1 %copy-start.18 = (bf16[128,1536]{1,0:T(8,128)(2,1)S(1)}, bf16[128,1536]{1,0:T(8,128)(2,1)}, u32[]{:S(2)}) copy-start(bf16[128,1536]{1,0:T(8,128)(2,1)} %copy-done.17) | copy-start | bytes 1179652
  232.2 4.8 copy-start.15
  232.2 4.8 copy-start.30
  263.3 3.1 copy-start.25
  281.2 3.1 copy-start.25
  301.7 1.0 copy-start.16
  301.7 3.8 copy-start.7
  301.7 3.8 copy-start.22
  301.8 4.1 copy-start.13
  301.8 4.3 copy-start.11
  301.8 4.3 copy-start.35
  301.8 4.3 copy-start.37
  301.8 4.7 copy-start.38
  564.6 4.6 copy-start.27
  569.2 3.8 copy-start.28
Sparse Core Ops, SparseCore 0:
  23.6 60.2 all-gather.6
  85.4 8.2 all-gather.10
  95.3 11.2 all-gather.8
  108.0 11.2 all-gather.12
  122.4 68.8 all-gather.14
  193.9 65.7 all-gather.16
  301.9 262.6 all-reduce.6
where the time goes:
time: 582 us; the launch traced here: 581 us
  waiting for transfers between devices  302 us (52%)
  blocking collectives  131 us (23%)
  matrix products  84.9 us (15%)
  local copies, waits for them, and re-layouts  31.4 us (5%)
  other arithmetic  16.2 us (3%)
  between operations  15.4 us (3%)
    psum x1, waiting for transfers between devices, body(): lax.psum((local_grads[0], local_grads[1], local_grads[2], local_grads[3],...  216 us
    all_gather x1, waiting for transfers between devices, body(): output_arriving = lax.all_gather(packed, 'ctx', axis=0, tiled=True)  50.9 us
    all_gather x1, blocking collectives, body(): total_split = lax.all_gather(sent_rows[2], 'ctx', axis=0, tiled=True)  42.3 us
    psum x1, blocking collectives, body(): lax.psum((local_grads[0], local_grads[1], local_grads[2], local_grads[3],...  40.4 us
    all_gather x1, blocking collectives, body(): inner_split = lax.all_gather(sent_rows[3], 'ctx', axis=0, tiled=True)  36.3 us
    all_gather x1, waiting for transfers between devices, body(): grad_rows = lax.all_gather(sent_rows[1], 'ctx', axis=0, tiled=True)  19.5 us
    dot_general x7, matrix products, transposed_times(): lax.dot_general(left, right, (((0,), (0,)), ((), ())), preferred_element_...  14.4 us
    dot_general x2, matrix products, block_step(): jnp.einsum('grst,sgrd->tgd', score_gradient, query_block, preferred_eleme...  12.7 us
  transfers between devices with their start and end apart: 7, of which 5 were waited for; matrix products, arithmetic and copies ran while one was open for 12% of the time, Pallas kernels for 0%

commit v1 on v0

v1 whole, which is shorter than its diff:
```python
import functools

import jax
import jax.numpy as jnp
from jax import lax
from jax.experimental import pallas as pl
from jax.experimental.pallas import tpu as pltpu
from jax.sharding import PartitionSpec as P

HEADS = 9
KV_HEADS = 3
HEAD_DIM = 64


norm_eps = 1e-05
rope_base = 10000.0
masked_score = -1e30


def rope_tables(first_pos, length, head_width):
    halfway = head_width // 2
    inverse = rope_base ** (-(jnp.arange(halfway, dtype=jnp.float32) * 2.0 / head_width))
    places = (first_pos + jnp.arange(length, dtype=jnp.int32)).astype(jnp.float32)
    angles = places[:, None] * inverse[None, :]
    return (jnp.cos(angles)[:, None, :], jnp.sin(angles)[:, None, :])


def rotate(values, cosine_table, sine_table):
    halfway = values.shape[-1] // 2
    former = values[..., :halfway]
    latter = values[..., halfway:]
    return jnp.concatenate(
        [former * cosine_table - latter * sine_table, latter * cosine_table + former * sine_table],
        -1,
    )


def unrotate(values, cosine_table, sine_table):
    halfway = values.shape[-1] // 2
    former = values[..., :halfway]
    latter = values[..., halfway:]
    return jnp.concatenate(
        [former * cosine_table + latter * sine_table, latter * cosine_table - former * sine_table],
        -1,
    )


def norm_forward(values, gain):
    factor = lax.rsqrt(jnp.mean(values * values, -1, keepdims=True) + norm_eps)
    normed = values * factor
    return (normed * gain, normed, factor)


def norm_backward(incoming, gain, normed, factor):
    scaled = incoming * gain
    back = factor * (scaled - normed * jnp.mean(scaled * normed, -1, keepdims=True))
    return (back, jnp.sum(incoming * normed, 0))


def times_transposed(left, right):
    return lax.dot_general(
        left, right, (((1,), (1,)), ((), ())), preferred_element_type=jnp.float32
    )


def transposed_times(left, right):
    return lax.dot_general(
        left, right, (((0,), (0,)), ((), ())), preferred_element_type=jnp.float32
    )


def block_span(count_rows):
    span_rows = count_rows
    while span_rows > 512 and span_rows % 2 == 0:
        span_rows = span_rows // 2
    return span_rows


def split_pair(block_rows, kv_width, groups):
    rows_here = block_rows.shape[0]
    return (
        block_rows[:, :kv_width].reshape(rows_here, groups, -1),
        block_rows[:, kv_width:].reshape(rows_here, groups, -1),
    )


def reduce_grads(partials):
    own_index = lax.axis_index("fsdp")
    part_count = lax.axis_size("fsdp")
    halves = []
    for partial in partials:
        rows = partial.shape[0] // part_count
        own = lax.dynamic_slice_in_dim(partial, own_index * rows, rows, 0)
        for shift in range(1, part_count):
            other = lax.rem(own_index + shift, part_count)
            sent = lax.dynamic_slice_in_dim(partial, other * rows, rows, 0).astype(jnp.bfloat16)
            moves = [(a, (a + shift) % part_count) for a in range(part_count)]
            own = own + lax.ppermute(sent, "fsdp", moves).astype(jnp.float32)
        halves.append(own.astype(jnp.bfloat16))
    return tuple(h.astype(jnp.float32) for h in lax.psum(tuple(halves), "ctx"))


def heads_stacked(ref, group, repeat):
    first = group * repeat * HEAD_DIM
    return jnp.concatenate(
        [ref[:, first + r * HEAD_DIM : first + (r + 1) * HEAD_DIM] for r in range(repeat)], 0
    )


def heads_beside(transposed, repeat):
    rows = transposed.shape[1] // repeat
    back = transposed.T
    return jnp.concatenate([back[r * rows : (r + 1) * rows] for r in range(repeat)], 1)


def allowed_pairs(first_ref, key_first, keys, rows, repeat):
    key_place = lax.broadcasted_iota(jnp.int32, (keys, repeat * rows), 0)
    query_place = lax.rem(lax.broadcasted_iota(jnp.int32, (keys, repeat * rows), 1), rows)
    return key_place - query_place <= first_ref[0] - key_first


def forward_kernel(first_ref, query_ref, pair_ref, out_ref, log_ref, high_ref, total_ref, sum_ref):
    block, blocks = pl.program_id(0), pl.num_programs(0)
    keys, rows = pair_ref.shape[0], query_ref.shape[0]
    repeat = HEADS // KV_HEADS
    kv_width = KV_HEADS * HEAD_DIM

    @pl.when(block == 0)
    def _():
        high_ref[...] = jnp.full_like(high_ref, masked_score)
        total_ref[...] = jnp.zeros_like(total_ref)
        sum_ref[...] = jnp.zeros_like(sum_ref)

    allowed = allowed_pairs(first_ref, block * keys, keys, rows, repeat)
    for group in range(KV_HEADS):
        stacked = heads_stacked(query_ref, group, repeat)
        k = pair_ref[:, group * HEAD_DIM : (group + 1) * HEAD_DIM]
        v = pair_ref[:, kv_width + group * HEAD_DIM : kv_width + (group + 1) * HEAD_DIM]
        scores = jnp.where(allowed, times_transposed(k, stacked), masked_score)
        old_high = high_ref[group : group + 1, :]
        new_high = jnp.maximum(old_high, jnp.max(scores, 0, keepdims=True))
        weights = jnp.exp(scores - new_high)
        keep = jnp.exp(old_high - new_high)
        total = total_ref[group : group + 1, :] * keep + jnp.sum(weights, 0, keepdims=True)
        summed = sum_ref[group] * keep + transposed_times(v, weights.astype(jnp.bfloat16))
        high_ref[group : group + 1, :] = new_high
        total_ref[group : group + 1, :] = total
        sum_ref[group] = summed

        @pl.when(block == blocks - 1)
        def _():
            log_ref[group : group + 1, :] = new_high + jnp.log(total)
            width = repeat * HEAD_DIM
            out_ref[:, group * width : (group + 1) * width] = heads_beside(summed / total, repeat)


def backward_kernel(
    first_ref, query_ref, grad_ref, out_ref, log_ref, pair_ref, dq_ref, dpair_ref, sum_ref
):
    block, blocks = pl.program_id(0), pl.num_programs(0)
    keys, rows = pair_ref.shape[0], query_ref.shape[0]
    repeat = HEADS // KV_HEADS
    kv_width = KV_HEADS * HEAD_DIM

    @pl.when(block == 0)
    def _():
        sum_ref[...] = jnp.zeros_like(sum_ref)

    allowed = allowed_pairs(first_ref, block * keys, keys, rows, repeat)
    key_parts, value_parts = [], []
    for group in range(KV_HEADS):
        stacked = heads_stacked(query_ref, group, repeat)
        grads = heads_stacked(grad_ref, group, repeat)
        outs = heads_stacked(out_ref, group, repeat)
        inner = jnp.sum((grads.astype(jnp.float32) * outs).T, 0, keepdims=True)
        k = pair_ref[:, group * HEAD_DIM : (group + 1) * HEAD_DIM]
        v = pair_ref[:, kv_width + group * HEAD_DIM : kv_width + (group + 1) * HEAD_DIM]
        scores = times_transposed(k, stacked)
        shares = jnp.where(allowed, jnp.exp(scores - log_ref[group : group + 1, :]), 0.0)
        score_grads = (shares * (times_transposed(v, grads) - inner)).astype(jnp.bfloat16)
        value_parts.append(
            jnp.dot(shares.astype(jnp.bfloat16), grads, preferred_element_type=jnp.float32)
        )
        key_parts.append(jnp.dot(score_grads, stacked, preferred_element_type=jnp.float32))
        summed = sum_ref[group] + transposed_times(k, score_grads)
        sum_ref[group] = summed

        @pl.when(block == blocks - 1)
        def _():
            width = repeat * HEAD_DIM
            dq_ref[:, group * width : (group + 1) * width] = heads_beside(summed, repeat)

    dpair_ref[...] = jnp.concatenate(key_parts + value_parts, 1).astype(dpair_ref.dtype)


def whole_block(shape):
    return pl.BlockSpec(shape, lambda b: (0,) * len(shape))


def attention_forward(first_place, queries, pair):
    rows, width = queries.shape
    keys = block_span(pair.shape[0])
    columns = (HEADS // KV_HEADS) * rows
    return pl.pallas_call(
        forward_kernel,
        grid=(pair.shape[0] // keys,),
        in_specs=[
            pl.BlockSpec(memory_space=pltpu.SMEM),
            whole_block((rows, width)),
            pl.BlockSpec((keys, pair.shape[1]), lambda b: (b, 0)),
        ],
        out_specs=[whole_block((rows, width)), whole_block((KV_HEADS, columns))],
        out_shape=[
            jax.ShapeDtypeStruct((rows, width), jnp.float32),
            jax.ShapeDtypeStruct((KV_HEADS, columns), jnp.float32),
        ],
        scratch_shapes=[
            pltpu.VMEM((KV_HEADS, columns), jnp.float32),
            pltpu.VMEM((KV_HEADS, columns), jnp.float32),
            pltpu.VMEM((KV_HEADS, HEAD_DIM, columns), jnp.float32),
        ],
        compiler_params=pltpu.CompilerParams(vmem_limit_bytes=40 * 1024 * 1024),
    )(first_place, queries, pair)


def attention_backward(first_place, queries, grads, outs, logs, pair):
    rows, width = queries.shape
    keys = block_span(pair.shape[0])
    columns = (HEADS // KV_HEADS) * rows
    return pl.pallas_call(
        backward_kernel,
        grid=(pair.shape[0] // keys,),
        in_specs=[
            pl.BlockSpec(memory_space=pltpu.SMEM),
            whole_block((rows, width)),
            whole_block((rows, width)),
            whole_block((rows, width)),
            whole_block((KV_HEADS, columns)),
            pl.BlockSpec((keys, pair.shape[1]), lambda b: (b, 0)),
        ],
        out_specs=[
            whole_block((rows, width)),
            pl.BlockSpec((keys, pair.shape[1]), lambda b: (b, 0)),
        ],
        out_shape=[
            jax.ShapeDtypeStruct((rows, width), jnp.float32),
            jax.ShapeDtypeStruct(pair.shape, jnp.bfloat16),
        ],
        scratch_shapes=[pltpu.VMEM((KV_HEADS, HEAD_DIM, columns), jnp.float32)],
        compiler_params=pltpu.CompilerParams(vmem_limit_bytes=40 * 1024 * 1024),
    )(first_place, queries, grads, outs, logs, pair)


def body(
    tokens, cotangent, norm_attn, w_query, w_key, w_value, w_out, norm_ffn, w_gate, w_up, w_down
):
    gathered = (
        lax.all_gather(norm_attn, "fsdp", axis=0, tiled=True),
        lax.all_gather(w_query, "fsdp", axis=0, tiled=True),
        lax.all_gather(w_key, "fsdp", axis=0, tiled=True),
        lax.all_gather(w_value, "fsdp", axis=0, tiled=True),
        lax.all_gather(w_out, "fsdp", axis=0, tiled=True),
        lax.all_gather(norm_ffn, "fsdp", axis=0, tiled=True),
        lax.all_gather(w_gate, "fsdp", axis=0, tiled=True),
        lax.all_gather(w_up, "fsdp", axis=0, tiled=True),
        lax.all_gather(w_down, "fsdp", axis=0, tiled=True),
    )
    gain_attn, query_w, key_w, value_w, out_w, gain_ffn, gate_w, up_w, down_w = gathered
    gain_attn = gain_attn.astype(jnp.float32)
    gain_ffn = gain_ffn.astype(jnp.float32)
    local_rows = tokens.shape[1]
    model_width = tokens.shape[2]
    groups = KV_HEADS
    repeat = HEADS // KV_HEADS
    kv_width = KV_HEADS * HEAD_DIM
    score_scale = HEAD_DIM ** (-0.5)
    first_pos = lax.axis_index("ctx") * local_rows
    inputs = tokens[0].astype(jnp.float32)
    grad_output = cotangent[0]
    attn_in, normed_one, factor_one = norm_forward(inputs, gain_attn)
    act_one = attn_in.astype(jnp.bfloat16)
    cosine_table, sine_table = rope_tables(first_pos, local_rows, HEAD_DIM)
    query_pre = jnp.dot(act_one, query_w, preferred_element_type=jnp.float32)
    key_pre = jnp.dot(act_one, key_w, preferred_element_type=jnp.float32)
    value_pre = jnp.dot(act_one, value_w, preferred_element_type=jnp.float32)
    query_matrix = rotate(
        query_pre.reshape(local_rows, HEADS, HEAD_DIM), cosine_table, sine_table
    ).astype(jnp.bfloat16)
    query_matrix = query_matrix.reshape(local_rows, groups, repeat, HEAD_DIM)
    keys_here = rotate(
        key_pre.reshape(local_rows, groups, HEAD_DIM), cosine_table, sine_table
    ).astype(jnp.bfloat16)
    values_here = value_pre.reshape(local_rows, groups, HEAD_DIM).astype(jnp.bfloat16)
    packed = jnp.concatenate(
        [keys_here.reshape(local_rows, kv_width), values_here.reshape(local_rows, kv_width)], 1
    )
    arriving = lax.all_gather(packed, "ctx", axis=0, tiled=True)
    all_rows = arriving.shape[0]
    scaled_queries = (
        query_matrix.reshape(local_rows, model_width) * jnp.bfloat16(score_scale)
    )
    first_place = first_pos.astype(jnp.int32).reshape(1)
    attended, log_totals = attention_forward(first_place, scaled_queries, arriving)
    out_act = attended.reshape(local_rows, model_width).astype(jnp.bfloat16)
    residual = inputs + jnp.dot(out_act, out_w, preferred_element_type=jnp.float32)
    ffn_in, normed_two, factor_two = norm_forward(residual, gain_ffn)
    act_two = ffn_in.astype(jnp.bfloat16)
    gate_pre = jnp.dot(act_two, gate_w, preferred_element_type=jnp.float32)
    upward = jnp.dot(act_two, up_w, preferred_element_type=jnp.float32)
    silu_gate = jax.nn.silu(gate_pre)
    hidden = (silu_gate * upward).astype(jnp.bfloat16)
    result = (residual + jnp.dot(hidden, down_w, preferred_element_type=jnp.float32)).astype(
        jnp.bfloat16
    )
    grad_hidden = times_transposed(grad_output, down_w)
    grad_down_w = transposed_times(hidden, grad_output)
    sigmoid_gate = jax.nn.sigmoid(gate_pre)
    grad_gate = (
        grad_hidden * upward * sigmoid_gate * (1.0 + gate_pre * (1.0 - sigmoid_gate))
    ).astype(jnp.bfloat16)
    grad_upward = (grad_hidden * silu_gate).astype(jnp.bfloat16)
    grad_gate_w = transposed_times(act_two, grad_gate)
    grad_up_w = transposed_times(act_two, grad_upward)
    grad_act_two = times_transposed(grad_gate, gate_w) + times_transposed(grad_upward, up_w)
    back_two, grad_gain_ffn = norm_backward(grad_act_two, gain_ffn, normed_two, factor_two)
    grad_residual = grad_output.astype(jnp.float32) + back_two
    grad_attn = grad_residual.astype(jnp.bfloat16)
    grad_out_w = transposed_times(out_act, grad_attn)
    reduce_early = reduce_grads((grad_gate_w, grad_up_w, grad_down_w, grad_out_w))
    grad_flat = times_transposed(grad_attn, out_w).astype(jnp.bfloat16)
    grad_queries, partial_pair = attention_backward(
        first_place, scaled_queries, grad_flat, attended, log_totals, arriving
    )
    grad_queries = grad_queries * score_scale
    summed_pair = lax.psum_scatter(partial_pair, "ctx", scatter_dimension=0, tiled=True)
    grad_keys, grad_values = split_pair(summed_pair.astype(jnp.float32), kv_width, groups)
    grad_query_pre = (
        unrotate(grad_queries.reshape(local_rows, HEADS, HEAD_DIM), cosine_table, sine_table)
        .reshape(local_rows, model_width)
        .astype(jnp.bfloat16)
    )
    grad_key_pre = (
        unrotate(grad_keys, cosine_table, sine_table)
        .reshape(local_rows, kv_width)
        .astype(jnp.bfloat16)
    )
    grad_value_pre = grad_values.reshape(local_rows, kv_width).astype(jnp.bfloat16)
    grad_query_w = transposed_times(act_one, grad_query_pre)
    grad_key_w = transposed_times(act_one, grad_key_pre)
    grad_value_w = transposed_times(act_one, grad_value_pre)
    grad_act_one = (
        times_transposed(grad_query_pre, query_w)
        + times_transposed(grad_key_pre, key_w)
        + times_transposed(grad_value_pre, value_w)
    )
    back_one, grad_gain_attn = norm_backward(grad_act_one, gain_attn, normed_one, factor_one)
    grad_input = grad_residual + back_one
    reduce_early, late_grads = lax.optimization_barrier(
        (
            reduce_early,
            (grad_query_w, grad_key_w, grad_value_w, grad_gain_attn, grad_gain_ffn),
        )
    )
    shards = reduce_early + reduce_grads(late_grads)
    return (
        result[None],
        grad_input[None],
        shards[7],
        shards[4],
        shards[5],
        shards[6],
        shards[3],
        shards[8],
        shards[0],
        shards[1],
        shards[2],
    )


def solution(mesh):
    placed = (
        P("fsdp", "ctx", None),
        P("fsdp", "ctx", None),
        P("fsdp"),
        P("fsdp", None),
        P("fsdp", None),
        P("fsdp", None),
        P("fsdp", None),
        P("fsdp"),
        P("fsdp", None),
        P("fsdp", None),
        P("fsdp", None),
    )
    return jax.shard_map(
        body,
        mesh=mesh,
        in_specs=placed,
        out_specs=(
            P("fsdp", "ctx", None),
            P("fsdp", "ctx", None),
            P("fsdp"),
            P("fsdp", None),
            P("fsdp", None),
            P("fsdp", None),
            P("fsdp", None),
            P("fsdp"),
            P("fsdp", None),
            P("fsdp", None),
            P("fsdp", None),
        ),
        check_vma=False,
    )
```

time: 582 us -> 552 us (0.948)
  waiting for transfers between devices: 302 us -> 404 us
  blocking collectives: 131 us -> 50.9 us
  matrix products: 84.9 us -> 20.9 us
  Pallas kernels: 0 us -> 20.3 us
  local copies, waits for them, and re-layouts: 31.4 us -> 14.8 us
    reduce_scatter x0 -> x1, waiting for transfers between devices: none -> 110 us  [body(): lax.psum_scatter(partial_pair, 'ctx', scatter_dimension=0, tiled=True)]
    all_gather x2 -> x0, blocking collectives: 78.6 us -> none  [the longest x1 42.3 us: body(): total_split = lax.all_gather(sent_rows[2], 'ctx', axis=0, tiled=True)]
    dot_general x14 -> x0, matrix products: 51.7 us -> none  [the longest x2 12.7 us: block_step(): jnp.einsum('grst,sgrd->tgd', score_gradient, query_block, preferred_eleme...]
    pallas_call x0 -> x2, Pallas kernels: none -> 20.3 us  [the longest x1 11.3 us: attention_backward(): pl.pallas_call(backward_kernel, grid=(pair.shape[0] // keys,), in_specs=[...]
    all_gather x3 -> x1, waiting for transfers between devices: 70.4 us -> 52.6 us  [body(): arriving = lax.all_gather(packed, 'ctx', axis=0, tiled=True)]
    dynamic_slice x10 -> x2, local copies, waits for them, and re-layouts: 16.4 us -> 0.15 us  [reduce_grads(): lax.dynamic_slice_in_dim(partial, other * rows, rows, 0)]
    convert_element_type x7 -> x16, other arithmetic: 0.98 us -> 16.3 us  [the longest x7 9.39 us: reduce_grads(): h.astype(jnp.float32)]
    all_gather x1, waiting for transfers between devices: 0.02 us -> 10.2 us  [body(): lax.all_gather(w_up, 'fsdp', axis=0, tiled=True)]
  transfers between devices with their start and end apart: 7 -> 16, of which waited for: 5 -> 9; matrix products, arithmetic and copies ran while one was open for 12% -> 5% of each run, Pallas kernels for 0% -> 2%
where the time goes in v1:
time: 552 us; the launch traced here: 551 us
  waiting for transfers between devices  404 us (73%)
  blocking collectives  50.9 us (9%)
  other arithmetic  21.3 us (4%)
  matrix products  20.9 us (4%)
  Pallas kernels  20.3 us (4%)
  between operations  15.4 us (3%)
  local copies, waits for them, and re-layouts  14.8 us (3%)
    psum x2, waiting for transfers between devices, reduce_grads(): lax.psum(tuple(halves), 'ctx')  217 us
    reduce_scatter x1, waiting for transfers between devices, body(): lax.psum_scatter(partial_pair, 'ctx', scatter_dimension=0, tiled=True)  110 us
    all_gather x1, waiting for transfers between devices, body(): arriving = lax.all_gather(packed, 'ctx', axis=0, tiled=True)  52.6 us
    psum x1, blocking collectives, reduce_grads(): lax.psum(tuple(halves), 'ctx')  39.5 us
    pallas_call x1, Pallas kernels, attention_backward(): pl.pallas_call(backward_kernel, grid=(pair.shape[0] // keys,), in_specs=[...  11.3 us
    unnamed x75, local copies, waits for them, and re-layouts  11.1 us
  transfers between devices with their start and end apart: 16, of which 9 were waited for; matrix products, arithmetic and copies ran while one was open for 5% of the time, Pallas kernels for 2%

profile of v1, /device:TPU:0, one launch (start us, length us, event | category | flops | bytes accessed | tf_op | source)
XLA Modules:
  0.0 551.3 jit_solution(5715214780026108886)
XLA Ops:
  7.3 1.3 dynamic-slice
  9.2 0.9 dynamic-update-slice
  10.1 0.9 dynamic-update-slice.1
  10.9 2.6 all-reduce.5
  13.5 1.0 fusion.17
  14.6 2.2 all_gather.33
  17.0 1.2 convolution_convert_fusion.1
  18.3 2.0 all_gather.32
  21.2 0.7 pad_maximum_fusion
  22.0 0.7 all-gather.7.cloned.1.call-update
  22.8 0.7 all-gather.9.cloned.1.call-update
  23.5 0.5 all-gather.11.cloned.1.call-update
  24.1 2.3 all_gather.31
  26.8 0.4 fusion.29
  27.7 2.3 all_gather.35
  30.0 52.6 %all-gather.5.cloned.1.call-done.pair_ref = bf16[2048,384]{1,0:T(8,128)(2,1)} async-done(((bf16[128,384]{1,0:T(8,128)(2,1)}), bf16[2048,384]{1,0:T(8,128)(2,1)}) %all-gather.5.cloned.1.call-update) | async-done | bytes 1572880 | tf_op jit(solution)/shard_map/all_gather | solution.py:297
  82.6 1.4 copy-done
  84.0 9.0 %shard_map.194 = (f32[128,576]{1,0:T(8,128)S(1)}, f32[3,384]{1,0:T(4,128)S(1)}) custom-call(s32[1]{0:T(128)} %bitcast.1.first_ref, bf16[128,576]{1,0:T(8,128)(2,1)S(1)} %copy.52.query_ref, bf16[2048,384]{1,0:T(8,128)(2,1)S(1)} %copy-done), custom_call_target="tpu_custom_call" | custom-call | tf_op jit(solution)/shard_map/pallas_call | solution.py:204
  93.0 0.5 multiply_reduce_fusion.2
  93.6 2.0 fusion.50
  95.6 10.2 %all-gather.9.cloned.1.call-done = bf16[576,1536]{1,0:T(8,128)(2,1)} async-done(((bf16[288,1536]{1,0:T(8,128)(2,1)}), bf16[576,1536]{1,0:T(8,128)(2,1)}) %all-gather.9.cloned.1.call-update) | async-done | bytes 1769488 | tf_op jit(solution)/shard_map/all_gather | solution.py:265
  105.8 2.0 fusion.51
  107.8 10.7 %all-gather.11.cloned.1.call-done = bf16[1536,576]{0,1:T(8,128)(2,1)} async-done(((bf16[768,576]{0,1:T(8,128)(2,1)}), bf16[1536,576]{0,1:T(8,128)(2,1)}) %all-gather.11.cloned.1.call-update) | async-done | bytes 1769488 | tf_op jit(solution)/shard_map/all_gather | solution.py:266
  118.5 3.0 multiply_convert_fusion
  121.5 2.3 fusion.53
  123.9 0.6 fusion.52
  124.5 0.8 copy-done.5
  125.4 1.3 multiply_reduce_fusion
  127.4 0.7 copy-done.1
  128.1 11.3 %shard_map.195 = (f32[128,576]{1,0:T(8,128)S(1)}, bf16[2048,384]{1,0:T(8,128)(2,1)}) custom-call(s32[1]{0:T(128)} %bitcast.1.first_ref, bf16[128,576]{1,0:T(8,128)(2,1)S(1)} %copy.52.query_ref, bf16[128,576]{1,0:T(8,128)(2,1)S(1)} %copy.54.grad_ref, f32[128,576]{1,0:T(8,128)S(1)} %get-tuple-element.24.out_ref, f32[3,384]{1,0:T(4,128)S(1)} %get-tuple-element.25.log_ref, ...), custom_call_target="tpu_custom_call" | custom-call | tf_op jit(solution)/shard_map/pallas_call | solution.py:230
  139.6 1.6 dynamic-slice_convert_fusion.2
  141.5 0.6 fusion.22
  143.3 0.6 fusion.54
  144.4 1.1 collective-permute-done.3
  145.5 0.8 add_convert_fusion.4
  146.3 1.2 add_convert_fusion
  147.6 1.1 copy-done.3
  148.7 1.2 add_convert_fusion.2
  149.8 1.2 add_convert_fusion.1
  151.3 0.9 multiply_add_fusion.1
  152.5 2.3 fusion.2
  155.2 0.4 fusion.33
  155.6 109.6 %reduce-scatter.2.cloned.1.call-done = bf16[128,384]{1,0:T(8,128)(2,1)} async-done(((bf16[2048,384]{1,0:T(8,128)(2,1)}), bf16[128,384]{1,0:T(8,128)(2,1)}) %reduce-scatter.2.cloned.1.call-update) | async-done | bytes 98320 | tf_op jit(solution)/shard_map/reduce_scatter | solution.py:335
  265.3 0.8 slice_convert_fusion
  266.3 1.1 fusion.43
  268.5 149.7 %all-reduce.11.cloned.1.call-done = (bf16[288,1536]{1,0:T(8,128)(2,1)}, bf16[288,1536]{1,0:T(8,128)(2,1)}, bf16[768,576]{0,1:T(8,128)(2,1)}, bf16[288,576]{1,0:T(8,128)(2,1)}) async-done(((bf16[288,1536]{1,0:T(8,128)(2,1)}, bf16[288,1536]{1,0:T(8,128)(2,1)}, bf16[768,576]{0,1:T(8,128)(2,1)}, bf16[288,576]{1,0:T(8,128)(2,1)}), (bf16[288,1536]{1,0:T(8,128)(2,1)}, bf16[288,1536]{1,0:T(8,128)(2,1)}, ...) | async-done | bytes 2986000 | tf_op jit(solution)/shard_map/psum | solution.py:100
  418.3 2.7 convert_element_type.238
  421.0 1.4 convert_element_type.242
  422.4 1.3 convert_element_type.246
  423.7 0.9 convert_element_type.250
  424.8 0.6 collective-permute-start.6
  425.6 0.5 collective-permute-start.5
  426.4 0.8 add_convert_fusion.6
  427.2 0.8 add_convert_fusion.5
  428.0 0.8 add_convert_fusion.3
  428.9 0.9 fusion.14
  430.3 0.7 collective-permute-done.8
  431.1 39.5 %all-reduce.2 = (bf16[288]{0:T(512)(128)(2,1)S(1)}, bf16[288]{0:T(512)(128)(2,1)S(1)}) all-reduce(bf16[288]{0:T(512)(128)(2,1)S(1)} %add_convert_fusion.10, bf16[288]{0:T(512)(128)(2,1)S(1)} %add_convert_fusion.9), channel_id=1, replica_groups=mesh['ctx'=16,'fsdp'=2] {'ctx'}, use_global_device_ids=true, to_apply=%region_11.12 | all-reduce | flops 576 | bytes 2304 | tf_op jit(solution)/shard_map/psum | solution.py:100
  470.5 0.6 convert_element_type.255
  471.1 0.6 convert_element_type.271
  471.7 67.4 %all-reduce.9.cloned.1.call-done = (bf16[288,192]{0,1:T(8,128)(2,1)}, bf16[288,192]{0,1:T(8,128)(2,1)}, bf16[288,576]{1,0:T(8,128)(2,1)}) async-done(((bf16[288,192]{0,1:T(8,128)(2,1)}, bf16[288,192]{0,1:T(8,128)(2,1)}, bf16[288,576]{1,0:T(8,128)(2,1)}), (bf16[288,192]{0,1:T(8,128)(2,1)}, bf16[288,192]{0,1:T(8,128)(2,1)}, bf16[288,576]{1,0:T(8,128)(2,1)})) %all-reduce.9.cloned.1.call-update) | async-done | bytes 552976 | tf_op jit(solution)/shard_map/psum | solution.py:100
  539.1 1.9 convert_element_type.259
  541.0 1.7 copy.57
  542.7 1.7 copy.58
  (137 shorter events, 8.5 us)
Async XLA Ops:
  7.2 13.4 %copy-start.2 = (bf16[1,128,576]{1,2,0:T(8,128)(2,1)S(1)}, bf16[1,128,576]{1,2,0:T(8,128)(2,1)}, u32[]{:S(2)}) copy-start(bf16[1,128,576]{1,2,0:T(8,128)(2,1)} %param.11) | copy-start | bytes 442372
  7.2 11.1 %copy-start.30 = (bf16[288,192]{1,0:T(8,128)(2,1)S(1)}, bf16[288,192]{1,0:T(8,128)(2,1)}, u32[]{:S(2)}) copy-start(bf16[288,192]{1,0:T(8,128)(2,1)} %param.15) | copy-start | bytes 331780
  7.2 75.4 %all-gather.5.cloned.1.call-start = ((), (), s32[]{:S(2)}) async-start(), calls=%async_computation.1 | async-start | bytes 1671168 | tf_op jit(solution)/shard_map/all_gather | solution.py:297
  13.5 13.3 %copy-start.28 = (f32[576]{0:T(1024)}, f32[576]{0:T(1024)S(1)}, u32[]{:S(2)}) copy-start(f32[576]{0:T(1024)S(1)} %convert_element_type.215) | copy-start | bytes 6916
  14.5 12.3 %copy-start.31 = (f32[128]{0:T(128)}, f32[128]{0:T(128)S(1)}, u32[]{:S(2)}) copy-start(f32[128]{0:T(128)S(1)} %add_rsqrt_fusion.1) | copy-start | bytes 1540
  16.8 5.9 %copy-start.10 = (bf16[576,192]{1,0:T(8,128)(2,1)}, bf16[576,192]{1,0:T(8,128)(2,1)S(1)}, u32[]{:S(2)}) copy-start(bf16[576,192]{1,0:T(8,128)(2,1)S(1)} %all_gather.33) | copy-start | bytes 663556
  20.4 3.1 copy-start.12
  20.9 3.2 copy-start.25
  21.0 6.2 %copy-start.22 = (f32[128,32]{0,1:T(8,128)}, f32[128,32]{0,1:T(8,128)S(1)}, u32[]{:S(2)}) copy-start(f32[128,32]{0,1:T(8,128)S(1)} %get-tuple-element.97) | copy-start | bytes 49156
  22.0 71.7 %all-gather.7.cloned.1.call-start = ((), (), s32[]{:S(2)}) async-start(), calls=%async_computation.2 | async-start | bytes 2654208 | tf_op jit(solution)/shard_map/all_gather | solution.py:264
  22.7 83.1 %all-gather.9.cloned.1.call-start = ((), (), s32[]{:S(2)}) async-start(), calls=%async_computation.3 | async-start | bytes 2654208 | tf_op jit(solution)/shard_map/all_gather | solution.py:265
  23.5 95.1 %all-gather.11.cloned.1.call-start = ((), (), s32[]{:S(2)}) async-start(), calls=%async_computation.4 | async-start | bytes 2654208 | tf_op jit(solution)/shard_map/all_gather | solution.py:266
  24.0 241.2 %reduce-scatter.2.cloned.1.call-start = ((), (), s32[]{:S(2)}) async-start(), calls=%async_computation.5 | async-start | bytes 1671168 | tf_op jit(solution)/shard_map/reduce_scatter | solution.py:335
  26.4 1.1 copy-start.6
  26.5 1.2 copy-start.26
  30.0 63.6 %copy-start.8 = (bf16[576,576]{1,0:T(8,128)(2,1)}, bf16[576,576]{1,0:T(8,128)(2,1)S(1)}, u32[]{:S(2)}) copy-start(bf16[576,576]{1,0:T(8,128)(2,1)S(1)} %all_gather.35) | copy-start | bytes 1990660
  82.6 1.4 copy-start
  95.6 22.9 %copy-start.20 = (bf16[1,128,576]{1,2,0:T(8,128)(2,1)S(1)}, bf16[1,128,576]{1,2,0:T(8,128)(2,1)}, u32[]{:S(2)}) copy-start(bf16[1,128,576]{1,2,0:T(8,128)(2,1)} %param.12) | copy-start | bytes 442372
  121.5 3.0 copy-start.16
  121.5 2.3 copy-start.4
  123.9 1.5 copy-start.5
  125.4 1.5 copy-start.9
  126.7 1.4 copy-start.1
  139.4 2.1 copy-start.15
  139.4 2.1 copy-start.21
  139.4 278.9 %all-reduce.11.cloned.1.call-start = ((), (), s32[]{:S(2)}) async-start(), calls=%async_computation.7 | async-start | bytes 6045696 | tf_op jit(solution)/shard_map/psum | solution.py:100
  141.2 6.3 %collective-permute-start = (bf16[288,1536]{1,0:T(8,128)(2,1)S(1)}, bf16[288,1536]{1,0:T(8,128)(2,1)S(1)}, u32[]{:S(2)}, u32[]{:S(2)}) collective-permute-start(bf16[288,1536]{1,0:T(8,128)(2,1)S(1)} %dynamic-slice_convert_fusion.2), channel_id=1, source_target_pairs={{0,1},{1,0},{2,3},{3,2},{4,5},{5,4},{6,7},{7,6},{8,9},{9,8},{10,11... | collective-permute-start | bytes 2654216 | tf_op jit(solution)/shard_map/ppermute | solution.py:98
  142.2 1.1 copy-start.17
  142.2 4.1 collective-permute-start.2
  143.1 2.5 collective-permute-start.3
  144.0 5.8 %collective-permute-start.1 = (bf16[288,1536]{1,0:T(8,128)(2,1)S(1)}, bf16[288,1536]{1,0:T(8,128)(2,1)S(1)}, u32[]{:S(2)}, u32[]{:S(2)}) collective-permute-start(bf16[288,1536]{1,0:T(8,128)(2,1)S(1)} %dynamic-slice_convert_fusion.1), channel_id=1, source_target_pairs={{0,1},{1,0},{2,3},{3,2},{4,5},{5,4},{6,7},{7,6},{8,9},{9,8},{10,11... | collective-permute-start | bytes 2654216 | tf_op jit(solution)/shard_map/ppermute | solution.py:98
  146.3 2.3 copy-start.3
  151.0 1.5 copy-start.14
  151.0 388.1 %all-reduce.9.cloned.1.call-start = ((), (), s32[]{:S(2)}) async-start(), calls=%async_computation.6 | async-start | bytes 1327104 | tf_op jit(solution)/shard_map/psum | solution.py:100
  151.3 3.6 copy-start.7
  152.5 2.7 copy-start.29
  152.5 2.7 copy-start.32
  154.8 111.4 %copy-start.23 = (f32[128,32]{0,1:T(8,128)S(1)}, f32[128,32]{0,1:T(8,128)}, u32[]{:S(2)}) copy-start(f32[128,32]{0,1:T(8,128)} %copy-done.22) | copy-start | bytes 49156
  154.8 111.5 %copy-start.11 = (bf16[576,192]{1,0:T(8,128)(2,1)S(1)}, bf16[576,192]{1,0:T(8,128)(2,1)}, u32[]{:S(2)}) copy-start(bf16[576,192]{1,0:T(8,128)(2,1)} %copy-done.10) | copy-start | bytes 663556
  155.2 112.2 %copy-start.13 = (bf16[576,192]{1,0:T(8,128)(2,1)S(1)}, bf16[576,192]{1,0:T(8,128)(2,1)}, u32[]{:S(2)}) copy-start(bf16[576,192]{1,0:T(8,128)(2,1)} %copy-done.12) | copy-start | bytes 663556
  266.2 2.0 copy-start.24
  418.3 2.7 copy-start.19
  421.0 1.4 copy-start.18
  422.4 1.3 copy-start.27
  424.7 5.5 collective-permute-start.4
  424.8 1.6 collective-permute-start.6
  425.5 1.7 collective-permute-start.7
  425.6 2.4 collective-permute-start.5
  427.2 2.5 copy-start.33
  429.8 1.2 collective-permute-start.8
Sparse Core Ops, SparseCore 0:
  22.1 60.4 all-gather.4
  84.1 8.8 all-gather.6
  94.6 11.2 all-gather.8
  107.2 11.2 all-gather.10
  139.5 125.6 reduce-scatter.1
  272.5 145.7 all-reduce.10
  429.0 110.0 all-reduce.8

commit v2 on v1

--- a/solution.py
+++ b/solution.py
@@ -76,28 +76,108 @@
     return span_rows
 
 
-def split_pair(block_rows, kv_width, groups):
-    rows_here = block_rows.shape[0]
-    return (
-        block_rows[:, :kv_width].reshape(rows_here, groups, -1),
-        block_rows[:, kv_width:].reshape(rows_here, groups, -1),
-    )
-
-
-def reduce_grads(partials):
+def bit_count(devices):
+    return devices.bit_length() - 1
+
+
+def gather_orders(devices):
+    order = list(range(bit_count(devices)))[::-1]
+    return (order, order[:-2] + order[-2:][::-1])
+
+
+def reduce_orders(devices):
+    order = list(range(bit_count(devices)))
+    return (order, order[:2][::-1] + order[2:], order[2:] + order[:2])
+
+
+def swap(values, bit):
+    count = lax.axis_size("ctx")
+    return lax.ppermute(values, "ctx", [(i, i ^ (1 << bit)) for i in range(count)])
+
+
+def own_bit(bit):
+    return lax.rem(lax.axis_index("ctx") // (1 << bit), 2)
+
+
+def gather_tree(block, order):
+    held = block
+    for bit in order:
+        held = jnp.concatenate([held, swap(held, bit)], 0)
+    return held
+
+
+def scatter_tree(slots, order):
+    held = slots.astype(jnp.float32)
+    for bit in order[::-1]:
+        half = held.shape[0] // 2
+        held = held[:half] + swap(held[half:].astype(jnp.bfloat16), bit).astype(jnp.float32)
+    return held
+
+
+def middle_swapped(slots, order):
+    if len(order) < 2:
+        return slots
+    part = slots.shape[0] // 4
+    return jnp.concatenate(
+        [slots[:part], slots[2 * part : 3 * part], slots[part : 2 * part], slots[3 * part :]], 0
+    )
+
+
+def slot_places(rows, order):
+    slots = jnp.arange(1 << len(order), dtype=jnp.int32)
+    flips = jnp.zeros_like(slots)
+    for place, bit in enumerate(order):
+        flips = flips + ((slots >> place) & 1) * (1 << bit)
+    owners = flips ^ lax.axis_index("ctx").astype(jnp.int32)
+    return (owners[:, None] * rows + jnp.arange(rows, dtype=jnp.int32)[None, :]).reshape(-1, 1)
+
+
+def core_half(partial):
     own_index = lax.axis_index("fsdp")
     part_count = lax.axis_size("fsdp")
-    halves = []
-    for partial in partials:
-        rows = partial.shape[0] // part_count
-        own = lax.dynamic_slice_in_dim(partial, own_index * rows, rows, 0)
-        for shift in range(1, part_count):
-            other = lax.rem(own_index + shift, part_count)
-            sent = lax.dynamic_slice_in_dim(partial, other * rows, rows, 0).astype(jnp.bfloat16)
-            moves = [(a, (a + shift) % part_count) for a in range(part_count)]
-            own = own + lax.ppermute(sent, "fsdp", moves).astype(jnp.float32)
-        halves.append(own.astype(jnp.bfloat16))
-    return tuple(h.astype(jnp.float32) for h in lax.psum(tuple(halves), "ctx"))
+    rows = partial.shape[0] // part_count
+    own = lax.dynamic_slice_in_dim(partial, own_index * rows, rows, 0)
+    for shift in range(1, part_count):
+        other = lax.rem(own_index + shift, part_count)
+        sent = lax.dynamic_slice_in_dim(partial, other * rows, rows, 0).astype(jnp.bfloat16)
+        moves = [(a, (a + shift) % part_count) for a in range(part_count)]
+        own = own + lax.ppermute(sent, "fsdp", moves).astype(jnp.float32)
+    return own
+
+
+def reduce_tree(partial, order):
+    held = partial
+    path = []
+    for bit in order:
+        axis = 0 if held.shape[0] % 16 == 0 else 1
+        half = held.shape[axis] // 2
+        mine = own_bit(bit)
+        kept = lax.dynamic_slice_in_dim(held, mine * half, half, axis)
+        sent = lax.dynamic_slice_in_dim(held, (1 - mine) * half, half, axis)
+        held = kept + swap(sent.astype(jnp.bfloat16), bit).astype(jnp.float32)
+        path.append((bit, axis))
+    held = held.astype(jnp.bfloat16)
+    for bit, axis in path[::-1]:
+        other = swap(held, bit)
+        held = jnp.where(
+            own_bit(bit) == 0,
+            jnp.concatenate([held, other], axis),
+            jnp.concatenate([other, held], axis),
+        )
+    return held.astype(jnp.float32)
+
+
+def sum_tree(partial, order):
+    held = partial
+    for bit in order:
+        held = held + swap(held, bit)
+    count = lax.axis_size("fsdp")
+    parts = held
+    for shift in range(1, count):
+        moves = [(a, (a + shift) % count) for a in range(count)]
+        parts = parts + lax.ppermute(held, "fsdp", moves)
+    held = parts
+    return held
 
 
 def heads_stacked(ref, group, repeat):
@@ -113,17 +193,26 @@
     return jnp.concatenate([back[r * rows : (r + 1) * rows] for r in range(repeat)], 1)
 
 
-def allowed_pairs(first_ref, key_first, keys, rows, repeat):
-    key_place = lax.broadcasted_iota(jnp.int32, (keys, repeat * rows), 0)
-    query_place = lax.rem(lax.broadcasted_iota(jnp.int32, (keys, repeat * rows), 1), rows)
-    return key_place - query_place <= first_ref[0] - key_first
-
-
-def forward_kernel(first_ref, query_ref, pair_ref, out_ref, log_ref, high_ref, total_ref, sum_ref):
+def allowed_pairs(first_ref, place_ref, rows, repeat):
+    query_place = lax.rem(lax.broadcasted_iota(jnp.int32, (1, repeat * rows), 1), rows)
+    return place_ref[...] <= query_place + first_ref[0]
+
+
+def forward_kernel(
+    first_ref,
+    place_ref,
+    query_ref,
+    key_ref,
+    value_ref,
+    out_ref,
+    log_ref,
+    high_ref,
+    total_ref,
+    sum_ref,
+):
     block, blocks = pl.program_id(0), pl.num_programs(0)
-    keys, rows = pair_ref.shape[0], query_ref.shape[0]
+    rows = query_ref.shape[0]
     repeat = HEADS // KV_HEADS
-    kv_width = KV_HEADS * HEAD_DIM
 
     @pl.when(block == 0)
     def _():
@@ -131,11 +220,11 @@
         total_ref[...] = jnp.zeros_like(total_ref)
         sum_ref[...] = jnp.zeros_like(sum_ref)
 
-    allowed = allowed_pairs(first_ref, block * keys, keys, rows, repeat)
+    allowed = allowed_pairs(first_ref, place_ref, rows, repeat)
     for group in range(KV_HEADS):
         stacked = heads_stacked(query_ref, group, repeat)
-        k = pair_ref[:, group * HEAD_DIM : (group + 1) * HEAD_DIM]
-        v = pair_ref[:, kv_width + group * HEAD_DIM : kv_width + (group + 1) * HEAD_DIM]
+        k = key_ref[:, group * HEAD_DIM : (group + 1) * HEAD_DIM]
+        v = value_ref[:, group * HEAD_DIM : (group + 1) * HEAD_DIM]
         scores = jnp.where(allowed, times_transposed(k, stacked), masked_score)
         old_high = high_ref[group : group + 1, :]
         new_high = jnp.maximum(old_high, jnp.max(scores, 0, keepdims=True))
@@ -155,26 +244,36 @@
 
 
 def backward_kernel(
-    first_ref, query_ref, grad_ref, out_ref, log_ref, pair_ref, dq_ref, dpair_ref, sum_ref
+    first_ref,
+    place_ref,
+    query_ref,
+    grad_ref,
+    out_ref,
+    log_ref,
+    key_ref,
+    value_ref,
+    dq_ref,
+    dkey_ref,
+    dvalue_ref,
+    sum_ref,
 ):
     block, blocks = pl.program_id(0), pl.num_programs(0)
-    keys, rows = pair_ref.shape[0], query_ref.shape[0]
+    rows = query_ref.shape[0]
     repeat = HEADS // KV_HEADS
-    kv_width = KV_HEADS * HEAD_DIM
 
     @pl.when(block == 0)
     def _():
         sum_ref[...] = jnp.zeros_like(sum_ref)
 
-    allowed = allowed_pairs(first_ref, block * keys, keys, rows, repeat)
+    allowed = allowed_pairs(first_ref, place_ref, rows, repeat)
     key_parts, value_parts = [], []
     for group in range(KV_HEADS):
         stacked = heads_stacked(query_ref, group, repeat)
         grads = heads_stacked(grad_ref, group, repeat)
         outs = heads_stacked(out_ref, group, repeat)
         inner = jnp.sum((grads.astype(jnp.float32) * outs).T, 0, keepdims=True)
-        k = pair_ref[:, group * HEAD_DIM : (group + 1) * HEAD_DIM]
-        v = pair_ref[:, kv_width + group * HEAD_DIM : kv_width + (group + 1) * HEAD_DIM]
+        k = key_ref[:, group * HEAD_DIM : (group + 1) * HEAD_DIM]
+        v = value_ref[:, group * HEAD_DIM : (group + 1) * HEAD_DIM]
         scores = times_transposed(k, stacked)
         shares = jnp.where(allowed, jnp.exp(scores - log_ref[group : group + 1, :]), 0.0)
         score_grads = (shares * (times_transposed(v, grads) - inner)).astype(jnp.bfloat16)
@@ -190,24 +289,28 @@
             width = repeat * HEAD_DIM
             dq_ref[:, group * width : (group + 1) * width] = heads_beside(summed, repeat)
 
-    dpair_ref[...] = jnp.concatenate(key_parts + value_parts, 1).astype(dpair_ref.dtype)
+    dkey_ref[...] = jnp.concatenate(key_parts, 1).astype(dkey_ref.dtype)
+    dvalue_ref[...] = jnp.concatenate(value_parts, 1).astype(dvalue_ref.dtype)
 
 
 def whole_block(shape):
     return pl.BlockSpec(shape, lambda b: (0,) * len(shape))
 
 
-def attention_forward(first_place, queries, pair):
+def attention_forward(first_place, places, queries, all_keys, all_values):
     rows, width = queries.shape
-    keys = block_span(pair.shape[0])
+    keys = block_span(all_keys.shape[0])
+    kv_block = pl.BlockSpec((keys, all_keys.shape[1]), lambda b: (b, 0))
     columns = (HEADS // KV_HEADS) * rows
     return pl.pallas_call(
         forward_kernel,
-        grid=(pair.shape[0] // keys,),
+        grid=(all_keys.shape[0] // keys,),
         in_specs=[
             pl.BlockSpec(memory_space=pltpu.SMEM),
+            pl.BlockSpec((keys, 1), lambda b: (b, 0)),
             whole_block((rows, width)),
-            pl.BlockSpec((keys, pair.shape[1]), lambda b: (b, 0)),
+            kv_block,
+            kv_block,
         ],
         out_specs=[whole_block((rows, width)), whole_block((KV_HEADS, columns))],
         out_shape=[
@@ -220,35 +323,40 @@
             pltpu.VMEM((KV_HEADS, HEAD_DIM, columns), jnp.float32),
         ],
         compiler_params=pltpu.CompilerParams(vmem_limit_bytes=40 * 1024 * 1024),
-    )(first_place, queries, pair)
-
-
-def attention_backward(first_place, queries, grads, outs, logs, pair):
+    )(first_place, places, queries, all_keys, all_values)
+
+
+def attention_backward(first_place, places, queries, grads, outs, logs, all_keys, all_values):
     rows, width = queries.shape
-    keys = block_span(pair.shape[0])
+    keys = block_span(all_keys.shape[0])
+    kv_block = pl.BlockSpec((keys, all_keys.shape[1]), lambda b: (b, 0))
     columns = (HEADS // KV_HEADS) * rows
     return pl.pallas_call(
         backward_kernel,
-        grid=(pair.shape[0] // keys,),
+        grid=(all_keys.shape[0] // keys,),
         in_specs=[
             pl.BlockSpec(memory_space=pltpu.SMEM),
+            pl.BlockSpec((keys, 1), lambda b: (b, 0)),
             whole_block((rows, width)),
             whole_block((rows, width)),
             whole_block((rows, width)),
             whole_block((KV_HEADS, columns)),
-            pl.BlockSpec((keys, pair.shape[1]), lambda b: (b, 0)),
+            kv_block,
+            kv_block,
         ],
         out_specs=[
             whole_block((rows, width)),
-            pl.BlockSpec((keys, pair.shape[1]), lambda b: (b, 0)),
+            kv_block,
+            kv_block,
         ],
         out_shape=[
             jax.ShapeDtypeStruct((rows, width), jnp.float32),
-            jax.ShapeDtypeStruct(pair.shape, jnp.bfloat16),
+            jax.ShapeDtypeStruct(all_keys.shape, jnp.bfloat16),
+            jax.ShapeDtypeStruct(all_keys.shape, jnp.bfloat16),
         ],
         scratch_shapes=[pltpu.VMEM((KV_HEADS, HEAD_DIM, columns), jnp.float32)],
         compiler_params=pltpu.CompilerParams(vmem_limit_bytes=40 * 1024 * 1024),
-    )(first_place, queries, grads, outs, logs, pair)
+    )(first_place, places, queries, grads, outs, logs, all_keys, all_values)
 
 
 def body(
@@ -291,16 +399,19 @@
         key_pre.reshape(local_rows, groups, HEAD_DIM), cosine_table, sine_table
     ).astype(jnp.bfloat16)
     values_here = value_pre.reshape(local_rows, groups, HEAD_DIM).astype(jnp.bfloat16)
-    packed = jnp.concatenate(
-        [keys_here.reshape(local_rows, kv_width), values_here.reshape(local_rows, kv_width)], 1
-    )
-    arriving = lax.all_gather(packed, "ctx", axis=0, tiled=True)
-    all_rows = arriving.shape[0]
+    key_order, value_order = gather_orders(lax.axis_size("ctx"))
+    all_keys = gather_tree(keys_here.reshape(local_rows, kv_width), key_order)
+    all_values = middle_swapped(
+        gather_tree(values_here.reshape(local_rows, kv_width), value_order), value_order
+    )
+    places = slot_places(local_rows, key_order)
     scaled_queries = (
         query_matrix.reshape(local_rows, model_width) * jnp.bfloat16(score_scale)
     )
     first_place = first_pos.astype(jnp.int32).reshape(1)
-    attended, log_totals = attention_forward(first_place, scaled_queries, arriving)
+    attended, log_totals = attention_forward(
+        first_place, places, scaled_queries, all_keys, all_values
+    )
     out_act = attended.reshape(local_rows, model_width).astype(jnp.bfloat16)
     residual = inputs + jnp.dot(out_act, out_w, preferred_element_type=jnp.float32)
     ffn_in, normed_two, factor_two = norm_forward(residual, gain_ffn)
@@ -326,14 +437,17 @@
     grad_residual = grad_output.astype(jnp.float32) + back_two
     grad_attn = grad_residual.astype(jnp.bfloat16)
     grad_out_w = transposed_times(out_act, grad_attn)
-    reduce_early = reduce_grads((grad_gate_w, grad_up_w, grad_down_w, grad_out_w))
+    first_order, second_order, third_order = reduce_orders(lax.axis_size("ctx"))
+    shard_gate = reduce_tree(core_half(grad_gate_w), first_order)
+    shard_up = reduce_tree(core_half(grad_up_w), second_order)
+    shard_down = reduce_tree(core_half(grad_down_w), third_order)
     grad_flat = times_transposed(grad_attn, out_w).astype(jnp.bfloat16)
-    grad_queries, partial_pair = attention_backward(
-        first_place, scaled_queries, grad_flat, attended, log_totals, arriving
+    grad_queries, partial_keys, partial_values = attention_backward(
+        first_place, places, scaled_queries, grad_flat, attended, log_totals, all_keys, all_values
     )
     grad_queries = grad_queries * score_scale
-    summed_pair = lax.psum_scatter(partial_pair, "ctx", scatter_dimension=0, tiled=True)
-    grad_keys, grad_values = split_pair(summed_pair.astype(jnp.float32), kv_width, groups)
+    grad_keys = scatter_tree(partial_keys, key_order).reshape(local_rows, groups, HEAD_DIM)
+    grad_values = scatter_tree(middle_swapped(partial_values, value_order), value_order)
     grad_query_pre = (
         unrotate(grad_queries.reshape(local_rows, HEADS, HEAD_DIM), cosine_table, sine_table)
         .reshape(local_rows, model_width)
@@ -355,25 +469,30 @@
     )
     back_one, grad_gain_attn = norm_backward(grad_act_one, gain_attn, normed_one, factor_one)
     grad_input = grad_residual + back_one
-    reduce_early, late_grads = lax.optimization_barrier(
-        (
-            reduce_early,
-            (grad_query_w, grad_key_w, grad_value_w, grad_gain_attn, grad_gain_ffn),
-        )
-    )
-    shards = reduce_early + reduce_grads(late_grads)
+    shard_one = reduce_tree(
+        core_half(jnp.concatenate([grad_out_w, grad_key_w], 1)), first_order
+    )
+    shard_two = reduce_tree(
+        core_half(jnp.concatenate([grad_query_w, grad_value_w], 1)), second_order
+    )
+    shard_out, shard_key = shard_one[:, :model_width], shard_one[:, model_width:]
+    shard_query, shard_value = shard_two[:, :model_width], shard_two[:, model_width:]
+    gains = sum_tree(jnp.stack([grad_gain_attn, grad_gain_ffn]), first_order)
+    shard_gains = lax.dynamic_slice_in_dim(
+        gains, lax.axis_index("fsdp") * norm_attn.shape[0], norm_attn.shape[0], 1
+    )
     return (
         result[None],
         grad_input[None],
-        shards[7],
-        shards[4],
-        shards[5],
-        shards[6],
-        shards[3],
-        shards[8],
-        shards[0],
-        shards[1],
-        shards[2],
+        shard_gains[0],
+        shard_query,
+        shard_key,
+        shard_value,
+        shard_out,
+        shard_gains[1],
+        shard_gate,
+        shard_up,
+        shard_down,
     )
 
 

time: 552 us -> 271 us (0.49)
  waiting for transfers between devices: 404 us -> 72.7 us
  starting transfers between devices: 3.3 us -> 83.2 us
  blocking collectives: 50.9 us -> 12.1 us
  local copies, waits for them, and re-layouts: 14.8 us -> 26.3 us
    psum x2 -> x0, waiting for transfers between devices: 217 us -> none  [reduce_grads(): lax.psum(tuple(halves), 'ctx')]
    reduce_scatter x1 -> x0, waiting for transfers between devices: 110 us -> none  [body(): lax.psum_scatter(partial_pair, 'ctx', scatter_dimension=0, tiled=True)]
    ppermute x9 -> x66, starting transfers between devices: 2.84 us -> 83.1 us  [the longest x60 82.3 us: swap(): lax.ppermute(values, 'ctx', [(i, i ^ 1 << bit) for i in range(count)])]
    ppermute x9 -> x66, waiting for transfers between devices: 2.06 us -> 71.3 us  [the longest x60 70.3 us: swap(): lax.ppermute(values, 'ctx', [(i, i ^ 1 << bit) for i in range(count)])]
    all_gather x1 -> x0, waiting for transfers between devices: 52.6 us -> none  [body(): arriving = lax.all_gather(packed, 'ctx', axis=0, tiled=True)]
    psum x1 -> x0, blocking collectives: 39.5 us -> none  [reduce_grads(): lax.psum(tuple(halves), 'ctx')]
    convert_element_type x16 -> x12, other arithmetic: 16.3 us -> 4.96 us  [the longest x5 4.37 us: reduce_tree(): return held.astype(jnp.float32)]
    all_gather x1, waiting for transfers between devices: 10.7 us -> 0.01 us  [body(): lax.all_gather(w_down, 'fsdp', axis=0, tiled=True)]
  transfers between devices with their start and end apart: 16 -> 69, of which waited for: 9 -> 30; matrix products, arithmetic and copies ran while one was open for 5% -> 16% of each run, Pallas kernels for 2% -> 3%
where the time goes in v2:
time: 271 us; the launch traced here: 270 us
  starting transfers between devices  83.2 us (31%)
  waiting for transfers between devices  72.7 us (27%)
  local copies, waits for them, and re-layouts  26.3 us (10%)
  matrix products  23.5 us (9%)
  Pallas kernels  19.6 us (7%)
  other arithmetic  16.7 us (6%)
  between operations  15.9 us (6%)
  blocking collectives  12.1 us (4%)
    ppermute x60, starting transfers between devices, swap(): lax.ppermute(values, 'ctx', [(i, i ^ 1 << bit) for i in range(count)])  82.3 us
    ppermute x60, waiting for transfers between devices, swap(): lax.ppermute(values, 'ctx', [(i, i ^ 1 << bit) for i in range(count)])  70.3 us
    pallas_call x1, Pallas kernels, attention_backward(): pl.pallas_call(backward_kernel, grid=(all_keys.shape[0] // keys,), in_spe...  10.6 us
    pallas_call x1, Pallas kernels, attention_forward(): pl.pallas_call(forward_kernel, grid=(all_keys.shape[0] // keys,), in_spec...  8.97 us
    unnamed x114, local copies, waits for them, and re-layouts  8.92 us
    dot_general x7, matrix products, transposed_times(): lax.dot_general(left, right, (((0,), (0,)), ((), ())), preferred_element_...  7.87 us
    dot_general x7, matrix products, times_transposed(): lax.dot_general(left, right, (((1,), (1,)), ((), ())), preferred_element_...  6.89 us
    convert_element_type x3, local copies, waits for them, and re-layouts, core_half(): lax.dynamic_slice_in_dim(partial, other * rows, rows, 0)  6.09 us
  transfers between devices with their start and end apart: 69, of which 30 were waited for; matrix products, arithmetic and copies ran while one was open for 16% of the time, Pallas kernels for 3%

profile of v2, /device:TPU:0, one launch (start us, length us, event | category | flops | bytes accessed | tf_op | source)
XLA Modules:
  0.0 269.9 jit_solution(12333128535093759959)
XLA Ops:
  10.5 3.1 %all-reduce.2 = (bf16[576]{0:T(1024)(128)(2,1)S(1)}, bf16[576]{0:T(1024)(128)(2,1)}) all-reduce(bf16[576]{0:T(1024)(128)(2,1)S(1)} %dynamic-update-slice, bf16[576]{0:T(1024)(128)(2,1)S(1)} %dynamic-update-slice.1), channel_id=1, replica_groups=mesh['ctx'=16,'fsdp'=2] {'fsdp'}, use_global_device_ids=true, to_apply=%add | all-reduce | flops 1152 | bytes 4608
  13.7 2.0 all_gather.29
  16.7 4.0 %collective-permute-start = (bf16[128,192]{1,0:T(8,128)(2,1)S(1)}, bf16[128,192]{1,0:T(8,128)(2,1)S(1)}, u32[]{:S(2)}, u32[]{:S(2)}) collective-permute-start(bf16[128,192]{1,0:T(8,128)(2,1)S(1)} %copy.63), channel_id=1, source_target_pairs={{0,16},{2,18},{4,20},{6,22},{8,24},{10,26},{12,28},{14,30},{16,0},... | collective-permute-start | bytes 147464 | tf_op jit(solution)/shard_map/ppermute | solution.py:95
  20.7 2.0 all_gather.30
  23.6 2.5 all_gather.31
  26.8 2.5 all_gather.28
  33.0 1.8 collective-permute-start.1
  35.2 6.2 %collective-permute-done.5 = bf16[256,192]{1,0:T(8,128)(2,1)S(1)} collective-permute-done((bf16[256,192]{1,0:T(8,128)(2,1)S(1)}, bf16[256,192]{1,0:T(8,128)(2,1)S(1)}, u32[]{:S(2)}, u32[]{:S(2)}) %collective-permute-start.5) | collective-permute-done | bytes 98336 | tf_op jit(solution)/shard_map/ppermute | solution.py:95
  41.4 1.7 collective-permute-start.6
  43.2 1.6 collective-permute-start.2
  44.8 4.2 %collective-permute-done.6 = bf16[512,192]{1,0:T(8,128)(2,1)S(1)} collective-permute-done((bf16[512,192]{1,0:T(8,128)(2,1)S(1)}, bf16[512,192]{1,0:T(8,128)(2,1)S(1)}, u32[]{:S(2)}, u32[]{:S(2)}) %collective-permute-start.6) | collective-permute-done | bytes 196640 | tf_op jit(solution)/shard_map/ppermute | solution.py:95
  49.1 1.7 collective-permute-start.7
  51.0 1.5 collective-permute-start.3
  52.6 9.2 %collective-permute-done.7 = bf16[1024,192]{1,0:T(8,128)(2,1)S(1)} collective-permute-done((bf16[1024,192]{1,0:T(8,128)(2,1)S(1)}, bf16[1024,192]{1,0:T(8,128)(2,1)S(1)}, u32[]{:S(2)}, u32[]{:S(2)}) %collective-permute-start.7) | collective-permute-done | bytes 393248 | tf_op jit(solution)/shard_map/ppermute | solution.py:95
  63.1 9.0 %shard_map.194 = (f32[128,576]{1,0:T(8,128)S(1)}, f32[3,384]{1,0:T(4,128)S(1)}) custom-call(s32[1]{0:T(128)} %bitcast.1.first_ref, s32[2048,1]{1,0:T(8,128)S(1)} %copy.70.place_ref, bf16[128,576]{1,0:T(8,128)(2,1)S(1)} %copy-done, bf16[2048,192]{1,0:T(8,128)(2,1)S(1)} %constant_dynamic-update-slice_fusion.key_ref, ...), custom_call_target="tpu_custom_call" | custom-call | tf_op jit(solution)/shard_map/pallas_call | solution.py:305
  74.1 2.9 %fusion.77 = f32[128,1536]{1,0:T(8,128)} fusion(bf16[128,576]{0,1:T(8,128)(2,1)} %multiply_convert_fusion.3, bf16[576,1536]{1,0:T(8,128)(2,1)} %all-gather.4.cloned.1.call-done), kind=kOutput, calls=%fused_computation.224 | convolution fusion | flops 226492416 | bytes 2703360 | tf_op jit(solution)/shard_map/dot_general | solution.py:419
  77.0 2.9 %fusion.78 = f32[128,1536]{1,0:T(8,128)} fusion(bf16[128,576]{0,1:T(8,128)(2,1)} %multiply_convert_fusion.3, bf16[576,1536]{1,0:T(8,128)(2,1)} %all-gather.6.cloned.1.call-done), kind=kOutput, calls=%fused_computation.225 | convolution fusion | flops 226492416 | bytes 2703360 | tf_op jit(solution)/shard_map/dot_general | solution.py:420
  80.0 3.6 %multiply_convert_fusion = (bf16[128,1536]{1,0:T(8,128)(2,1)S(1)}, bf16[128,1536]{1,0:T(8,128)(2,1)S(1)}, bf16[128,1536]{1,0:T(8,128)(2,1)}) fusion(f32[128,1536]{1,0:T(8,128)} %fusion.77, f32[128,1536]{1,0:T(8,128)} %fusion.78, bf16[1536,576]{0,1:T(8,128)(2,1)} %all-gather.8.cloned.1.call-done, bf16[1,128,576]{1,2,0:T(8,128)(2,1)} %param.12), kind=kOutput, calls=%fused_computation.45 | convolution fusion | flops 229441536 | bytes 4669440 | tf_op jit(solution)/shard_map/dot_general | solution.py:61
  87.3 1.5 fusion.50
  88.8 2.4 fusion.80
  91.2 2.4 fusion.81
  93.6 1.7 copy.74.grad_ref
  97.2 10.6 %shard_map.195 = (f32[128,576]{1,0:T(8,128)S(1)}, bf16[2048,192]{1,0:T(8,128)(2,1)S(1)}, bf16[2048,192]{1,0:T(8,128)(2,1)S(1)}) custom-call(s32[1]{0:T(128)} %bitcast.1.first_ref, s32[2048,1]{1,0:T(8,128)S(1)} %copy.70.place_ref, bf16[128,576]{1,0:T(8,128)(2,1)S(1)} %copy-done.1, bf16[128,576]{1,0:T(8,128)(2,1)S(1)} %copy-done.6, ...), custom_call_target="tpu_custom_call" | custom-call | tf_op jit(solution)/shard_map/pallas_call | solution.py:334
  111.2 1.5 collective-permute-start.8
  114.0 2.5 dynamic-slice_convert_fusion.2
  116.5 2.5 dynamic-slice_convert_fusion.1
  125.0 1.5 collective-permute-start.9
  127.3 5.9 %collective-permute-done.9 = bf16[512,192]{1,0:T(8,128)(2,1)S(1)} collective-permute-done((bf16[512,192]{1,0:T(8,128)(2,1)S(1)}, bf16[512,192]{1,0:T(8,128)(2,1)S(1)}, u32[]{:S(2)}, u32[]{:S(2)}) %collective-permute-start.9) | collective-permute-done | bytes 196640 | tf_op jit(solution)/shard_map/ppermute | solution.py:95
  133.3 1.6 collective-permute-start.10
  136.5 3.0 %collective-permute-done.10 = bf16[256,192]{1,0:T(8,128)(2,1)S(1)} collective-permute-done((bf16[256,192]{1,0:T(8,128)(2,1)S(1)}, bf16[256,192]{1,0:T(8,128)(2,1)S(1)}, u32[]{:S(2)}, u32[]{:S(2)}) %collective-permute-start.10) | collective-permute-done | bytes 98336 | tf_op jit(solution)/shard_map/ppermute | solution.py:95
  139.5 3.0 %collective-permute-start.11 = (bf16[128,192]{1,0:T(8,128)(2,1)S(1)}, bf16[128,192]{1,0:T(8,128)(2,1)S(1)}, u32[]{:S(2)}, u32[]{:S(2)}) collective-permute-start(bf16[128,192]{1,0:T(8,128)(2,1)S(1)} %slice.228), channel_id=1, source_target_pairs={{0,16},{2,18},{4,20},{6,22},{8,24},{10,26},{12,28},{14,30},{16,0},... | collective-permute-start | bytes 147464 | tf_op jit(solution)/shard_map/ppermute | solution.py:95
  142.5 1.7 collective-permute-start.15
  145.4 2.3 collective-permute-done.15
  149.6 2.2 collective-permute-done.16
  151.9 1.5 collective-permute-start.17
  153.6 2.0 collective-permute-done.17
  157.7 1.5 collective-permute-done.18
  159.2 1.8 collective-permute-start.19
  161.3 2.4 collective-permute-done.19
  165.8 1.6 convert_add_fusion.2
  176.5 4.0 %collective-permute-done.40 = bf16[144,1536]{1,0:T(8,128)(2,1)S(1)} collective-permute-done((bf16[144,1536]{1,0:T(8,128)(2,1)S(1)}, bf16[144,1536]{1,0:T(8,128)(2,1)S(1)}, u32[]{:S(2)}, u32[]{:S(2)}) %collective-permute-start.40) | collective-permute-done | bytes 442400 | tf_op jit(solution)/shard_map/ppermute | solution.py:95
  180.6 1.5 collective-permute-start.41
  185.3 2.2 collective-permute-start.59
  189.1 1.5 collective-permute-start.32
  190.6 2.2 collective-permute-done.23
  197.9 2.8 %collective-permute-done.59 = bf16[192,576]{0,1:T(8,128)(2,1)S(1)} collective-permute-done((bf16[192,576]{0,1:T(8,128)(2,1)S(1)}, bf16[192,576]{0,1:T(8,128)(2,1)S(1)}, u32[]{:S(2)}, u32[]{:S(2)}) %collective-permute-start.59) | collective-permute-done | bytes 221216 | tf_op jit(solution)/shard_map/ppermute | solution.py:95
  202.0 1.6 collective-permute-start.25
  203.6 1.5 collective-permute-start.34
  205.2 1.8 collective-permute-done.25
  207.0 1.6 collective-permute-start.26
  210.2 1.8 collective-permute-done.26
  212.1 1.6 collective-permute-start.27
  214.3 2.4 collective-permute-start.36
  217.5 2.3 collective-permute-start.52
  220.8 1.9 collective-permute-start.28
  224.4 2.2 collective-permute-start.53
  229.7 1.6 collective-permute-start.54
  231.3 1.6 collective-permute-done.62
  234.5 2.1 collective-permute-start.29
  239.3 1.6 collective-permute-start.64
  241.0 4.6 %collective-permute-done.46 = bf16[72,1536]{1,0:T(8,128)(2,1)S(1)} collective-permute-done((bf16[72,1536]{1,0:T(8,128)(2,1)S(1)}, bf16[72,1536]{1,0:T(8,128)(2,1)S(1)}, u32[]{:S(2)}, u32[]{:S(2)}) %collective-permute-start.46) | collective-permute-done | bytes 221216 | tf_op jit(solution)/shard_map/ppermute | solution.py:95
  245.7 1.6 collective-permute-start.47
  247.3 1.5 collective-permute-done.55
  258.7 3.4 %collective-permute-done.65 = bf16[384,576]{0,1:T(8,128)(2,1)S(1)} collective-permute-done((bf16[384,576]{0,1:T(8,128)(2,1)S(1)}, bf16[384,576]{0,1:T(8,128)(2,1)S(1)}, u32[]{:S(2)}, u32[]{:S(2)}) %collective-permute-start.65) | collective-permute-done | bytes 442400 | tf_op jit(solution)/shard_map/ppermute | solution.py:95
  (360 shorter events, 83.2 us)
Async XLA Ops:
  7.2 66.8 %all-gather.4.cloned.1.call-start = ((), (), s32[]{:S(2)}) async-start(), calls=%async_computation | async-start | bytes 2654208 | tf_op jit(solution)/shard_map/all_gather | solution.py:372
  8.0 69.1 %all-gather.6.cloned.1.call-start = ((), (), s32[]{:S(2)}) async-start(), calls=%async_computation.1 | async-start | bytes 2654208 | tf_op jit(solution)/shard_map/all_gather | solution.py:373
  8.7 71.3 %all-gather.8.cloned.1.call-start = ((), (), s32[]{:S(2)}) async-start(), calls=%async_computation.2 | async-start | bytes 2654208 | tf_op jit(solution)/shard_map/all_gather | solution.py:374
  16.7 16.3 %collective-permute-start = (bf16[128,192]{1,0:T(8,128)(2,1)S(1)}, bf16[128,192]{1,0:T(8,128)(2,1)S(1)}, u32[]{:S(2)}, u32[]{:S(2)}) collective-permute-start(bf16[128,192]{1,0:T(8,128)(2,1)S(1)} %copy.63), channel_id=1, source_target_pairs={{0,16},{2,18},{4,20},{6,22},{8,24},{10,26},{12,28},{14,30},{16,0},... | collective-permute-start | bytes 147464 | tf_op jit(solution)/shard_map/ppermute | solution.py:95
  23.3 11.5 %collective-permute-start.4 = (bf16[128,192]{1,0:T(8,128)(2,1)S(1)}, bf16[128,192]{1,0:T(8,128)(2,1)S(1)}, u32[]{:S(2)}, u32[]{:S(2)}) collective-permute-start(bf16[128,192]{1,0:T(8,128)(2,1)S(1)} %copy.69), channel_id=1, source_target_pairs={{0,16},{2,18},{4,20},{6,22},{8,24},{10,26},{12,28},{14,30},{16,0},... | collective-permute-start | bytes 147464 | tf_op jit(solution)/shard_map/ppermute | solution.py:95
  33.0 10.2 %collective-permute-start.1 = (bf16[256,192]{1,0:T(8,128)(2,1)S(1)}, bf16[256,192]{1,0:T(8,128)(2,1)S(1)}, u32[]{:S(2)}, u32[]{:S(2)}) collective-permute-start(bf16[256,192]{1,0:T(8,128)(2,1)S(1)} %pad_maximum_fusion.5), channel_id=1, source_target_pairs={{0,8},{2,10},{4,12},{6,14},{8,0},{10,2},{12,4},{14,6},{16,24},{18,... | collective-permute-start | bytes 294920 | tf_op jit(solution)/shard_map/ppermute | solution.py:95
  34.8 6.6 %collective-permute-start.5 = (bf16[256,192]{1,0:T(8,128)(2,1)S(1)}, bf16[256,192]{1,0:T(8,128)(2,1)S(1)}, u32[]{:S(2)}, u32[]{:S(2)}) collective-permute-start(bf16[256,192]{1,0:T(8,128)(2,1)S(1)} %pad_maximum_fusion.6), channel_id=1, source_target_pairs={{0,8},{2,10},{4,12},{6,14},{8,0},{10,2},{12,4},{14,6},{16,24},{18,... | collective-permute-start | bytes 294920 | tf_op jit(solution)/shard_map/ppermute | solution.py:95
  41.4 7.6 %collective-permute-start.6 = (bf16[512,192]{1,0:T(8,128)(2,1)S(1)}, bf16[512,192]{1,0:T(8,128)(2,1)S(1)}, u32[]{:S(2)}, u32[]{:S(2)}) collective-permute-start(bf16[512,192]{1,0:T(8,128)(2,1)S(1)} %pad_maximum_fusion.4), channel_id=1, source_target_pairs={{0,2},{2,0},{4,6},{6,4},{8,10},{10,8},{12,14},{14,12},{16,18},{18,... | collective-permute-start | bytes 589832 | tf_op jit(solution)/shard_map/ppermute | solution.py:95
  43.2 7.7 %collective-permute-start.2 = (bf16[512,192]{1,0:T(8,128)(2,1)S(1)}, bf16[512,192]{1,0:T(8,128)(2,1)S(1)}, u32[]{:S(2)}, u32[]{:S(2)}) collective-permute-start(bf16[512,192]{1,0:T(8,128)(2,1)S(1)} %pad_maximum_fusion.3), channel_id=1, source_target_pairs={{0,4},{2,6},{4,0},{6,2},{8,12},{10,14},{12,8},{14,10},{16,20},{18,... | collective-permute-start | bytes 589832 | tf_op jit(solution)/shard_map/ppermute | solution.py:95
  49.1 12.6 %collective-permute-start.7 = (bf16[1024,192]{1,0:T(8,128)(2,1)S(1)}, bf16[1024,192]{1,0:T(8,128)(2,1)S(1)}, u32[]{:S(2)}, u32[]{:S(2)}) collective-permute-start(bf16[1024,192]{1,0:T(8,128)(2,1)S(1)} %pad_maximum_fusion.1), channel_id=1, source_target_pairs={{0,4},{2,6},{4,0},{6,2},{8,12},{10,14},{12,8},{14,10},{16,20},{18,... | collective-permute-start | bytes 1179656 | tf_op jit(solution)/shard_map/ppermute | solution.py:95
  51.0 12.0 %collective-permute-start.3 = (bf16[1024,192]{1,0:T(8,128)(2,1)S(1)}, bf16[1024,192]{1,0:T(8,128)(2,1)S(1)}, u32[]{:S(2)}, u32[]{:S(2)}) collective-permute-start(bf16[1024,192]{1,0:T(8,128)(2,1)S(1)} %pad_maximum_fusion), channel_id=1, source_target_pairs={{0,2},{2,0},{4,6},{6,4},{8,10},{10,8},{12,14},{14,12},{16,18},{18,... | collective-permute-start | bytes 1179656 | tf_op jit(solution)/shard_map/ppermute | solution.py:95
  111.2 13.6 %collective-permute-start.8 = (bf16[1024,192]{1,0:T(8,128)(2,1)S(1)}, bf16[1024,192]{1,0:T(8,128)(2,1)S(1)}, u32[]{:S(2)}, u32[]{:S(2)}) collective-permute-start(bf16[1024,192]{1,0:T(8,128)(2,1)S(1)} %slice.130), channel_id=1, source_target_pairs={{0,2},{2,0},{4,6},{6,4},{8,10},{10,8},{12,14},{14,12},{16,18},{18,... | collective-permute-start | bytes 1179656 | tf_op jit(solution)/shard_map/ppermute | solution.py:95
  112.9 13.7 %collective-permute-start.12 = (bf16[1024,192]{1,0:T(8,128)(2,1)S(1)}, bf16[1024,192]{1,0:T(8,128)(2,1)S(1)}, u32[]{:S(2)}, u32[]{:S(2)}) collective-permute-start(bf16[1024,192]{1,0:T(8,128)(2,1)S(1)} %pad_maximum_fusion.2), channel_id=1, source_target_pairs={{0,4},{2,6},{4,0},{6,2},{8,12},{10,14},{12,8},{14,10},{16,20},{18,... | collective-permute-start | bytes 1179656 | tf_op jit(solution)/shard_map/ppermute | solution.py:95
  116.5 49.3 %collective-permute-start.39 = (bf16[288,1536]{1,0:T(8,128)(2,1)}, bf16[288,1536]{1,0:T(8,128)(2,1)}, u32[]{:S(2)}, u32[]{:S(2)}) collective-permute-start(bf16[288,1536]{1,0:T(8,128)(2,1)} %dynamic-slice_convert_fusion.2), channel_id=1, source_target_pairs={{0,1},{1,0},{2,3},{3,2},{4,5},{5,4},{6,7},{7,6},{8,9},{9,8},{10,11... | collective-permute-start | bytes 2654216 | tf_op jit(solution)/shard_map/ppermute | solution.py:144
  119.0 49.6 %collective-permute-start.48 = (bf16[288,1536]{1,0:T(8,128)(2,1)}, bf16[288,1536]{1,0:T(8,128)(2,1)}, u32[]{:S(2)}, u32[]{:S(2)}) collective-permute-start(bf16[288,1536]{1,0:T(8,128)(2,1)} %dynamic-slice_convert_fusion.1), channel_id=1, source_target_pairs={{0,1},{1,0},{2,3},{3,2},{4,5},{5,4},{6,7},{7,6},{8,9},{9,8},{10,11... | collective-permute-start | bytes 2654216 | tf_op jit(solution)/shard_map/ppermute | solution.py:144
  121.2 50.1 %collective-permute-start.57 = (bf16[768,576]{0,1:T(8,128)(2,1)}, bf16[768,576]{0,1:T(8,128)(2,1)}, u32[]{:S(2)}, u32[]{:S(2)}) collective-permute-start(bf16[768,576]{0,1:T(8,128)(2,1)} %dynamic-slice_convert_fusion), channel_id=1, source_target_pairs={{0,1},{1,0},{2,3},{3,2},{4,5},{5,4},{6,7},{7,6},{8,9},{9,8},{10,11... | collective-permute-start | bytes 2654216 | tf_op jit(solution)/shard_map/ppermute | solution.py:144
  125.0 8.3 %collective-permute-start.9 = (bf16[512,192]{1,0:T(8,128)(2,1)S(1)}, bf16[512,192]{1,0:T(8,128)(2,1)S(1)}, u32[]{:S(2)}, u32[]{:S(2)}) collective-permute-start(bf16[512,192]{1,0:T(8,128)(2,1)S(1)} %slice.224), channel_id=1, source_target_pairs={{0,4},{2,6},{4,0},{6,2},{8,12},{10,14},{12,8},{14,10},{16,20},{18,... | collective-permute-start | bytes 589832 | tf_op jit(solution)/shard_map/ppermute | solution.py:95
  126.7 8.3 %collective-permute-start.13 = (bf16[512,192]{1,0:T(8,128)(2,1)S(1)}, bf16[512,192]{1,0:T(8,128)(2,1)S(1)}, u32[]{:S(2)}, u32[]{:S(2)}) collective-permute-start(bf16[512,192]{1,0:T(8,128)(2,1)S(1)} %slice.223), channel_id=1, source_target_pairs={{0,2},{2,0},{4,6},{6,4},{8,10},{10,8},{12,14},{14,12},{16,18},{18,... | collective-permute-start | bytes 589832 | tf_op jit(solution)/shard_map/ppermute | solution.py:95
  133.3 6.1 %collective-permute-start.10 = (bf16[256,192]{1,0:T(8,128)(2,1)S(1)}, bf16[256,192]{1,0:T(8,128)(2,1)S(1)}, u32[]{:S(2)}, u32[]{:S(2)}) collective-permute-start(bf16[256,192]{1,0:T(8,128)(2,1)S(1)} %slice.226), channel_id=1, source_target_pairs={{0,8},{2,10},{4,12},{6,14},{8,0},{10,2},{12,4},{14,6},{16,24},{18,... | collective-permute-start | bytes 294920 | tf_op jit(solution)/shard_map/ppermute | solution.py:95
  135.1 7.3 %collective-permute-start.14 = (bf16[256,192]{1,0:T(8,128)(2,1)S(1)}, bf16[256,192]{1,0:T(8,128)(2,1)S(1)}, u32[]{:S(2)}, u32[]{:S(2)}) collective-permute-start(bf16[256,192]{1,0:T(8,128)(2,1)S(1)} %slice.225), channel_id=1, source_target_pairs={{0,8},{2,10},{4,12},{6,14},{8,0},{10,2},{12,4},{14,6},{16,24},{18,... | collective-permute-start | bytes 294920 | tf_op jit(solution)/shard_map/ppermute | solution.py:95
  139.5 5.6 %collective-permute-start.11 = (bf16[128,192]{1,0:T(8,128)(2,1)S(1)}, bf16[128,192]{1,0:T(8,128)(2,1)S(1)}, u32[]{:S(2)}, u32[]{:S(2)}) collective-permute-start(bf16[128,192]{1,0:T(8,128)(2,1)S(1)} %slice.228), channel_id=1, source_target_pairs={{0,16},{2,18},{4,20},{6,22},{8,24},{10,26},{12,28},{14,30},{16,0},... | collective-permute-start | bytes 147464 | tf_op jit(solution)/shard_map/ppermute | solution.py:95
  142.5 5.2 %collective-permute-start.15 = (bf16[128,192]{1,0:T(8,128)(2,1)S(1)}, bf16[128,192]{1,0:T(8,128)(2,1)S(1)}, u32[]{:S(2)}, u32[]{:S(2)}) collective-permute-start(bf16[128,192]{1,0:T(8,128)(2,1)S(1)} %slice.227), channel_id=1, source_target_pairs={{0,16},{2,18},{4,20},{6,22},{8,24},{10,26},{12,28},{14,30},{16,0},... | collective-permute-start | bytes 147464 | tf_op jit(solution)/shard_map/ppermute | solution.py:95
  153.5 20.7 %collective-permute-start.21 = (bf16[288,768]{1,0:T(8,128)(2,1)S(1)}, bf16[288,768]{1,0:T(8,128)(2,1)S(1)}, u32[]{:S(2)}, u32[]{:S(2)}) collective-permute-start(bf16[288,768]{1,0:T(8,128)(2,1)S(1)} %fusion.7), channel_id=1, source_target_pairs={{0,1},{1,0},{2,3},{3,2},{4,5},{5,4},{6,7},{7,6},{8,9},{9,8},{10,11... | collective-permute-start | bytes 1327112 | tf_op jit(solution)/shard_map/ppermute | solution.py:144
  164.9 10.4 %collective-permute-start.30 = (bf16[288,768]{1,0:T(8,128)(2,1)S(1)}, bf16[288,768]{1,0:T(8,128)(2,1)S(1)}, u32[]{:S(2)}, u32[]{:S(2)}) collective-permute-start(bf16[288,768]{1,0:T(8,128)(2,1)S(1)} %fusion.3), channel_id=1, source_target_pairs={{0,1},{1,0},{2,3},{3,2},{4,5},{5,4},{6,7},{7,6},{8,9},{9,8},{10,11... | collective-permute-start | bytes 1327112 | tf_op jit(solution)/shard_map/ppermute | solution.py:144
  167.4 13.1 %collective-permute-start.40 = (bf16[144,1536]{1,0:T(8,128)(2,1)S(1)}, bf16[144,1536]{1,0:T(8,128)(2,1)S(1)}, u32[]{:S(2)}, u32[]{:S(2)}) collective-permute-start(bf16[144,1536]{1,0:T(8,128)(2,1)S(1)} %dynamic-slice_convert_fusion.5), channel_id=1, source_target_pairs={{0,2},{2,0},{4,6},{6,4},{8,10},{10,8},{12,14},{14,12},{16,18},{18,... | collective-permute-start | bytes 1327112 | tf_op jit(solution)/shard_map/ppermute | solution.py:95
  170.1 13.1 %collective-permute-start.49 = (bf16[144,1536]{1,0:T(8,128)(2,1)S(1)}, bf16[144,1536]{1,0:T(8,128)(2,1)S(1)}, u32[]{:S(2)}, u32[]{:S(2)}) collective-permute-start(bf16[144,1536]{1,0:T(8,128)(2,1)S(1)} %dynamic-slice_convert_fusion.4), channel_id=1, source_target_pairs={{0,4},{2,6},{4,0},{6,2},{8,12},{10,14},{12,8},{14,10},{16,20},{18,... | collective-permute-start | bytes 1327112 | tf_op jit(solution)/shard_map/ppermute | solution.py:95
  172.9 12.2 %collective-permute-start.58 = (bf16[384,576]{0,1:T(8,128)(2,1)S(1)}, bf16[384,576]{0,1:T(8,128)(2,1)S(1)}, u32[]{:S(2)}, u32[]{:S(2)}) collective-permute-start(bf16[384,576]{0,1:T(8,128)(2,1)S(1)} %dynamic-slice_convert_fusion.3), channel_id=1, source_target_pairs={{0,8},{2,10},{4,12},{6,14},{8,0},{10,2},{12,4},{14,6},{16,24},{18,... | collective-permute-start | bytes 1327112 | tf_op jit(solution)/shard_map/ppermute | solution.py:95
  174.4 13.5 %collective-permute-start.22 = (bf16[144,768]{1,0:T(8,128)(2,1)S(1)}, bf16[144,768]{1,0:T(8,128)(2,1)S(1)}, u32[]{:S(2)}, u32[]{:S(2)}) collective-permute-start(bf16[144,768]{1,0:T(8,128)(2,1)S(1)} %dynamic-slice_convert_fusion.10), channel_id=1, source_target_pairs={{0,4},{2,6},{4,0},{6,2},{8,12},{10,14},{12,8},{14,10},{16,20},{18,... | collective-permute-start | bytes 663560 | tf_op jit(solution)/shard_map/ppermute | solution.py:95
  175.5 13.5 %collective-permute-start.31 = (bf16[144,768]{1,0:T(8,128)(2,1)S(1)}, bf16[144,768]{1,0:T(8,128)(2,1)S(1)}, u32[]{:S(2)}, u32[]{:S(2)}) collective-permute-start(bf16[144,768]{1,0:T(8,128)(2,1)S(1)} %dynamic-slice_convert_fusion.9), channel_id=1, source_target_pairs={{0,2},{2,0},{4,6},{6,4},{8,10},{10,8},{12,14},{14,12},{16,18},{18,... | collective-permute-start | bytes 663560 | tf_op jit(solution)/shard_map/ppermute | solution.py:95
  180.6 15.0 %collective-permute-start.41 = (bf16[72,1536]{1,0:T(8,128)(2,1)S(1)}, bf16[72,1536]{1,0:T(8,128)(2,1)S(1)}, u32[]{:S(2)}, u32[]{:S(2)}) collective-permute-start(bf16[72,1536]{1,0:T(8,128)(2,1)S(1)} %dynamic-slice_convert_fusion.8), channel_id=1, source_target_pairs={{0,4},{2,6},{4,0},{6,2},{8,12},{10,14},{12,8},{14,10},{16,20},{18,... | collective-permute-start | bytes 663560 | tf_op jit(solution)/shard_map/ppermute | solution.py:95
  183.3 13.3 %collective-permute-start.50 = (bf16[72,1536]{1,0:T(8,128)(2,1)S(1)}, bf16[72,1536]{1,0:T(8,128)(2,1)S(1)}, u32[]{:S(2)}, u32[]{:S(2)}) collective-permute-start(bf16[72,1536]{1,0:T(8,128)(2,1)S(1)} %dynamic-slice_convert_fusion.7), channel_id=1, source_target_pairs={{0,2},{2,0},{4,6},{6,4},{8,10},{10,8},{12,14},{14,12},{16,18},{18,... | collective-permute-start | bytes 663560 | tf_op jit(solution)/shard_map/ppermute | solution.py:95
  185.3 15.5 %collective-permute-start.59 = (bf16[192,576]{0,1:T(8,128)(2,1)S(1)}, bf16[192,576]{0,1:T(8,128)(2,1)S(1)}, u32[]{:S(2)}, u32[]{:S(2)}) collective-permute-start(bf16[192,576]{0,1:T(8,128)(2,1)S(1)} %dynamic-slice_convert_fusion.6), channel_id=1, source_target_pairs={{0,16},{2,18},{4,20},{6,22},{8,24},{10,26},{12,28},{14,30},{16,0},... | collective-permute-start | bytes 663560 | tf_op jit(solution)/shard_map/ppermute | solution.py:95
  188.0 4.8 %collective-permute-start.23 = (bf16[72,768]{1,0:T(8,128)(2,1)S(1)}, bf16[72,768]{1,0:T(8,128)(2,1)S(1)}, u32[]{:S(2)}, u32[]{:S(2)}) collective-permute-start(bf16[72,768]{1,0:T(8,128)(2,1)S(1)} %dynamic-slice_convert_fusion.16), channel_id=1, source_target_pairs={{0,2},{2,0},{4,6},{6,4},{8,10},{10,8},{12,14},{14,12},{16,18},{18,... | collective-permute-start | bytes 331784 | tf_op jit(solution)/shard_map/ppermute | solution.py:95
  189.1 5.2 %collective-permute-start.32 = (bf16[72,768]{1,0:T(8,128)(2,1)S(1)}, bf16[72,768]{1,0:T(8,128)(2,1)S(1)}, u32[]{:S(2)}, u32[]{:S(2)}) collective-permute-start(bf16[72,768]{1,0:T(8,128)(2,1)S(1)} %dynamic-slice_convert_fusion.15), channel_id=1, source_target_pairs={{0,4},{2,6},{4,0},{6,2},{8,12},{10,14},{12,8},{14,10},{16,20},{18,... | collective-permute-start | bytes 331784 | tf_op jit(solution)/shard_map/ppermute | solution.py:95
  192.9 9.0 %collective-permute-start.24 = (bf16[72,384]{1,0:T(8,128)(2,1)S(1)}, bf16[72,384]{1,0:T(8,128)(2,1)S(1)}, u32[]{:S(2)}, u32[]{:S(2)}) collective-permute-start(bf16[72,384]{1,0:T(8,128)(2,1)S(1)} %dynamic-slice_convert_fusion.20), channel_id=1, source_target_pairs={{0,8},{2,10},{4,12},{6,14},{8,0},{10,2},{12,4},{14,6},{16,24},{18,... | collective-permute-start | bytes 165896 | tf_op jit(solution)/shard_map/ppermute | solution.py:95
  194.3 9.2 %collective-permute-start.33 = (bf16[72,384]{1,0:T(8,128)(2,1)S(1)}, bf16[72,384]{1,0:T(8,128)(2,1)S(1)}, u32[]{:S(2)}, u32[]{:S(2)}) collective-permute-start(bf16[72,384]{1,0:T(8,128)(2,1)S(1)} %dynamic-slice_convert_fusion.19), channel_id=1, source_target_pairs={{0,8},{2,10},{4,12},{6,14},{8,0},{10,2},{12,4},{14,6},{16,24},{18,... | collective-permute-start | bytes 165896 | tf_op jit(solution)/shard_map/ppermute | solution.py:95
  195.7 21.0 %collective-permute-start.42 = (bf16[72,768]{1,0:T(8,128)(2,1)S(1)}, bf16[72,768]{1,0:T(8,128)(2,1)S(1)}, u32[]{:S(2)}, u32[]{:S(2)}) collective-permute-start(bf16[72,768]{1,0:T(8,128)(2,1)S(1)} %dynamic-slice_convert_fusion.14), channel_id=1, source_target_pairs={{0,8},{2,10},{4,12},{6,14},{8,0},{10,2},{12,4},{14,6},{16,24},{18,... | collective-permute-start | bytes 331784 | tf_op jit(solution)/shard_map/ppermute | solution.py:95
  196.7 20.8 %collective-permute-start.51 = (bf16[72,768]{1,0:T(8,128)(2,1)S(1)}, bf16[72,768]{1,0:T(8,128)(2,1)S(1)}, u32[]{:S(2)}, u32[]{:S(2)}) collective-permute-start(bf16[72,768]{1,0:T(8,128)(2,1)S(1)} %dynamic-slice_convert_fusion.13), channel_id=1, source_target_pairs={{0,8},{2,10},{4,12},{6,14},{8,0},{10,2},{12,4},{14,6},{16,24},{18,... | collective-permute-start | bytes 331784 | tf_op jit(solution)/shard_map/ppermute | solution.py:95
  201.1 18.7 %collective-permute-start.60 = (bf16[96,576]{0,1:T(8,128)(2,1)S(1)}, bf16[96,576]{0,1:T(8,128)(2,1)S(1)}, u32[]{:S(2)}, u32[]{:S(2)}) collective-permute-start(bf16[96,576]{0,1:T(8,128)(2,1)S(1)} %dynamic-slice_convert_fusion.12), channel_id=1, source_target_pairs={{0,2},{2,0},{4,6},{6,4},{8,10},{10,8},{12,14},{14,12},{16,18},{18,... | collective-permute-start | bytes 331784 | tf_op jit(solution)/shard_map/ppermute | solution.py:95
  202.0 5.0 %collective-permute-start.25 = (bf16[72,192]{1,0:T(8,128)(2,1)S(1)}, bf16[72,192]{1,0:T(8,128)(2,1)S(1)}, u32[]{:S(2)}, u32[]{:S(2)}) collective-permute-start(bf16[72,192]{1,0:T(8,128)(2,1)S(1)} %dynamic-slice_convert_fusion.22), channel_id=1, source_target_pairs={{0,16},{2,18},{4,20},{6,22},{8,24},{10,26},{12,28},{14,30},{16,0},... | collective-permute-start | bytes 82952 | tf_op jit(solution)/shard_map/ppermute | solution.py:95
  203.6 5.5 %collective-permute-start.34 = (bf16[72,192]{1,0:T(8,128)(2,1)S(1)}, bf16[72,192]{1,0:T(8,128)(2,1)S(1)}, u32[]{:S(2)}, u32[]{:S(2)}) collective-permute-start(bf16[72,192]{1,0:T(8,128)(2,1)S(1)} %dynamic-slice_convert_fusion.21), channel_id=1, source_target_pairs={{0,16},{2,18},{4,20},{6,22},{8,24},{10,26},{12,28},{14,30},{16,0},... | collective-permute-start | bytes 82952 | tf_op jit(solution)/shard_map/ppermute | solution.py:95
  207.0 4.9 %collective-permute-start.26 = (bf16[72,192]{1,0:T(8,128)(2,1)S(1)}, bf16[72,192]{1,0:T(8,128)(2,1)S(1)}, u32[]{:S(2)}, u32[]{:S(2)}) collective-permute-start(bf16[72,192]{1,0:T(8,128)(2,1)S(1)} %add_convert_fusion.5), channel_id=1, source_target_pairs={{0,16},{2,18},{4,20},{6,22},{8,24},{10,26},{12,28},{14,30},{16,0},... | collective-permute-start | bytes 82952 | tf_op jit(solution)/shard_map/ppermute | solution.py:95
  209.3 4.9 %collective-permute-start.35 = (bf16[72,192]{1,0:T(8,128)(2,1)S(1)}, bf16[72,192]{1,0:T(8,128)(2,1)S(1)}, u32[]{:S(2)}, u32[]{:S(2)}) collective-permute-start(bf16[72,192]{1,0:T(8,128)(2,1)S(1)} %add_convert_fusion.4), channel_id=1, source_target_pairs={{0,16},{2,18},{4,20},{6,22},{8,24},{10,26},{12,28},{14,30},{16,0},... | collective-permute-start | bytes 82952 | tf_op jit(solution)/shard_map/ppermute | solution.py:95
  212.1 8.7 %collective-permute-start.27 = (bf16[72,384]{1,0:T(8,128)(2,1)S(1)}, bf16[72,384]{1,0:T(8,128)(2,1)S(1)}, u32[]{:S(2)}, u32[]{:S(2)}) collective-permute-start(bf16[72,384]{1,0:T(8,128)(2,1)S(1)} %maximum_select_fusion.18), channel_id=1, source_target_pairs={{0,8},{2,10},{4,12},{6,14},{8,0},{10,2},{12,4},{14,6},{16,24},{18,... | collective-permute-start | bytes 165896 | tf_op jit(solution)/shard_map/ppermute | solution.py:95
  214.3 8.5 %collective-permute-start.36 = (bf16[72,384]{1,0:T(8,128)(2,1)S(1)}, bf16[72,384]{1,0:T(8,128)(2,1)S(1)}, u32[]{:S(2)}, u32[]{:S(2)}) collective-permute-start(bf16[72,384]{1,0:T(8,128)(2,1)S(1)} %maximum_select_fusion.19), channel_id=1, source_target_pairs={{0,8},{2,10},{4,12},{6,14},{8,0},{10,2},{12,4},{14,6},{16,24},{18,... | collective-permute-start | bytes 165896 | tf_op jit(solution)/shard_map/ppermute | solution.py:95
  216.7 6.8 %collective-permute-start.43 = (bf16[72,384]{1,0:T(8,128)(2,1)S(1)}, bf16[72,384]{1,0:T(8,128)(2,1)S(1)}, u32[]{:S(2)}, u32[]{:S(2)}) collective-permute-start(bf16[72,384]{1,0:T(8,128)(2,1)S(1)} %dynamic-slice_convert_fusion.18), channel_id=1, source_target_pairs={{0,16},{2,18},{4,20},{6,22},{8,24},{10,26},{12,28},{14,30},{16,0},... | collective-permute-start | bytes 165896 | tf_op jit(solution)/shard_map/ppermute | solution.py:95
  217.5 6.9 %collective-permute-start.52 = (bf16[72,384]{1,0:T(8,128)(2,1)S(1)}, bf16[72,384]{1,0:T(8,128)(2,1)S(1)}, u32[]{:S(2)}, u32[]{:S(2)}) collective-permute-start(bf16[72,384]{1,0:T(8,128)(2,1)S(1)} %dynamic-slice_convert_fusion.17), channel_id=1, source_target_pairs={{0,16},{2,18},{4,20},{6,22},{8,24},{10,26},{12,28},{14,30},{16,0},... | collective-permute-start | bytes 165896 | tf_op jit(solution)/shard_map/ppermute | solution.py:95
  220.1 6.5 %collective-permute-start.61 = (bf16[48,576]{0,1:T(8,128)(2,1)S(1)}, bf16[48,576]{0,1:T(8,128)(2,1)S(1)}, u32[]{:S(2)}, u32[]{:S(2)}) collective-permute-start(bf16[48,576]{0,1:T(8,128)(2,1)S(1)} %dynamic-slice_convert_fusion.11), channel_id=1, source_target_pairs={{0,4},{2,6},{4,0},{6,2},{8,12},{10,14},{12,8},{14,10},{16,20},{18,... | collective-permute-start | bytes 165896 | tf_op jit(solution)/shard_map/ppermute | solution.py:95
  220.8 13.6 %collective-permute-start.28 = (bf16[72,768]{1,0:T(8,128)(2,1)S(1)}, bf16[72,768]{1,0:T(8,128)(2,1)S(1)}, u32[]{:S(2)}, u32[]{:S(2)}) collective-permute-start(bf16[72,768]{1,0:T(8,128)(2,1)S(1)} %maximum_select_fusion.14), channel_id=1, source_target_pairs={{0,2},{2,0},{4,6},{6,4},{8,10},{10,8},{12,14},{14,12},{16,18},{18,... | collective-permute-start | bytes 331784 | tf_op jit(solution)/shard_map/ppermute | solution.py:95
  222.8 13.8 %collective-permute-start.37 = (bf16[72,768]{1,0:T(8,128)(2,1)S(1)}, bf16[72,768]{1,0:T(8,128)(2,1)S(1)}, u32[]{:S(2)}, u32[]{:S(2)}) collective-permute-start(bf16[72,768]{1,0:T(8,128)(2,1)S(1)} %maximum_select_fusion.15), channel_id=1, source_target_pairs={{0,4},{2,6},{4,0},{6,2},{8,12},{10,14},{12,8},{14,10},{16,20},{18,... | collective-permute-start | bytes 331784 | tf_op jit(solution)/shard_map/ppermute | solution.py:95
  223.6 5.5 %collective-permute-start.44 = (bf16[72,384]{1,0:T(8,128)(2,1)S(1)}, bf16[72,384]{1,0:T(8,128)(2,1)S(1)}, u32[]{:S(2)}, u32[]{:S(2)}) collective-permute-start(bf16[72,384]{1,0:T(8,128)(2,1)S(1)} %add_convert_fusion.3), channel_id=1, source_target_pairs={{0,16},{2,18},{4,20},{6,22},{8,24},{10,26},{12,28},{14,30},{16,0},... | collective-permute-start | bytes 165896 | tf_op jit(solution)/shard_map/ppermute | solution.py:95
  224.4 5.3 %collective-permute-start.53 = (bf16[72,384]{1,0:T(8,128)(2,1)S(1)}, bf16[72,384]{1,0:T(8,128)(2,1)S(1)}, u32[]{:S(2)}, u32[]{:S(2)}) collective-permute-start(bf16[72,384]{1,0:T(8,128)(2,1)S(1)} %add_convert_fusion.2), channel_id=1, source_target_pairs={{0,16},{2,18},{4,20},{6,22},{8,24},{10,26},{12,28},{14,30},{16,0},... | collective-permute-start | bytes 165896 | tf_op jit(solution)/shard_map/ppermute | solution.py:95
  226.8 6.1 %collective-permute-start.62 = (bf16[48,576]{0,1:T(8,128)(2,1)S(1)}, bf16[48,576]{0,1:T(8,128)(2,1)S(1)}, u32[]{:S(2)}, u32[]{:S(2)}) collective-permute-start(bf16[48,576]{0,1:T(8,128)(2,1)S(1)} %add_convert_fusion), channel_id=1, source_target_pairs={{0,4},{2,6},{4,0},{6,2},{8,12},{10,14},{12,8},{14,10},{16,20},{18,... | collective-permute-start | bytes 165896 | tf_op jit(solution)/shard_map/ppermute | solution.py:95
  229.1 7.9 %collective-permute-start.45 = (bf16[72,768]{1,0:T(8,128)(2,1)S(1)}, bf16[72,768]{1,0:T(8,128)(2,1)S(1)}, u32[]{:S(2)}, u32[]{:S(2)}) collective-permute-start(bf16[72,768]{1,0:T(8,128)(2,1)S(1)} %maximum_select_fusion.16), channel_id=1, source_target_pairs={{0,8},{2,10},{4,12},{6,14},{8,0},{10,2},{12,4},{14,6},{16,24},{18,... | collective-permute-start | bytes 331784 | tf_op jit(solution)/shard_map/ppermute | solution.py:95
  229.7 7.9 %collective-permute-start.54 = (bf16[72,768]{1,0:T(8,128)(2,1)S(1)}, bf16[72,768]{1,0:T(8,128)(2,1)S(1)}, u32[]{:S(2)}, u32[]{:S(2)}) collective-permute-start(bf16[72,768]{1,0:T(8,128)(2,1)S(1)} %maximum_select_fusion.17), channel_id=1, source_target_pairs={{0,8},{2,10},{4,12},{6,14},{8,0},{10,2},{12,4},{14,6},{16,24},{18,... | collective-permute-start | bytes 331784 | tf_op jit(solution)/shard_map/ppermute | solution.py:95
  233.1 5.9 %collective-permute-start.63 = (bf16[96,576]{0,1:T(8,128)(2,1)S(1)}, bf16[96,576]{0,1:T(8,128)(2,1)S(1)}, u32[]{:S(2)}, u32[]{:S(2)}) collective-permute-start(bf16[96,576]{0,1:T(8,128)(2,1)S(1)} %maximum_select_fusion.13), channel_id=1, source_target_pairs={{0,2},{2,0},{4,6},{6,4},{8,10},{10,8},{12,14},{14,12},{16,18},{18,... | collective-permute-start | bytes 331784 | tf_op jit(solution)/shard_map/ppermute | solution.py:95
  234.5 6.5 %collective-permute-start.29 = (bf16[144,768]{1,0:T(8,128)(2,1)S(1)}, bf16[144,768]{1,0:T(8,128)(2,1)S(1)}, u32[]{:S(2)}, u32[]{:S(2)}) collective-permute-start(bf16[144,768]{1,0:T(8,128)(2,1)S(1)} %maximum_select_fusion.9), channel_id=1, source_target_pairs={{0,4},{2,6},{4,0},{6,2},{8,12},{10,14},{12,8},{14,10},{16,20},{18,... | collective-permute-start | bytes 663560 | tf_op jit(solution)/shard_map/ppermute | solution.py:95
  236.6 13.0 %collective-permute-start.38 = (bf16[144,768]{1,0:T(8,128)(2,1)S(1)}, bf16[144,768]{1,0:T(8,128)(2,1)S(1)}, u32[]{:S(2)}, u32[]{:S(2)}) collective-permute-start(bf16[144,768]{1,0:T(8,128)(2,1)S(1)} %maximum_select_fusion.10), channel_id=1, source_target_pairs={{0,2},{2,0},{4,6},{6,4},{8,10},{10,8},{12,14},{14,12},{16,18},{18,... | collective-permute-start | bytes 663560 | tf_op jit(solution)/shard_map/ppermute | solution.py:95
  237.1 8.6 %collective-permute-start.46 = (bf16[72,1536]{1,0:T(8,128)(2,1)S(1)}, bf16[72,1536]{1,0:T(8,128)(2,1)S(1)}, u32[]{:S(2)}, u32[]{:S(2)}) collective-permute-start(bf16[72,1536]{1,0:T(8,128)(2,1)S(1)} %maximum_select_fusion.11), channel_id=1, source_target_pairs={{0,4},{2,6},{4,0},{6,2},{8,12},{10,14},{12,8},{14,10},{16,20},{18,... | collective-permute-start | bytes 663560 | tf_op jit(solution)/shard_map/ppermute | solution.py:95
  237.7 11.1 %collective-permute-start.55 = (bf16[72,1536]{1,0:T(8,128)(2,1)S(1)}, bf16[72,1536]{1,0:T(8,128)(2,1)S(1)}, u32[]{:S(2)}, u32[]{:S(2)}) collective-permute-start(bf16[72,1536]{1,0:T(8,128)(2,1)S(1)} %maximum_select_fusion.12), channel_id=1, source_target_pairs={{0,2},{2,0},{4,6},{6,4},{8,10},{10,8},{12,14},{14,12},{16,18},{18,... | collective-permute-start | bytes 663560 | tf_op jit(solution)/shard_map/ppermute | solution.py:95
  239.3 14.0 %collective-permute-start.64 = (bf16[192,576]{0,1:T(8,128)(2,1)S(1)}, bf16[192,576]{0,1:T(8,128)(2,1)S(1)}, u32[]{:S(2)}, u32[]{:S(2)}) collective-permute-start(bf16[192,576]{0,1:T(8,128)(2,1)S(1)} %maximum_select_fusion.8), channel_id=1, source_target_pairs={{0,16},{2,18},{4,20},{6,22},{8,24},{10,26},{12,28},{14,30},{16,0},... | collective-permute-start | bytes 663560 | tf_op jit(solution)/shard_map/ppermute | solution.py:95
  245.7 8.8 %collective-permute-start.47 = (bf16[144,1536]{1,0:T(8,128)(2,1)S(1)}, bf16[144,1536]{1,0:T(8,128)(2,1)S(1)}, u32[]{:S(2)}, u32[]{:S(2)}) collective-permute-start(bf16[144,1536]{1,0:T(8,128)(2,1)S(1)} %maximum_select_fusion.5), channel_id=1, source_target_pairs={{0,2},{2,0},{4,6},{6,4},{8,10},{10,8},{12,14},{14,12},{16,18},{18,... | collective-permute-start | bytes 1327112 | tf_op jit(solution)/shard_map/ppermute | solution.py:95
  248.9 8.4 %collective-permute-start.56 = (bf16[144,1536]{1,0:T(8,128)(2,1)S(1)}, bf16[144,1536]{1,0:T(8,128)(2,1)S(1)}, u32[]{:S(2)}, u32[]{:S(2)}) collective-permute-start(bf16[144,1536]{1,0:T(8,128)(2,1)S(1)} %maximum_select_fusion.6), channel_id=1, source_target_pairs={{0,4},{2,6},{4,0},{6,2},{8,12},{10,14},{12,8},{14,10},{16,20},{18,... | collective-permute-start | bytes 1327112 | tf_op jit(solution)/shard_map/ppermute | solution.py:95
  253.7 8.4 %collective-permute-start.65 = (bf16[384,576]{0,1:T(8,128)(2,1)S(1)}, bf16[384,576]{0,1:T(8,128)(2,1)S(1)}, u32[]{:S(2)}, u32[]{:S(2)}) collective-permute-start(bf16[384,576]{0,1:T(8,128)(2,1)S(1)} %maximum_select_fusion.7), channel_id=1, source_target_pairs={{0,8},{2,10},{4,12},{6,14},{8,0},{10,2},{12,4},{14,6},{16,24},{18,... | collective-permute-start | bytes 1327112 | tf_op jit(solution)/shard_map/ppermute | solution.py:95
  (55 other events, 307.8 us)
Sparse Core Ops, SparseCore 0:
  9.6 12.7 all-gather.3
  24.0 11.2 all-gather.5
  36.8 11.2 all-gather.7

commit v3 on v2

--- a/solution.py
+++ b/solution.py
@@ -106,11 +106,31 @@
     return held
 
 
+def lockstep(*trees):
+    results = [None] * len(trees)
+    running = list(range(len(trees)))
+    sent = [None] * len(trees)
+    while running:
+        held = {}
+        for place in list(running):
+            try:
+                held[place] = trees[place].send(sent[place])
+            except StopIteration as done:
+                results[place] = done.value
+                running.remove(place)
+        if held:
+            tied = lax.optimization_barrier(tuple(held.values()))
+            for place, value in zip(held, tied):
+                sent[place] = value
+    return results
+
+
 def scatter_tree(slots, order):
     held = slots.astype(jnp.float32)
     for bit in order[::-1]:
         half = held.shape[0] // 2
         held = held[:half] + swap(held[half:].astype(jnp.bfloat16), bit).astype(jnp.float32)
+        held = yield held
     return held
 
 
@@ -145,32 +165,56 @@
     return own
 
 
-def reduce_tree(partial, order):
+def halve_tree(partial, order):
     held = partial
-    path = []
-    for bit in order:
-        axis = 0 if held.shape[0] % 16 == 0 else 1
+    for bit, axis in tree_path(partial.shape, order):
         half = held.shape[axis] // 2
         mine = own_bit(bit)
         kept = lax.dynamic_slice_in_dim(held, mine * half, half, axis)
         sent = lax.dynamic_slice_in_dim(held, (1 - mine) * half, half, axis)
         held = kept + swap(sent.astype(jnp.bfloat16), bit).astype(jnp.float32)
-        path.append((bit, axis))
-    held = held.astype(jnp.bfloat16)
-    for bit, axis in path[::-1]:
+        held = yield held
+    return held.astype(jnp.bfloat16)
+
+
+def double_tree(piece, shape, order):
+    held = piece
+    for bit, axis in tree_path(shape, order)[::-1]:
         other = swap(held, bit)
         held = jnp.where(
             own_bit(bit) == 0,
             jnp.concatenate([held, other], axis),
             jnp.concatenate([other, held], axis),
         )
+        held = yield held
     return held.astype(jnp.float32)
+
+
+def tree_path(shape, order):
+    rows, path = shape[0], []
+    for bit in order:
+        axis = 0 if rows % 16 == 0 else 1
+        rows = rows // 2 if axis == 0 else rows
+        path.append((bit, axis))
+    return path
+
+
+def core_gather(block, axis):
+    if lax.axis_size("fsdp") != 2:
+        return lax.all_gather(block, "fsdp", axis=axis, tiled=True)
+    other = lax.ppermute(block, "fsdp", [(0, 1), (1, 0)])
+    return jnp.where(
+        lax.axis_index("fsdp") == 0,
+        jnp.concatenate([block, other], axis),
+        jnp.concatenate([other, block], axis),
+    )
 
 
 def sum_tree(partial, order):
     held = partial
     for bit in order:
         held = held + swap(held, bit)
+        held = yield held
     count = lax.axis_size("fsdp")
     parts = held
     for shift in range(1, count):
@@ -323,6 +367,11 @@
             pltpu.VMEM((KV_HEADS, HEAD_DIM, columns), jnp.float32),
         ],
         compiler_params=pltpu.CompilerParams(vmem_limit_bytes=40 * 1024 * 1024),
+        cost_estimate=pl.CostEstimate(
+            flops=40 * all_keys.shape[0] * columns * HEAD_DIM,
+            bytes_accessed=16 * 1024 * all_keys.shape[0],
+            transcendentals=KV_HEADS * all_keys.shape[0] * columns,
+        ),
     )(first_place, places, queries, all_keys, all_values)
 
 
@@ -356,28 +405,29 @@
         ],
         scratch_shapes=[pltpu.VMEM((KV_HEADS, HEAD_DIM, columns), jnp.float32)],
         compiler_params=pltpu.CompilerParams(vmem_limit_bytes=40 * 1024 * 1024),
+        cost_estimate=pl.CostEstimate(
+            flops=40 * all_keys.shape[0] * columns * HEAD_DIM,
+            bytes_accessed=16 * 1024 * all_keys.shape[0],
+            transcendentals=KV_HEADS * all_keys.shape[0] * columns,
+        ),
     )(first_place, places, queries, grads, outs, logs, all_keys, all_values)
 
 
 def body(
     tokens, cotangent, norm_attn, w_query, w_key, w_value, w_out, norm_ffn, w_gate, w_up, w_down
 ):
-    gathered = (
-        lax.all_gather(norm_attn, "fsdp", axis=0, tiled=True),
-        lax.all_gather(w_query, "fsdp", axis=0, tiled=True),
-        lax.all_gather(w_key, "fsdp", axis=0, tiled=True),
-        lax.all_gather(w_value, "fsdp", axis=0, tiled=True),
-        lax.all_gather(w_out, "fsdp", axis=0, tiled=True),
-        lax.all_gather(norm_ffn, "fsdp", axis=0, tiled=True),
-        lax.all_gather(w_gate, "fsdp", axis=0, tiled=True),
-        lax.all_gather(w_up, "fsdp", axis=0, tiled=True),
-        lax.all_gather(w_down, "fsdp", axis=0, tiled=True),
-    )
-    gain_attn, query_w, key_w, value_w, out_w, gain_ffn, gate_w, up_w, down_w = gathered
+    model_width = tokens.shape[2]
+    kv_width = KV_HEADS * HEAD_DIM
+    gains = core_gather(jnp.stack([norm_attn, norm_ffn]), 1)
+    gain_attn, gain_ffn = gains[0], gains[1]
+    joined_w = core_gather(jnp.concatenate([w_query, w_key, w_value], 1), 0)
+    out_w = core_gather(w_out, 0)
+    gate_w = lax.all_gather(w_gate, "fsdp", axis=0, tiled=True)
+    up_w = lax.all_gather(w_up, "fsdp", axis=0, tiled=True)
+    down_w = lax.all_gather(w_down, "fsdp", axis=0, tiled=True)
     gain_attn = gain_attn.astype(jnp.float32)
     gain_ffn = gain_ffn.astype(jnp.float32)
     local_rows = tokens.shape[1]
-    model_width = tokens.shape[2]
     groups = KV_HEADS
     repeat = HEADS // KV_HEADS
     kv_width = KV_HEADS * HEAD_DIM
@@ -388,9 +438,10 @@
     attn_in, normed_one, factor_one = norm_forward(inputs, gain_attn)
     act_one = attn_in.astype(jnp.bfloat16)
     cosine_table, sine_table = rope_tables(first_pos, local_rows, HEAD_DIM)
-    query_pre = jnp.dot(act_one, query_w, preferred_element_type=jnp.float32)
-    key_pre = jnp.dot(act_one, key_w, preferred_element_type=jnp.float32)
-    value_pre = jnp.dot(act_one, value_w, preferred_element_type=jnp.float32)
+    joined_pre = jnp.dot(act_one, joined_w, preferred_element_type=jnp.float32)
+    query_pre = joined_pre[:, :model_width]
+    key_pre = joined_pre[:, model_width : model_width + kv_width]
+    value_pre = joined_pre[:, model_width + kv_width :]
     query_matrix = rotate(
         query_pre.reshape(local_rows, HEADS, HEAD_DIM), cosine_table, sine_table
     ).astype(jnp.bfloat16)
@@ -438,16 +489,27 @@
     grad_attn = grad_residual.astype(jnp.bfloat16)
     grad_out_w = transposed_times(out_act, grad_attn)
     first_order, second_order, third_order = reduce_orders(lax.axis_size("ctx"))
-    shard_gate = reduce_tree(core_half(grad_gate_w), first_order)
-    shard_up = reduce_tree(core_half(grad_up_w), second_order)
-    shard_down = reduce_tree(core_half(grad_down_w), third_order)
+    half_gate, half_up, half_down = (
+        core_half(grad_gate_w),
+        core_half(grad_up_w),
+        core_half(grad_down_w),
+    )
     grad_flat = times_transposed(grad_attn, out_w).astype(jnp.bfloat16)
+    half_gate, half_up, half_down, grad_flat = lax.optimization_barrier(
+        (half_gate, half_up, half_down, grad_flat)
+    )
     grad_queries, partial_keys, partial_values = attention_backward(
         first_place, places, scaled_queries, grad_flat, attended, log_totals, all_keys, all_values
     )
     grad_queries = grad_queries * score_scale
-    grad_keys = scatter_tree(partial_keys, key_order).reshape(local_rows, groups, HEAD_DIM)
-    grad_values = scatter_tree(middle_swapped(partial_values, value_order), value_order)
+    grad_keys, grad_values, piece_gate, piece_up, piece_down = lockstep(
+        scatter_tree(partial_keys, key_order),
+        scatter_tree(middle_swapped(partial_values, value_order), value_order),
+        halve_tree(half_gate, first_order),
+        halve_tree(half_up, second_order),
+        halve_tree(half_down, third_order),
+    )
+    grad_keys = grad_keys.reshape(local_rows, groups, HEAD_DIM)
     grad_query_pre = (
         unrotate(grad_queries.reshape(local_rows, HEADS, HEAD_DIM), cosine_table, sine_table)
         .reshape(local_rows, model_width)
@@ -462,24 +524,28 @@
     grad_query_w = transposed_times(act_one, grad_query_pre)
     grad_key_w = transposed_times(act_one, grad_key_pre)
     grad_value_w = transposed_times(act_one, grad_value_pre)
-    grad_act_one = (
-        times_transposed(grad_query_pre, query_w)
-        + times_transposed(grad_key_pre, key_w)
-        + times_transposed(grad_value_pre, value_w)
-    )
+    grad_joined_pre = jnp.concatenate([grad_query_pre, grad_key_pre, grad_value_pre], 1)
+    grad_act_one = times_transposed(grad_joined_pre, joined_w)
     back_one, grad_gain_attn = norm_backward(grad_act_one, gain_attn, normed_one, factor_one)
     grad_input = grad_residual + back_one
-    shard_one = reduce_tree(
-        core_half(jnp.concatenate([grad_out_w, grad_key_w], 1)), first_order
-    )
-    shard_two = reduce_tree(
-        core_half(jnp.concatenate([grad_query_w, grad_value_w], 1)), second_order
+    half_one = core_half(jnp.concatenate([grad_out_w, grad_key_w], 1))
+    half_two = core_half(jnp.concatenate([grad_query_w, grad_value_w], 1))
+    piece_one, piece_two, gains_sum, shard_gate, shard_up, shard_down = lockstep(
+        halve_tree(half_one, first_order),
+        halve_tree(half_two, second_order),
+        sum_tree(jnp.stack([grad_gain_attn, grad_gain_ffn]), first_order),
+        double_tree(piece_gate, half_gate.shape, first_order),
+        double_tree(piece_up, half_up.shape, second_order),
+        double_tree(piece_down, half_down.shape, third_order),
+    )
+    shard_one, shard_two = lockstep(
+        double_tree(piece_one, half_one.shape, first_order),
+        double_tree(piece_two, half_two.shape, second_order),
     )
     shard_out, shard_key = shard_one[:, :model_width], shard_one[:, model_width:]
     shard_query, shard_value = shard_two[:, :model_width], shard_two[:, model_width:]
-    gains = sum_tree(jnp.stack([grad_gain_attn, grad_gain_ffn]), first_order)
     shard_gains = lax.dynamic_slice_in_dim(
-        gains, lax.axis_index("fsdp") * norm_attn.shape[0], norm_attn.shape[0], 1
+        gains_sum, lax.axis_index("fsdp") * norm_attn.shape[0], norm_attn.shape[0], 1
     )
     return (
         result[None],

time: 271 us -> 280 us (1.033)
  waiting for transfers between devices: 72.7 us -> 111 us
  blocking collectives: 12.1 us -> 0 us
  local copies, waits for them, and re-layouts: 26.3 us -> 17.6 us
  starting transfers between devices: 83.2 us -> 75 us
  other arithmetic: 16.7 us -> 20.8 us
  matrix products: 23.5 us -> 20.6 us
    ppermute x60, waiting for transfers between devices: 70.3 us -> 109 us  [swap(): lax.ppermute(values, 'ctx', [(i, i ^ 1 << bit) for i in range(count)])]
    ppermute x60, starting transfers between devices: 82.3 us -> 72.6 us  [swap(): lax.ppermute(values, 'ctx', [(i, i ^ 1 << bit) for i in range(count)])]
    all_gather x4 -> x0, blocking collectives: 8.98 us -> none  [the longest x1 2.5 us: body(): lax.all_gather(w_query, 'fsdp', axis=0, tiled=True)]
    convert_element_type x3, local copies, waits for them, and re-layouts: 6.09 us -> 0.32 us  [core_half(): lax.dynamic_slice_in_dim(partial, other * rows, rows, 0)]
    add x15 -> x20, other arithmetic: 0.91 us -> 5.55 us  [halve_tree(): held = kept + swap(sent.astype(jnp.bfloat16), bit).astype(jnp.float32)]
    add x5, other arithmetic: 4.72 us -> 1.07 us  [core_half(): own = own + lax.ppermute(sent, 'fsdp', moves).astype(jnp.float32)]
    dot_general x7, matrix products: 7.87 us -> 4.31 us  [transposed_times(): lax.dot_general(left, right, (((0,), (0,)), ((), ())), preferred_element_...]
    add x7 -> x8, other arithmetic: 0.44 us -> 3.58 us  [scatter_tree(): held[:half]]
  transfers between devices with their start and end apart: 69 -> 72, of which waited for: 30 -> 44; matrix products, arithmetic and copies ran while one was open for 16% -> 14% of each run, Pallas kernels for 3% -> 3%
where the time goes in v3:
time: 280 us
  waiting for transfers between devices  111 us (40%)
  starting transfers between devices  75 us (27%)
  other arithmetic  20.8 us (7%)
  matrix products  20.6 us (7%)
  Pallas kernels  19.8 us (7%)
  local copies, waits for them, and re-layouts  17.6 us (6%)
  between operations  15.2 us (5%)
    ppermute x60, waiting for transfers between devices, swap(): lax.ppermute(values, 'ctx', [(i, i ^ 1 << bit) for i in range(count)])  109 us
    ppermute x60, starting transfers between devices, swap(): lax.ppermute(values, 'ctx', [(i, i ^ 1 << bit) for i in range(count)])  72.6 us
    pallas_call x1, Pallas kernels, attention_backward(): pl.pallas_call(backward_kernel, grid=(all_keys.shape[0] // keys,), in_spe...  10.6 us
    pallas_call x1, Pallas kernels, attention_forward(): pl.pallas_call(forward_kernel, grid=(all_keys.shape[0] // keys,), in_spec...  9.22 us
    dot_general x5, matrix products, times_transposed(): lax.dot_general(left, right, (((1,), (1,)), ((), ())), preferred_element_...  7.08 us
    unnamed x64, local copies, waits for them, and re-layouts  6.15 us
  transfers between devices with their start and end apart: 72, of which 44 were waited for; matrix products, arithmetic and copies ran while one was open for 14% of the time, Pallas kernels for 3%

profile of v3, /device:TPU:0, one launch (start us, length us, event | category | flops | bytes accessed | tf_op | source)
XLA Modules:
  0.0 279.7 jit_solution(2413510653623741577)
XLA Ops:
  14.8 3.9 %collective-permute-start.2 = (bf16[128,192]{1,0:T(8,128)(2,1)S(1)}, bf16[128,192]{1,0:T(8,128)(2,1)S(1)}, u32[]{:S(2)}, u32[]{:S(2)}) collective-permute-start(bf16[128,192]{1,0:T(8,128)(2,1)S(1)} %copy.50), channel_id=1, source_target_pairs={{0,16},{2,18},{4,20},{6,22},{8,24},{10,26},{12,28},{14,30},{16,0},... | collective-permute-start | bytes 147464 | tf_op jit(solution)/shard_map/ppermute | solution.py:95
  19.2 3.6 %collective-permute-done.2 = bf16[128,192]{1,0:T(8,128)(2,1)S(1)} collective-permute-done((bf16[128,192]{1,0:T(8,128)(2,1)S(1)}, bf16[128,192]{1,0:T(8,128)(2,1)S(1)}, u32[]{:S(2)}, u32[]{:S(2)}) %collective-permute-start.2) | collective-permute-done | bytes 49184 | tf_op jit(solution)/shard_map/ppermute | solution.py:95
  22.8 2.1 collective-permute-start.3
  26.8 4.5 %collective-permute-done.7 = bf16[256,192]{1,0:T(8,128)(2,1)S(1)} collective-permute-done((bf16[256,192]{1,0:T(8,128)(2,1)S(1)}, bf16[256,192]{1,0:T(8,128)(2,1)S(1)}, u32[]{:S(2)}, u32[]{:S(2)}) %collective-permute-start.7) | collective-permute-done | bytes 98336 | tf_op jit(solution)/shard_map/ppermute | solution.py:95
  31.3 1.6 collective-permute-start.8
  33.0 1.6 collective-permute-start.4
  34.5 4.5 %collective-permute-done.8 = bf16[512,192]{1,0:T(8,128)(2,1)S(1)} collective-permute-done((bf16[512,192]{1,0:T(8,128)(2,1)S(1)}, bf16[512,192]{1,0:T(8,128)(2,1)S(1)}, u32[]{:S(2)}, u32[]{:S(2)}) %collective-permute-start.8) | collective-permute-done | bytes 196640 | tf_op jit(solution)/shard_map/ppermute | solution.py:95
  40.6 1.5 collective-permute-start.5
  42.1 9.5 %collective-permute-done.9 = bf16[1024,192]{1,0:T(8,128)(2,1)S(1)} collective-permute-done((bf16[1024,192]{1,0:T(8,128)(2,1)S(1)}, bf16[1024,192]{1,0:T(8,128)(2,1)S(1)}, u32[]{:S(2)}, u32[]{:S(2)}) %collective-permute-start.9) | collective-permute-done | bytes 393248 | tf_op jit(solution)/shard_map/ppermute | solution.py:95
  52.6 9.2 %shard_map.194 = (f32[128,576]{1,0:T(8,128)S(1)}, f32[3,384]{1,0:T(4,128)S(1)}) custom-call(s32[1]{0:T(128)} %bitcast.1.first_ref, s32[2048,1]{1,0:T(8,128)S(1)} %copy.52.place_ref, bf16[128,576]{1,0:T(8,128)(2,1)S(1)} %copy.53.query_ref, bf16[2048,192]{1,0:T(8,128)(2,1)S(1)} %constant_dynamic-update-slice_fusion.key_ref, ...), custom_call_target="tpu_custom_call" | custom-call | flops 2013265920 | bytes 33554432 | tf_op jit(solution)/shard_map/pallas_call | solution.py:349
  61.8 1.9 multiply_reduce_fusion.2
  63.9 2.0 fusion.36
  65.9 2.9 %fusion.71 = f32[128,1536]{1,0:T(8,128)} fusion(bf16[128,576]{0,1:T(8,128)(2,1)S(1)} %multiply_convert_fusion.3, bf16[576,1536]{1,0:T(8,128)(2,1)} %all-gather.6.cloned.1.call-done), kind=kOutput, calls=%fused_computation.227 | convolution fusion | flops 226492416 | bytes 2703360 | tf_op jit(solution)/shard_map/dot_general | solution.py:471
  68.8 2.5 multiply_convert_fusion
  76.5 1.8 convolution_convert_fusion.grad_ref
  78.3 1.5 fusion.38
  80.7 1.7 copy-done.1
  83.5 10.6 %shard_map.195 = (f32[128,576]{1,0:T(8,128)S(1)}, bf16[2048,192]{1,0:T(8,128)(2,1)S(1)}, bf16[2048,192]{1,0:T(8,128)(2,1)S(1)}) custom-call(s32[1]{0:T(128)} %bitcast.1.first_ref, s32[2048,1]{1,0:T(8,128)S(1)} %copy.52.place_ref, bf16[128,576]{1,0:T(8,128)(2,1)S(1)} %copy.53.query_ref, bf16[128,576]{1,0:T(8,128)(2,1)S(1)} %convolution_convert_fusion.grad_ref, ...), custom_call_target="tpu_custom_call" | custom-call | flops 2013265920 | bytes 33554432 | tf_op jit(solution)/shard_map/pallas_call | solution.py:383
  103.3 1.6 collective-permute-start.18
  105.6 7.6 %collective-permute-done.15 = bf16[1024,192]{1,0:T(8,128)(2,1)} collective-permute-done((bf16[1024,192]{1,0:T(8,128)(2,1)}, bf16[1024,192]{1,0:T(8,128)(2,1)}, u32[]{:S(2)}, u32[]{:S(2)}) %collective-permute-start.15) | collective-permute-done | bytes 393248 | tf_op jit(solution)/shard_map/ppermute | solution.py:95
  113.2 1.4 convert_add_fusion.3
  116.0 2.7 collective-permute-done.16
  119.7 1.7 collective-permute-done.17
  126.7 1.4 collective-permute-start.22
  128.2 4.1 %collective-permute-start.23 = (bf16[192,576]{0,1:T(8,128)(2,1)S(1)}, bf16[192,576]{0,1:T(8,128)(2,1)S(1)}, u32[]{:S(2)}, u32[]{:S(2)}) collective-permute-start(bf16[192,576]{0,1:T(8,128)(2,1)S(1)} %dynamic-slice_convert_fusion.6), channel_id=1, source_target_pairs={{0,16},{2,18},{4,20},{6,22},{8,24},{10,26},{12,28},{14,30},{16,0},... | collective-permute-start | bytes 663560 | tf_op jit(solution)/shard_map/ppermute | solution.py:95
  133.6 2.0 collective-permute-done.21
  135.9 7.7 %collective-permute-done.23 = bf16[192,576]{0,1:T(8,128)(2,1)S(1)} collective-permute-done((bf16[192,576]{0,1:T(8,128)(2,1)S(1)}, bf16[192,576]{0,1:T(8,128)(2,1)S(1)}, u32[]{:S(2)}, u32[]{:S(2)}) %collective-permute-start.23) | collective-permute-done | bytes 221216 | tf_op jit(solution)/shard_map/ppermute | solution.py:95
  144.3 1.7 collective-permute-start.25
  146.5 1.7 collective-permute-start.27
  148.9 1.4 collective-permute-done.24
  150.4 2.8 collective-permute-done.25
  153.2 1.9 collective-permute-done.26
  156.5 2.3 collective-permute-start.29
  159.6 2.3 collective-permute-start.31
  165.0 2.6 collective-permute-done.30
  167.7 1.7 collective-permute-done.31
  172.5 1.9 fusion.23
  175.7 2.9 %collective-permute-start.40 = (bf16[72,384]{1,0:T(8,128)(2,1)S(1)}, bf16[72,384]{1,0:T(8,128)(2,1)S(1)}, u32[]{:S(2)}, u32[]{:S(2)}) collective-permute-start(bf16[72,384]{1,0:T(8,128)(2,1)S(1)} %copy-done.24), channel_id=1, source_target_pairs={{0,16},{2,18},{4,20},{6,22},{8,24},{10,26},{12,28},{14,30},{16,0},... | collective-permute-start | bytes 165896 | tf_op jit(solution)/shard_map/ppermute | solution.py:95
  179.8 4.3 %collective-permute-done.41 = bf16[48,576]{0,1:T(8,128)(2,1)S(1)} collective-permute-done((bf16[48,576]{0,1:T(8,128)(2,1)S(1)}, bf16[48,576]{0,1:T(8,128)(2,1)S(1)}, u32[]{:S(2)}, u32[]{:S(2)}) %collective-permute-start.41) | collective-permute-done | bytes 55328 | tf_op jit(solution)/shard_map/ppermute | solution.py:95
  184.6 1.6 collective-permute-start.35
  187.0 4.9 %collective-permute-done.35 = bf16[144,768]{1,0:T(8,128)(2,1)S(1)} collective-permute-done((bf16[144,768]{1,0:T(8,128)(2,1)S(1)}, bf16[144,768]{1,0:T(8,128)(2,1)S(1)}, u32[]{:S(2)}, u32[]{:S(2)}) %collective-permute-start.35) | collective-permute-done | bytes 221216 | tf_op jit(solution)/shard_map/ppermute | solution.py:95
  191.9 1.4 collective-permute-done.37
  194.0 1.5 collective-permute-start.44
  196.2 2.0 collective-permute-start.46
  198.3 1.4 collective-permute-start.47
  199.7 1.4 collective-permute-done.43
  203.8 2.0 collective-permute-start.50
  210.5 1.4 collective-permute-done.51
  213.0 7.4 %collective-permute-done.53 = bf16[192,576]{0,1:T(8,128)(2,1)S(1)} collective-permute-done((bf16[192,576]{0,1:T(8,128)(2,1)S(1)}, bf16[192,576]{0,1:T(8,128)(2,1)S(1)}, u32[]{:S(2)}, u32[]{:S(2)}) %collective-permute-start.53) | collective-permute-done | bytes 221216 | tf_op jit(solution)/shard_map/ppermute | solution.py:95
  221.0 2.9 %collective-permute-start.56 = (f32[2,576]{1,0:T(2,128)S(1)}, f32[2,576]{1,0:T(2,128)S(1)}, u32[]{:S(2)}, u32[]{:S(2)}) collective-permute-start(f32[2,576]{1,0:T(2,128)S(1)} %add.409), channel_id=1, source_target_pairs={{0,16},{2,18},{4,20},{6,22},{8,24},{10,26},{12,28},{14,30},{16,0},... | collective-permute-start | bytes 13832 | tf_op jit(solution)/shard_map/ppermute | solution.py:95
  224.1 1.9 collective-permute-start.57
  226.2 1.7 collective-permute-start.59
  229.1 4.9 %collective-permute-done.57 = bf16[144,1536]{1,0:T(8,128)(2,1)S(1)} collective-permute-done((bf16[144,1536]{1,0:T(8,128)(2,1)S(1)}, bf16[144,1536]{1,0:T(8,128)(2,1)S(1)}, u32[]{:S(2)}, u32[]{:S(2)}) %collective-permute-start.57) | collective-permute-done | bytes 442400 | tf_op jit(solution)/shard_map/ppermute | solution.py:95
  236.1 2.6 collective-permute-start.61
  241.1 3.9 %collective-permute-done.62 = bf16[72,192]{1,0:T(8,128)(2,1)S(1)} collective-permute-done((bf16[72,192]{1,0:T(8,128)(2,1)S(1)}, bf16[72,192]{1,0:T(8,128)(2,1)S(1)}, u32[]{:S(2)}, u32[]{:S(2)}) %collective-permute-start.62) | collective-permute-done | bytes 27680 | tf_op jit(solution)/shard_map/ppermute | solution.py:95
  245.4 1.8 collective-permute-start.64
  247.2 2.1 collective-permute-done.63
  250.0 1.8 collective-permute-start.65
  252.6 1.4 convert_element_type.397
  254.0 1.4 convert_element_type.398
  255.5 1.3 convert_element_type.399
  257.2 5.1 %collective-permute-done.66 = bf16[72,768]{1,0:T(8,128)(2,1)S(1)} collective-permute-done((bf16[72,768]{1,0:T(8,128)(2,1)S(1)}, bf16[72,768]{1,0:T(8,128)(2,1)S(1)}, u32[]{:S(2)}, u32[]{:S(2)}) %collective-permute-start.66) | collective-permute-done | bytes 110624 | tf_op jit(solution)/shard_map/ppermute | solution.py:95
  262.8 1.8 collective-permute-start.68
  265.1 4.3 %collective-permute-done.67 = bf16[144,768]{1,0:T(8,128)(2,1)S(1)} collective-permute-done((bf16[144,768]{1,0:T(8,128)(2,1)S(1)}, bf16[144,768]{1,0:T(8,128)(2,1)S(1)}, u32[]{:S(2)}, u32[]{:S(2)}) %collective-permute-start.67) | collective-permute-done | bytes 221216 | tf_op jit(solution)/shard_map/ppermute | solution.py:95
  (315 shorter events, 75.9 us)
Async XLA Ops:
  7.2 56.6 %all-gather.8.cloned.1.call-start = ((), (), s32[]{:S(2)}) async-start(), calls=%async_computation.2 | async-start | bytes 2654208 | tf_op jit(solution)/shard_map/all_gather | solution.py:427
  8.0 57.9 %all-gather.6.cloned.1.call-start = ((), (), s32[]{:S(2)}) async-start(), calls=%async_computation.1 | async-start | bytes 2654208 | tf_op jit(solution)/shard_map/all_gather | solution.py:426
  8.7 60.0 %all-gather.4.cloned.1.call-start = ((), (), s32[]{:S(2)}) async-start(), calls=%async_computation | async-start | bytes 2654208 | tf_op jit(solution)/shard_map/all_gather | solution.py:425
  8.8 53.0 %collective-permute-start.10 = (bf16[288,576]{1,0:T(8,128)(2,1)}, bf16[288,576]{1,0:T(8,128)(2,1)}, u32[]{:S(2)}, u32[]{:S(2)}) collective-permute-start(bf16[288,576]{1,0:T(8,128)(2,1)} %param.17), channel_id=1, source_target_pairs={{0,1},{1,0},{2,3},{3,2},{4,5},{5,4},{6,7},{7,6},{8,9},{9,8},{10,11... | collective-permute-start | bytes 995336 | tf_op jit(solution)/shard_map/ppermute | solution.py:205
  14.8 7.9 %collective-permute-start.2 = (bf16[128,192]{1,0:T(8,128)(2,1)S(1)}, bf16[128,192]{1,0:T(8,128)(2,1)S(1)}, u32[]{:S(2)}, u32[]{:S(2)}) collective-permute-start(bf16[128,192]{1,0:T(8,128)(2,1)S(1)} %copy.50), channel_id=1, source_target_pairs={{0,16},{2,18},{4,20},{6,22},{8,24},{10,26},{12,28},{14,30},{16,0},... | collective-permute-start | bytes 147464 | tf_op jit(solution)/shard_map/ppermute | solution.py:95
  18.8 6.6 %collective-permute-start.6 = (bf16[128,192]{1,0:T(8,128)(2,1)S(1)}, bf16[128,192]{1,0:T(8,128)(2,1)S(1)}, u32[]{:S(2)}, u32[]{:S(2)}) collective-permute-start(bf16[128,192]{1,0:T(8,128)(2,1)S(1)} %copy.65), channel_id=1, source_target_pairs={{0,16},{2,18},{4,20},{6,22},{8,24},{10,26},{12,28},{14,30},{16,0},... | collective-permute-start | bytes 147464 | tf_op jit(solution)/shard_map/ppermute | solution.py:95
  22.8 10.1 %collective-permute-start.3 = (bf16[256,192]{1,0:T(8,128)(2,1)S(1)}, bf16[256,192]{1,0:T(8,128)(2,1)S(1)}, u32[]{:S(2)}, u32[]{:S(2)}) collective-permute-start(bf16[256,192]{1,0:T(8,128)(2,1)S(1)} %pad_maximum_fusion.6), channel_id=1, source_target_pairs={{0,8},{2,10},{4,12},{6,14},{8,0},{10,2},{12,4},{14,6},{16,24},{18,... | collective-permute-start | bytes 294920 | tf_op jit(solution)/shard_map/ppermute | solution.py:95
  25.5 5.8 %collective-permute-start.7 = (bf16[256,192]{1,0:T(8,128)(2,1)S(1)}, bf16[256,192]{1,0:T(8,128)(2,1)S(1)}, u32[]{:S(2)}, u32[]{:S(2)}) collective-permute-start(bf16[256,192]{1,0:T(8,128)(2,1)S(1)} %pad_maximum_fusion.7), channel_id=1, source_target_pairs={{0,8},{2,10},{4,12},{6,14},{8,0},{10,2},{12,4},{14,6},{16,24},{18,... | collective-permute-start | bytes 294920 | tf_op jit(solution)/shard_map/ppermute | solution.py:95
  31.3 7.7 %collective-permute-start.8 = (bf16[512,192]{1,0:T(8,128)(2,1)S(1)}, bf16[512,192]{1,0:T(8,128)(2,1)S(1)}, u32[]{:S(2)}, u32[]{:S(2)}) collective-permute-start(bf16[512,192]{1,0:T(8,128)(2,1)S(1)} %pad_maximum_fusion.5), channel_id=1, source_target_pairs={{0,2},{2,0},{4,6},{6,4},{8,10},{10,8},{12,14},{14,12},{16,18},{18,... | collective-permute-start | bytes 589832 | tf_op jit(solution)/shard_map/ppermute | solution.py:95
  33.0 7.6 %collective-permute-start.4 = (bf16[512,192]{1,0:T(8,128)(2,1)S(1)}, bf16[512,192]{1,0:T(8,128)(2,1)S(1)}, u32[]{:S(2)}, u32[]{:S(2)}) collective-permute-start(bf16[512,192]{1,0:T(8,128)(2,1)S(1)} %pad_maximum_fusion.4), channel_id=1, source_target_pairs={{0,4},{2,6},{4,0},{6,2},{8,12},{10,14},{12,8},{14,10},{16,20},{18,... | collective-permute-start | bytes 589832 | tf_op jit(solution)/shard_map/ppermute | solution.py:95
  39.2 12.4 %collective-permute-start.9 = (bf16[1024,192]{1,0:T(8,128)(2,1)S(1)}, bf16[1024,192]{1,0:T(8,128)(2,1)S(1)}, u32[]{:S(2)}, u32[]{:S(2)}) collective-permute-start(bf16[1024,192]{1,0:T(8,128)(2,1)S(1)} %pad_maximum_fusion.2), channel_id=1, source_target_pairs={{0,4},{2,6},{4,0},{6,2},{8,12},{10,14},{12,8},{14,10},{16,20},{18,... | collective-permute-start | bytes 1179656 | tf_op jit(solution)/shard_map/ppermute | solution.py:95
  40.6 11.9 %collective-permute-start.5 = (bf16[1024,192]{1,0:T(8,128)(2,1)S(1)}, bf16[1024,192]{1,0:T(8,128)(2,1)S(1)}, u32[]{:S(2)}, u32[]{:S(2)}) collective-permute-start(bf16[1024,192]{1,0:T(8,128)(2,1)S(1)} %pad_maximum_fusion.1), channel_id=1, source_target_pairs={{0,2},{2,0},{4,6},{6,4},{8,10},{10,8},{12,14},{14,12},{16,18},{18,... | collective-permute-start | bytes 1179656 | tf_op jit(solution)/shard_map/ppermute | solution.py:95
  72.0 7.8 %collective-permute-start.11 = (bf16[288,1536]{1,0:T(8,128)(2,1)S(1)}, bf16[288,1536]{1,0:T(8,128)(2,1)S(1)}, u32[]{:S(2)}, u32[]{:S(2)}) collective-permute-start(bf16[288,1536]{1,0:T(8,128)(2,1)S(1)} %dynamic-slice_convert_fusion.2), channel_id=1, source_target_pairs={{0,1},{1,0},{2,3},{3,2},{4,5},{5,4},{6,7},{7,6},{8,9},{9,8},{10,11... | collective-permute-start | bytes 2654216 | tf_op jit(solution)/shard_map/ppermute | solution.py:164
  72.8 7.3 %collective-permute-start.12 = (bf16[288,1536]{1,0:T(8,128)(2,1)S(1)}, bf16[288,1536]{1,0:T(8,128)(2,1)S(1)}, u32[]{:S(2)}, u32[]{:S(2)}) collective-permute-start(bf16[288,1536]{1,0:T(8,128)(2,1)S(1)} %dynamic-slice_convert_fusion.1), channel_id=1, source_target_pairs={{0,1},{1,0},{2,3},{3,2},{4,5},{5,4},{6,7},{7,6},{8,9},{9,8},{10,11... | collective-permute-start | bytes 2654216 | tf_op jit(solution)/shard_map/ppermute | solution.py:164
  74.1 6.3 %collective-permute-start.13 = (bf16[768,576]{0,1:T(8,128)(2,1)S(1)}, bf16[768,576]{0,1:T(8,128)(2,1)S(1)}, u32[]{:S(2)}, u32[]{:S(2)}) collective-permute-start(bf16[768,576]{0,1:T(8,128)(2,1)S(1)} %dynamic-slice_convert_fusion), channel_id=1, source_target_pairs={{0,1},{1,0},{2,3},{3,2},{4,5},{5,4},{6,7},{7,6},{8,9},{9,8},{10,11... | collective-permute-start | bytes 2654216 | tf_op jit(solution)/shard_map/ppermute | solution.py:164
  95.0 19.7 %collective-permute-start.14 = (bf16[1024,192]{1,0:T(8,128)(2,1)}, bf16[1024,192]{1,0:T(8,128)(2,1)}, u32[]{:S(2)}, u32[]{:S(2)}) collective-permute-start(bf16[1024,192]{1,0:T(8,128)(2,1)} %slice.151), channel_id=1, source_target_pairs={{0,2},{2,0},{4,6},{6,4},{8,10},{10,8},{12,14},{14,12},{16,18},{18,... | collective-permute-start | bytes 1179656 | tf_op jit(solution)/shard_map/ppermute | solution.py:95
  98.0 15.1 %collective-permute-start.15 = (bf16[1024,192]{1,0:T(8,128)(2,1)}, bf16[1024,192]{1,0:T(8,128)(2,1)}, u32[]{:S(2)}, u32[]{:S(2)}) collective-permute-start(bf16[1024,192]{1,0:T(8,128)(2,1)} %pad_maximum_fusion.3), channel_id=1, source_target_pairs={{0,4},{2,6},{4,0},{6,2},{8,12},{10,14},{12,8},{14,10},{16,20},{18,... | collective-permute-start | bytes 1179656 | tf_op jit(solution)/shard_map/ppermute | solution.py:95
  99.4 19.3 %collective-permute-start.16 = (bf16[144,1536]{1,0:T(8,128)(2,1)}, bf16[144,1536]{1,0:T(8,128)(2,1)}, u32[]{:S(2)}, u32[]{:S(2)}) collective-permute-start(bf16[144,1536]{1,0:T(8,128)(2,1)} %dynamic-slice_convert_fusion.5), channel_id=1, source_target_pairs={{0,2},{2,0},{4,6},{6,4},{8,10},{10,8},{12,14},{14,12},{16,18},{18,... | collective-permute-start | bytes 1327112 | tf_op jit(solution)/shard_map/ppermute | solution.py:95
  101.4 20.0 %collective-permute-start.17 = (bf16[144,1536]{1,0:T(8,128)(2,1)}, bf16[144,1536]{1,0:T(8,128)(2,1)}, u32[]{:S(2)}, u32[]{:S(2)}) collective-permute-start(bf16[144,1536]{1,0:T(8,128)(2,1)} %dynamic-slice_convert_fusion.4), channel_id=1, source_target_pairs={{0,4},{2,6},{4,0},{6,2},{8,12},{10,14},{12,8},{14,10},{16,20},{18,... | collective-permute-start | bytes 1327112 | tf_op jit(solution)/shard_map/ppermute | solution.py:95
  103.3 19.2 %collective-permute-start.18 = (bf16[384,576]{0,1:T(8,128)(2,1)}, bf16[384,576]{0,1:T(8,128)(2,1)}, u32[]{:S(2)}, u32[]{:S(2)}) collective-permute-start(bf16[384,576]{0,1:T(8,128)(2,1)} %dynamic-slice_convert_fusion.3), channel_id=1, source_target_pairs={{0,8},{2,10},{4,12},{6,14},{8,0},{10,2},{12,4},{14,6},{16,24},{18,... | collective-permute-start | bytes 1327112 | tf_op jit(solution)/shard_map/ppermute | solution.py:95
  123.7 9.3 %collective-permute-start.19 = (bf16[512,192]{1,0:T(8,128)(2,1)S(1)}, bf16[512,192]{1,0:T(8,128)(2,1)S(1)}, u32[]{:S(2)}, u32[]{:S(2)}) collective-permute-start(bf16[512,192]{1,0:T(8,128)(2,1)S(1)} %slice.247), channel_id=1, source_target_pairs={{0,4},{2,6},{4,0},{6,2},{8,12},{10,14},{12,8},{14,10},{16,20},{18,... | collective-permute-start | bytes 589832 | tf_op jit(solution)/shard_map/ppermute | solution.py:95
  124.3 9.2 %collective-permute-start.20 = (bf16[512,192]{1,0:T(8,128)(2,1)S(1)}, bf16[512,192]{1,0:T(8,128)(2,1)S(1)}, u32[]{:S(2)}, u32[]{:S(2)}) collective-permute-start(bf16[512,192]{1,0:T(8,128)(2,1)S(1)} %slice.246), channel_id=1, source_target_pairs={{0,2},{2,0},{4,6},{6,4},{8,10},{10,8},{12,14},{14,12},{16,18},{18,... | collective-permute-start | bytes 589832 | tf_op jit(solution)/shard_map/ppermute | solution.py:95
  125.6 10.0 %collective-permute-start.21 = (bf16[72,1536]{1,0:T(8,128)(2,1)S(1)}, bf16[72,1536]{1,0:T(8,128)(2,1)S(1)}, u32[]{:S(2)}, u32[]{:S(2)}) collective-permute-start(bf16[72,1536]{1,0:T(8,128)(2,1)S(1)} %dynamic-slice_convert_fusion.10), channel_id=1, source_target_pairs={{0,4},{2,6},{4,0},{6,2},{8,12},{10,14},{12,8},{14,10},{16,20},{18,... | collective-permute-start | bytes 663560 | tf_op jit(solution)/shard_map/ppermute | solution.py:95
  126.7 9.2 %collective-permute-start.22 = (bf16[72,1536]{1,0:T(8,128)(2,1)S(1)}, bf16[72,1536]{1,0:T(8,128)(2,1)S(1)}, u32[]{:S(2)}, u32[]{:S(2)}) collective-permute-start(bf16[72,1536]{1,0:T(8,128)(2,1)S(1)} %dynamic-slice_convert_fusion.9), channel_id=1, source_target_pairs={{0,2},{2,0},{4,6},{6,4},{8,10},{10,8},{12,14},{14,12},{16,18},{18,... | collective-permute-start | bytes 663560 | tf_op jit(solution)/shard_map/ppermute | solution.py:95
  128.2 15.4 %collective-permute-start.23 = (bf16[192,576]{0,1:T(8,128)(2,1)S(1)}, bf16[192,576]{0,1:T(8,128)(2,1)S(1)}, u32[]{:S(2)}, u32[]{:S(2)}) collective-permute-start(bf16[192,576]{0,1:T(8,128)(2,1)S(1)} %dynamic-slice_convert_fusion.6), channel_id=1, source_target_pairs={{0,16},{2,18},{4,20},{6,22},{8,24},{10,26},{12,28},{14,30},{16,0},... | collective-permute-start | bytes 663560 | tf_op jit(solution)/shard_map/ppermute | solution.py:95
  143.8 6.5 %collective-permute-start.24 = (bf16[256,192]{1,0:T(8,128)(2,1)S(1)}, bf16[256,192]{1,0:T(8,128)(2,1)S(1)}, u32[]{:S(2)}, u32[]{:S(2)}) collective-permute-start(bf16[256,192]{1,0:T(8,128)(2,1)S(1)} %slice.249), channel_id=1, source_target_pairs={{0,8},{2,10},{4,12},{6,14},{8,0},{10,2},{12,4},{14,6},{16,24},{18,... | collective-permute-start | bytes 294920 | tf_op jit(solution)/shard_map/ppermute | solution.py:95
  144.3 8.8 %collective-permute-start.25 = (bf16[256,192]{1,0:T(8,128)(2,1)S(1)}, bf16[256,192]{1,0:T(8,128)(2,1)S(1)}, u32[]{:S(2)}, u32[]{:S(2)}) collective-permute-start(bf16[256,192]{1,0:T(8,128)(2,1)S(1)} %slice.248), channel_id=1, source_target_pairs={{0,8},{2,10},{4,12},{6,14},{8,0},{10,2},{12,4},{14,6},{16,24},{18,... | collective-permute-start | bytes 294920 | tf_op jit(solution)/shard_map/ppermute | solution.py:95
  146.0 9.0 %collective-permute-start.26 = (bf16[72,768]{1,0:T(8,128)(2,1)S(1)}, bf16[72,768]{1,0:T(8,128)(2,1)S(1)}, u32[]{:S(2)}, u32[]{:S(2)}) collective-permute-start(bf16[72,768]{1,0:T(8,128)(2,1)S(1)} %dynamic-slice_convert_fusion.16), channel_id=1, source_target_pairs={{0,8},{2,10},{4,12},{6,14},{8,0},{10,2},{12,4},{14,6},{16,24},{18,... | collective-permute-start | bytes 331784 | tf_op jit(solution)/shard_map/ppermute | solution.py:95
  146.5 9.8 %collective-permute-start.27 = (bf16[72,768]{1,0:T(8,128)(2,1)S(1)}, bf16[72,768]{1,0:T(8,128)(2,1)S(1)}, u32[]{:S(2)}, u32[]{:S(2)}) collective-permute-start(bf16[72,768]{1,0:T(8,128)(2,1)S(1)} %dynamic-slice_convert_fusion.15), channel_id=1, source_target_pairs={{0,8},{2,10},{4,12},{6,14},{8,0},{10,2},{12,4},{14,6},{16,24},{18,... | collective-permute-start | bytes 331784 | tf_op jit(solution)/shard_map/ppermute | solution.py:95
  148.3 8.0 %collective-permute-start.28 = (bf16[96,576]{0,1:T(8,128)(2,1)S(1)}, bf16[96,576]{0,1:T(8,128)(2,1)S(1)}, u32[]{:S(2)}, u32[]{:S(2)}) collective-permute-start(bf16[96,576]{0,1:T(8,128)(2,1)S(1)} %dynamic-slice_convert_fusion.12), channel_id=1, source_target_pairs={{0,2},{2,0},{4,6},{6,4},{8,10},{10,8},{12,14},{14,12},{16,18},{18,... | collective-permute-start | bytes 331784 | tf_op jit(solution)/shard_map/ppermute | solution.py:95
  156.5 7.9 %collective-permute-start.29 = (bf16[128,192]{1,0:T(8,128)(2,1)S(1)}, bf16[128,192]{1,0:T(8,128)(2,1)S(1)}, u32[]{:S(2)}, u32[]{:S(2)}) collective-permute-start(bf16[128,192]{1,0:T(8,128)(2,1)S(1)} %slice.251), channel_id=1, source_target_pairs={{0,16},{2,18},{4,20},{6,22},{8,24},{10,26},{12,28},{14,30},{16,0},... | collective-permute-start | bytes 147464 | tf_op jit(solution)/shard_map/ppermute | solution.py:95
  158.8 8.9 %collective-permute-start.30 = (bf16[128,192]{1,0:T(8,128)(2,1)S(1)}, bf16[128,192]{1,0:T(8,128)(2,1)S(1)}, u32[]{:S(2)}, u32[]{:S(2)}) collective-permute-start(bf16[128,192]{1,0:T(8,128)(2,1)S(1)} %slice.250), channel_id=1, source_target_pairs={{0,16},{2,18},{4,20},{6,22},{8,24},{10,26},{12,28},{14,30},{16,0},... | collective-permute-start | bytes 147464 | tf_op jit(solution)/shard_map/ppermute | solution.py:95
  159.6 9.8 %collective-permute-start.31 = (bf16[72,384]{1,0:T(8,128)(2,1)S(1)}, bf16[72,384]{1,0:T(8,128)(2,1)S(1)}, u32[]{:S(2)}, u32[]{:S(2)}) collective-permute-start(bf16[72,384]{1,0:T(8,128)(2,1)S(1)} %dynamic-slice_convert_fusion.20), channel_id=1, source_target_pairs={{0,16},{2,18},{4,20},{6,22},{8,24},{10,26},{12,28},{14,30},{16,0},... | collective-permute-start | bytes 165896 | tf_op jit(solution)/shard_map/ppermute | solution.py:95
  161.9 8.1 %collective-permute-start.32 = (bf16[72,384]{1,0:T(8,128)(2,1)S(1)}, bf16[72,384]{1,0:T(8,128)(2,1)S(1)}, u32[]{:S(2)}, u32[]{:S(2)}) collective-permute-start(bf16[72,384]{1,0:T(8,128)(2,1)S(1)} %dynamic-slice_convert_fusion.19), channel_id=1, source_target_pairs={{0,16},{2,18},{4,20},{6,22},{8,24},{10,26},{12,28},{14,30},{16,0},... | collective-permute-start | bytes 165896 | tf_op jit(solution)/shard_map/ppermute | solution.py:95
  162.7 7.9 %collective-permute-start.33 = (bf16[48,576]{0,1:T(8,128)(2,1)S(1)}, bf16[48,576]{0,1:T(8,128)(2,1)S(1)}, u32[]{:S(2)}, u32[]{:S(2)}) collective-permute-start(bf16[48,576]{0,1:T(8,128)(2,1)S(1)} %dynamic-slice_convert_fusion.11), channel_id=1, source_target_pairs={{0,4},{2,6},{4,0},{6,2},{8,12},{10,14},{12,8},{14,10},{16,20},{18,... | collective-permute-start | bytes 165896 | tf_op jit(solution)/shard_map/ppermute | solution.py:95
  174.6 9.8 %collective-permute-start.34 = (bf16[288,768]{1,0:T(8,128)(2,1)S(1)}, bf16[288,768]{1,0:T(8,128)(2,1)S(1)}, u32[]{:S(2)}, u32[]{:S(2)}) collective-permute-start(bf16[288,768]{1,0:T(8,128)(2,1)S(1)} %fusion.7), channel_id=1, source_target_pairs={{0,1},{1,0},{2,3},{3,2},{4,5},{5,4},{6,7},{7,6},{8,9},{9,8},{10,11... | collective-permute-start | bytes 1327112 | tf_op jit(solution)/shard_map/ppermute | solution.py:164
  175.5 10.8 %collective-permute-start.36 = (bf16[288,768]{1,0:T(8,128)(2,1)S(1)}, bf16[288,768]{1,0:T(8,128)(2,1)S(1)}, u32[]{:S(2)}, u32[]{:S(2)}) collective-permute-start(bf16[288,768]{1,0:T(8,128)(2,1)S(1)} %fusion.3), channel_id=1, source_target_pairs={{0,1},{1,0},{2,3},{3,2},{4,5},{5,4},{6,7},{7,6},{8,9},{9,8},{10,11... | collective-permute-start | bytes 1327112 | tf_op jit(solution)/shard_map/ppermute | solution.py:164
  175.7 8.6 %collective-permute-start.39 = (bf16[72,384]{1,0:T(8,128)(2,1)S(1)}, bf16[72,384]{1,0:T(8,128)(2,1)S(1)}, u32[]{:S(2)}, u32[]{:S(2)}) collective-permute-start(bf16[72,384]{1,0:T(8,128)(2,1)S(1)} %copy-done.23), channel_id=1, source_target_pairs={{0,16},{2,18},{4,20},{6,22},{8,24},{10,26},{12,28},{14,30},{16,0},... | collective-permute-start | bytes 165896 | tf_op jit(solution)/shard_map/ppermute | solution.py:95
  175.7 8.6 %collective-permute-start.40 = (bf16[72,384]{1,0:T(8,128)(2,1)S(1)}, bf16[72,384]{1,0:T(8,128)(2,1)S(1)}, u32[]{:S(2)}, u32[]{:S(2)}) collective-permute-start(bf16[72,384]{1,0:T(8,128)(2,1)S(1)} %copy-done.24), channel_id=1, source_target_pairs={{0,16},{2,18},{4,20},{6,22},{8,24},{10,26},{12,28},{14,30},{16,0},... | collective-permute-start | bytes 165896 | tf_op jit(solution)/shard_map/ppermute | solution.py:95
  178.7 5.5 %collective-permute-start.41 = (bf16[48,576]{0,1:T(8,128)(2,1)S(1)}, bf16[48,576]{0,1:T(8,128)(2,1)S(1)}, u32[]{:S(2)}, u32[]{:S(2)}) collective-permute-start(bf16[48,576]{0,1:T(8,128)(2,1)S(1)} %convert_add_fusion.15), channel_id=1, source_target_pairs={{0,4},{2,6},{4,0},{6,2},{8,12},{10,14},{12,8},{14,10},{16,20},{18,... | collective-permute-start | bytes 165896 | tf_op jit(solution)/shard_map/ppermute | solution.py:95
  184.6 7.2 %collective-permute-start.35 = (bf16[144,768]{1,0:T(8,128)(2,1)S(1)}, bf16[144,768]{1,0:T(8,128)(2,1)S(1)}, u32[]{:S(2)}, u32[]{:S(2)}) collective-permute-start(bf16[144,768]{1,0:T(8,128)(2,1)S(1)} %dynamic-slice_convert_fusion.8), channel_id=1, source_target_pairs={{0,2},{2,0},{4,6},{6,4},{8,10},{10,8},{12,14},{14,12},{16,18},{18,... | collective-permute-start | bytes 663560 | tf_op jit(solution)/shard_map/ppermute | solution.py:95
  186.4 6.9 %collective-permute-start.37 = (bf16[144,768]{1,0:T(8,128)(2,1)S(1)}, bf16[144,768]{1,0:T(8,128)(2,1)S(1)}, u32[]{:S(2)}, u32[]{:S(2)}) collective-permute-start(bf16[144,768]{1,0:T(8,128)(2,1)S(1)} %dynamic-slice_convert_fusion.7), channel_id=1, source_target_pairs={{0,4},{2,6},{4,0},{6,2},{8,12},{10,14},{12,8},{14,10},{16,20},{18,... | collective-permute-start | bytes 663560 | tf_op jit(solution)/shard_map/ppermute | solution.py:95
  193.4 6.2 %collective-permute-start.42 = (bf16[72,768]{1,0:T(8,128)(2,1)S(1)}, bf16[72,768]{1,0:T(8,128)(2,1)S(1)}, u32[]{:S(2)}, u32[]{:S(2)}) collective-permute-start(bf16[72,768]{1,0:T(8,128)(2,1)S(1)} %dynamic-slice_convert_fusion.14), channel_id=1, source_target_pairs={{0,4},{2,6},{4,0},{6,2},{8,12},{10,14},{12,8},{14,10},{16,20},{18,... | collective-permute-start | bytes 331784 | tf_op jit(solution)/shard_map/ppermute | solution.py:95
  195.5 5.6 %collective-permute-start.43 = (bf16[72,768]{1,0:T(8,128)(2,1)S(1)}, bf16[72,768]{1,0:T(8,128)(2,1)S(1)}, u32[]{:S(2)}, u32[]{:S(2)}) collective-permute-start(bf16[72,768]{1,0:T(8,128)(2,1)S(1)} %dynamic-slice_convert_fusion.13), channel_id=1, source_target_pairs={{0,2},{2,0},{4,6},{6,4},{8,10},{10,8},{12,14},{14,12},{16,18},{18,... | collective-permute-start | bytes 331784 | tf_op jit(solution)/shard_map/ppermute | solution.py:95
  196.2 5.0 %collective-permute-start.45 = (bf16[72,768]{1,0:T(8,128)(2,1)S(1)}, bf16[72,768]{1,0:T(8,128)(2,1)S(1)}, u32[]{:S(2)}, u32[]{:S(2)}) collective-permute-start(bf16[72,768]{1,0:T(8,128)(2,1)S(1)} %maximum_select_fusion.18), channel_id=1, source_target_pairs={{0,8},{2,10},{4,12},{6,14},{8,0},{10,2},{12,4},{14,6},{16,24},{18,... | collective-permute-start | bytes 331784 | tf_op jit(solution)/shard_map/ppermute | solution.py:95
  196.2 5.9 %collective-permute-start.46 = (bf16[72,768]{1,0:T(8,128)(2,1)S(1)}, bf16[72,768]{1,0:T(8,128)(2,1)S(1)}, u32[]{:S(2)}, u32[]{:S(2)}) collective-permute-start(bf16[72,768]{1,0:T(8,128)(2,1)S(1)} %maximum_select_fusion.19), channel_id=1, source_target_pairs={{0,8},{2,10},{4,12},{6,14},{8,0},{10,2},{12,4},{14,6},{16,24},{18,... | collective-permute-start | bytes 331784 | tf_op jit(solution)/shard_map/ppermute | solution.py:95
  198.3 5.1 %collective-permute-start.47 = (bf16[96,576]{0,1:T(8,128)(2,1)S(1)}, bf16[96,576]{0,1:T(8,128)(2,1)S(1)}, u32[]{:S(2)}, u32[]{:S(2)}) collective-permute-start(bf16[96,576]{0,1:T(8,128)(2,1)S(1)} %maximum_select_fusion.15), channel_id=1, source_target_pairs={{0,2},{2,0},{4,6},{6,4},{8,10},{10,8},{12,14},{14,12},{16,18},{18,... | collective-permute-start | bytes 331784 | tf_op jit(solution)/shard_map/ppermute | solution.py:95
  203.8 6.2 %collective-permute-start.48 = (bf16[72,384]{1,0:T(8,128)(2,1)S(1)}, bf16[72,384]{1,0:T(8,128)(2,1)S(1)}, u32[]{:S(2)}, u32[]{:S(2)}) collective-permute-start(bf16[72,384]{1,0:T(8,128)(2,1)S(1)} %dynamic-slice_convert_fusion.18), channel_id=1, source_target_pairs={{0,8},{2,10},{4,12},{6,14},{8,0},{10,2},{12,4},{14,6},{16,24},{18,... | collective-permute-start | bytes 165896 | tf_op jit(solution)/shard_map/ppermute | solution.py:95
  203.8 5.2 %collective-permute-start.50 = (f32[2,576]{1,0:T(2,128)S(1)}, f32[2,576]{1,0:T(2,128)S(1)}, u32[]{:S(2)}, u32[]{:S(2)}) collective-permute-start(f32[2,576]{1,0:T(2,128)S(1)} %add.406), channel_id=1, source_target_pairs={{0,8},{2,10},{4,12},{6,14},{8,0},{10,2},{12,4},{14,6},{16,24},{18,... | collective-permute-start | bytes 13832 | tf_op jit(solution)/shard_map/ppermute | solution.py:95
  206.0 5.9 %collective-permute-start.51 = (bf16[72,1536]{1,0:T(8,128)(2,1)S(1)}, bf16[72,1536]{1,0:T(8,128)(2,1)S(1)}, u32[]{:S(2)}, u32[]{:S(2)}) collective-permute-start(bf16[72,1536]{1,0:T(8,128)(2,1)S(1)} %maximum_select_fusion.11), channel_id=1, source_target_pairs={{0,4},{2,6},{4,0},{6,2},{8,12},{10,14},{12,8},{14,10},{16,20},{18,... | collective-permute-start | bytes 663560 | tf_op jit(solution)/shard_map/ppermute | solution.py:95
  207.0 5.9 %collective-permute-start.52 = (bf16[72,1536]{1,0:T(8,128)(2,1)S(1)}, bf16[72,1536]{1,0:T(8,128)(2,1)S(1)}, u32[]{:S(2)}, u32[]{:S(2)}) collective-permute-start(bf16[72,1536]{1,0:T(8,128)(2,1)S(1)} %maximum_select_fusion.12), channel_id=1, source_target_pairs={{0,2},{2,0},{4,6},{6,4},{8,10},{10,8},{12,14},{14,12},{16,18},{18,... | collective-permute-start | bytes 663560 | tf_op jit(solution)/shard_map/ppermute | solution.py:95
  209.0 11.4 %collective-permute-start.53 = (bf16[192,576]{0,1:T(8,128)(2,1)S(1)}, bf16[192,576]{0,1:T(8,128)(2,1)S(1)}, u32[]{:S(2)}, u32[]{:S(2)}) collective-permute-start(bf16[192,576]{0,1:T(8,128)(2,1)S(1)} %maximum_select_fusion.10), channel_id=1, source_target_pairs={{0,16},{2,18},{4,20},{6,22},{8,24},{10,26},{12,28},{14,30},{16,0},... | collective-permute-start | bytes 663560 | tf_op jit(solution)/shard_map/ppermute | solution.py:95
  220.9 7.0 %collective-permute-start.54 = (bf16[72,192]{1,0:T(8,128)(2,1)S(1)}, bf16[72,192]{1,0:T(8,128)(2,1)S(1)}, u32[]{:S(2)}, u32[]{:S(2)}) collective-permute-start(bf16[72,192]{1,0:T(8,128)(2,1)S(1)} %dynamic-slice_convert_fusion.22), channel_id=1, source_target_pairs={{0,16},{2,18},{4,20},{6,22},{8,24},{10,26},{12,28},{14,30},{16,0},... | collective-permute-start | bytes 82952 | tf_op jit(solution)/shard_map/ppermute | solution.py:95
  221.0 5.2 %collective-permute-start.56 = (f32[2,576]{1,0:T(2,128)S(1)}, f32[2,576]{1,0:T(2,128)S(1)}, u32[]{:S(2)}, u32[]{:S(2)}) collective-permute-start(f32[2,576]{1,0:T(2,128)S(1)} %add.409), channel_id=1, source_target_pairs={{0,16},{2,18},{4,20},{6,22},{8,24},{10,26},{12,28},{14,30},{16,0},... | collective-permute-start | bytes 13832 | tf_op jit(solution)/shard_map/ppermute | solution.py:95
  224.0 5.0 %collective-permute-start.55 = (bf16[72,192]{1,0:T(8,128)(2,1)S(1)}, bf16[72,192]{1,0:T(8,128)(2,1)S(1)}, u32[]{:S(2)}, u32[]{:S(2)}) collective-permute-start(bf16[72,192]{1,0:T(8,128)(2,1)S(1)} %dynamic-slice_convert_fusion.21), channel_id=1, source_target_pairs={{0,16},{2,18},{4,20},{6,22},{8,24},{10,26},{12,28},{14,30},{16,0},... | collective-permute-start | bytes 82952 | tf_op jit(solution)/shard_map/ppermute | solution.py:95
  224.1 9.9 %collective-permute-start.57 = (bf16[144,1536]{1,0:T(8,128)(2,1)S(1)}, bf16[144,1536]{1,0:T(8,128)(2,1)S(1)}, u32[]{:S(2)}, u32[]{:S(2)}) collective-permute-start(bf16[144,1536]{1,0:T(8,128)(2,1)S(1)} %maximum_select_fusion.5), channel_id=1, source_target_pairs={{0,2},{2,0},{4,6},{6,4},{8,10},{10,8},{12,14},{14,12},{16,18},{18,... | collective-permute-start | bytes 1327112 | tf_op jit(solution)/shard_map/ppermute | solution.py:95
  226.0 9.5 %collective-permute-start.58 = (bf16[144,1536]{1,0:T(8,128)(2,1)S(1)}, bf16[144,1536]{1,0:T(8,128)(2,1)S(1)}, u32[]{:S(2)}, u32[]{:S(2)}) collective-permute-start(bf16[144,1536]{1,0:T(8,128)(2,1)S(1)} %maximum_select_fusion.6), channel_id=1, source_target_pairs={{0,4},{2,6},{4,0},{6,2},{8,12},{10,14},{12,8},{14,10},{16,20},{18,... | collective-permute-start | bytes 1327112 | tf_op jit(solution)/shard_map/ppermute | solution.py:95
  226.2 9.7 %collective-permute-start.59 = (bf16[384,576]{0,1:T(8,128)(2,1)S(1)}, bf16[384,576]{0,1:T(8,128)(2,1)S(1)}, u32[]{:S(2)}, u32[]{:S(2)}) collective-permute-start(bf16[384,576]{0,1:T(8,128)(2,1)S(1)} %maximum_select_fusion.7), channel_id=1, source_target_pairs={{0,8},{2,10},{4,12},{6,14},{8,0},{10,2},{12,4},{14,6},{16,24},{18,... | collective-permute-start | bytes 1327112 | tf_op jit(solution)/shard_map/ppermute | solution.py:95
  240.0 5.0 %collective-permute-start.62 = (bf16[72,192]{1,0:T(8,128)(2,1)S(1)}, bf16[72,192]{1,0:T(8,128)(2,1)S(1)}, u32[]{:S(2)}, u32[]{:S(2)}) collective-permute-start(bf16[72,192]{1,0:T(8,128)(2,1)S(1)} %convert_add_fusion.29), channel_id=1, source_target_pairs={{0,16},{2,18},{4,20},{6,22},{8,24},{10,26},{12,28},{14,30},{16,0},... | collective-permute-start | bytes 82952 | tf_op jit(solution)/shard_map/ppermute | solution.py:95
  250.0 7.2 %collective-permute-start.65 = (bf16[72,768]{1,0:T(8,128)(2,1)S(1)}, bf16[72,768]{1,0:T(8,128)(2,1)S(1)}, u32[]{:S(2)}, u32[]{:S(2)}) collective-permute-start(bf16[72,768]{1,0:T(8,128)(2,1)S(1)} %maximum_select_fusion.20), channel_id=1, source_target_pairs={{0,4},{2,6},{4,0},{6,2},{8,12},{10,14},{12,8},{14,10},{16,20},{18,... | collective-permute-start | bytes 331784 | tf_op jit(solution)/shard_map/ppermute | solution.py:95
  252.6 10.1 %collective-permute-start.60 = (f32[2,576]{1,0:T(2,128)S(1)}, f32[2,576]{1,0:T(2,128)S(1)}, u32[]{:S(2)}, u32[]{:S(2)}) collective-permute-start(f32[2,576]{1,0:T(2,128)S(1)} %add.412), channel_id=1, source_target_pairs={{0,1},{1,0},{2,3},{3,2},{4,5},{5,4},{6,7},{7,6},{8,9},{9,8},{10,11... | collective-permute-start | bytes 13832 | tf_op jit(solution)/shard_map/ppermute | solution.py:222
  256.8 5.5 %collective-permute-start.66 = (bf16[72,768]{1,0:T(8,128)(2,1)S(1)}, bf16[72,768]{1,0:T(8,128)(2,1)S(1)}, u32[]{:S(2)}, u32[]{:S(2)}) collective-permute-start(bf16[72,768]{1,0:T(8,128)(2,1)S(1)} %maximum_select_fusion.21), channel_id=1, source_target_pairs={{0,2},{2,0},{4,6},{6,4},{8,10},{10,8},{12,14},{14,12},{16,18},{18,... | collective-permute-start | bytes 331784 | tf_op jit(solution)/shard_map/ppermute | solution.py:95
  262.3 7.1 %collective-permute-start.67 = (bf16[144,768]{1,0:T(8,128)(2,1)S(1)}, bf16[144,768]{1,0:T(8,128)(2,1)S(1)}, u32[]{:S(2)}, u32[]{:S(2)}) collective-permute-start(bf16[144,768]{1,0:T(8,128)(2,1)S(1)} %maximum_select_fusion.13), channel_id=1, source_target_pairs={{0,2},{2,0},{4,6},{6,4},{8,10},{10,8},{12,14},{14,12},{16,18},{18,... | collective-permute-start | bytes 663560 | tf_op jit(solution)/shard_map/ppermute | solution.py:95
  262.8 6.8 %collective-permute-start.68 = (bf16[144,768]{1,0:T(8,128)(2,1)S(1)}, bf16[144,768]{1,0:T(8,128)(2,1)S(1)}, u32[]{:S(2)}, u32[]{:S(2)}) collective-permute-start(bf16[144,768]{1,0:T(8,128)(2,1)S(1)} %maximum_select_fusion.14), channel_id=1, source_target_pairs={{0,4},{2,6},{4,0},{6,2},{8,12},{10,14},{12,8},{14,10},{16,20},{18,... | collective-permute-start | bytes 663560 | tf_op jit(solution)/shard_map/ppermute | solution.py:95
  (35 other events, 182.9 us)
Sparse Core Ops, SparseCore 0:
  9.6 12.7 all-gather.7
  24.0 11.2 all-gather.5
  36.8 11.2 all-gather.3

commit v4 on v3

--- a/solution.py
+++ b/solution.py
@@ -106,31 +106,11 @@
     return held
 
 
-def lockstep(*trees):
-    results = [None] * len(trees)
-    running = list(range(len(trees)))
-    sent = [None] * len(trees)
-    while running:
-        held = {}
-        for place in list(running):
-            try:
-                held[place] = trees[place].send(sent[place])
-            except StopIteration as done:
-                results[place] = done.value
-                running.remove(place)
-        if held:
-            tied = lax.optimization_barrier(tuple(held.values()))
-            for place, value in zip(held, tied):
-                sent[place] = value
-    return results
-
-
 def scatter_tree(slots, order):
     held = slots.astype(jnp.float32)
     for bit in order[::-1]:
         half = held.shape[0] // 2
         held = held[:half] + swap(held[half:].astype(jnp.bfloat16), bit).astype(jnp.float32)
-        held = yield held
     return held
 
 
@@ -152,14 +132,18 @@
     return (owners[:, None] * rows + jnp.arange(rows, dtype=jnp.int32)[None, :]).reshape(-1, 1)
 
 
-def core_half(partial):
+def core_half(*partials):
     own_index = lax.axis_index("fsdp")
     part_count = lax.axis_size("fsdp")
-    rows = partial.shape[0] // part_count
-    own = lax.dynamic_slice_in_dim(partial, own_index * rows, rows, 0)
+    rows = partials[0].shape[0] // part_count
+
+    def rows_of(index):
+        return [lax.dynamic_slice_in_dim(p, index * rows, rows, 0) for p in partials]
+
+    own = jnp.concatenate(rows_of(own_index), 1)
     for shift in range(1, part_count):
         other = lax.rem(own_index + shift, part_count)
-        sent = lax.dynamic_slice_in_dim(partial, other * rows, rows, 0).astype(jnp.bfloat16)
+        sent = jnp.concatenate([p.astype(jnp.bfloat16) for p in rows_of(other)], 1)
         moves = [(a, (a + shift) % part_count) for a in range(part_count)]
         own = own + lax.ppermute(sent, "fsdp", moves).astype(jnp.float32)
     return own
@@ -173,7 +157,6 @@
         kept = lax.dynamic_slice_in_dim(held, mine * half, half, axis)
         sent = lax.dynamic_slice_in_dim(held, (1 - mine) * half, half, axis)
         held = kept + swap(sent.astype(jnp.bfloat16), bit).astype(jnp.float32)
-        held = yield held
     return held.astype(jnp.bfloat16)
 
 
@@ -186,7 +169,6 @@
             jnp.concatenate([held, other], axis),
             jnp.concatenate([other, held], axis),
         )
-        held = yield held
     return held.astype(jnp.float32)
 
 
@@ -210,18 +192,8 @@
     )
 
 
-def sum_tree(partial, order):
-    held = partial
-    for bit in order:
-        held = held + swap(held, bit)
-        held = yield held
-    count = lax.axis_size("fsdp")
-    parts = held
-    for shift in range(1, count):
-        moves = [(a, (a + shift) % count) for a in range(count)]
-        parts = parts + lax.ppermute(held, "fsdp", moves)
-    held = parts
-    return held
+def reduce_tree(partial, order):
+    return double_tree(halve_tree(partial, order), partial.shape, order)
 
 
 def heads_stacked(ref, group, repeat):
@@ -481,34 +453,27 @@
         grad_hidden * upward * sigmoid_gate * (1.0 + gate_pre * (1.0 - sigmoid_gate))
     ).astype(jnp.bfloat16)
     grad_upward = (grad_hidden * silu_gate).astype(jnp.bfloat16)
-    grad_gate_w = transposed_times(act_two, grad_gate)
-    grad_up_w = transposed_times(act_two, grad_upward)
+    grad_up_rest = transposed_times(act_two, grad_upward[:, 2 * grad_upward.shape[1] // 3 :])
     grad_act_two = times_transposed(grad_gate, gate_w) + times_transposed(grad_upward, up_w)
     back_two, grad_gain_ffn = norm_backward(grad_act_two, gain_ffn, normed_two, factor_two)
     grad_residual = grad_output.astype(jnp.float32) + back_two
     grad_attn = grad_residual.astype(jnp.bfloat16)
     grad_out_w = transposed_times(out_act, grad_attn)
     first_order, second_order, third_order = reduce_orders(lax.axis_size("ctx"))
-    half_gate, half_up, half_down = (
-        core_half(grad_gate_w),
-        core_half(grad_up_w),
-        core_half(grad_down_w),
-    )
+    cut = 2 * grad_upward.shape[1] // 3
+    wide = grad_gate.shape[1] + cut
+    half_one = core_half(
+        transposed_times(act_two, jnp.concatenate([grad_gate, grad_upward[:, :cut]], 1))
+    )
+    half_three = core_half(grad_down_w)
     grad_flat = times_transposed(grad_attn, out_w).astype(jnp.bfloat16)
-    half_gate, half_up, half_down, grad_flat = lax.optimization_barrier(
-        (half_gate, half_up, half_down, grad_flat)
-    )
+    half_one, half_three, grad_flat = lax.optimization_barrier((half_one, half_three, grad_flat))
     grad_queries, partial_keys, partial_values = attention_backward(
         first_place, places, scaled_queries, grad_flat, attended, log_totals, all_keys, all_values
     )
     grad_queries = grad_queries * score_scale
-    grad_keys, grad_values, piece_gate, piece_up, piece_down = lockstep(
-        scatter_tree(partial_keys, key_order),
-        scatter_tree(middle_swapped(partial_values, value_order), value_order),
-        halve_tree(half_gate, first_order),
-        halve_tree(half_up, second_order),
-        halve_tree(half_down, third_order),
-    )
+    grad_keys = scatter_tree(partial_keys, key_order)
+    grad_values = scatter_tree(middle_swapped(partial_values, value_order), value_order)
     grad_keys = grad_keys.reshape(local_rows, groups, HEAD_DIM)
     grad_query_pre = (
         unrotate(grad_queries.reshape(local_rows, HEADS, HEAD_DIM), cosine_table, sine_table)
@@ -528,25 +493,23 @@
     grad_act_one = times_transposed(grad_joined_pre, joined_w)
     back_one, grad_gain_attn = norm_backward(grad_act_one, gain_attn, normed_one, factor_one)
     grad_input = grad_residual + back_one
-    half_one = core_half(jnp.concatenate([grad_out_w, grad_key_w], 1))
-    half_two = core_half(jnp.concatenate([grad_query_w, grad_value_w], 1))
-    piece_one, piece_two, gains_sum, shard_gate, shard_up, shard_down = lockstep(
-        halve_tree(half_one, first_order),
-        halve_tree(half_two, second_order),
-        sum_tree(jnp.stack([grad_gain_attn, grad_gain_ffn]), first_order),
-        double_tree(piece_gate, half_gate.shape, first_order),
-        double_tree(piece_up, half_up.shape, second_order),
-        double_tree(piece_down, half_down.shape, third_order),
-    )
-    shard_one, shard_two = lockstep(
-        double_tree(piece_one, half_one.shape, first_order),
-        double_tree(piece_two, half_two.shape, second_order),
-    )
-    shard_out, shard_key = shard_one[:, :model_width], shard_one[:, model_width:]
-    shard_query, shard_value = shard_two[:, :model_width], shard_two[:, model_width:]
-    shard_gains = lax.dynamic_slice_in_dim(
-        gains_sum, lax.axis_index("fsdp") * norm_attn.shape[0], norm_attn.shape[0], 1
-    )
+    gain_columns = jnp.stack([grad_gain_attn, grad_gain_ffn], 1)
+    kept_parts = (grad_up_rest, grad_out_w, grad_key_w, grad_query_w, grad_value_w)
+    spare = wide - sum(p.shape[1] for p in kept_parts)
+    gain_columns = jnp.pad(gain_columns, ((0, 0), (0, max(spare, 2) - 2)))
+    half_two = core_half(*kept_parts, gain_columns)
+    shard_one = reduce_tree(half_one, first_order)
+    shard_two = reduce_tree(half_two, second_order)
+    shard_down = reduce_tree(half_three, third_order)
+    ends = [0]
+    for part in kept_parts:
+        ends.append(ends[-1] + part.shape[1])
+    up_rest, shard_out, shard_key, shard_query, shard_value = (
+        shard_two[:, ends[i] : ends[i + 1]] for i in range(len(kept_parts))
+    )
+    shard_gate = shard_one[:, : grad_gate.shape[1]]
+    shard_up = jnp.concatenate([shard_one[:, grad_gate.shape[1] :], up_rest], 1)
+    shard_gains = shard_two[:, ends[-1] : ends[-1] + 2].T
     return (
         result[None],
         grad_input[None],

time: 280 us -> 272 us (0.971)
  starting transfers between devices: 75 us -> 50.4 us
  local copies, waits for them, and re-layouts: 17.6 us -> 31.1 us
    ppermute x60 -> x40, starting transfers between devices: 72.6 us -> 48.4 us  [swap(): lax.ppermute(values, 'ctx', [(i, i ^ 1 << bit) for i in range(count)])]
    concatenate x0 -> x2, local copies, waits for them, and re-layouts: none -> 6.55 us  [the longest x1 3.67 us: core_half(): sent = jnp.concatenate([p.astype(jnp.bfloat16) for p in rows_of(other)], 1)]
    dynamic_slice x0 -> x5, local copies, waits for them, and re-layouts: none -> 4.43 us  [rows_of(): lax.dynamic_slice_in_dim(p, index * rows, rows, 0)]
    add x5 -> x3, other arithmetic: 1.07 us -> 5.13 us  [core_half(): own = own + lax.ppermute(sent, 'fsdp', moves).astype(jnp.float32)]
    convert_element_type x3 -> x7, local copies, waits for them, and re-layouts: 0.32 us -> 4.2 us  [core_half(): sent = jnp.concatenate([p.astype(jnp.bfloat16) for p in rows_of(other)], 1)]
    unnamed x64 -> x92, local copies, waits for them, and re-layouts: 6.15 us -> 4.43 us
    ppermute x60 -> x40, waiting for transfers between devices: 109 us -> 110 us  [swap(): lax.ppermute(values, 'ctx', [(i, i ^ 1 << bit) for i in range(count)])]
  transfers between devices with their start and end apart: 72 -> 49, of which waited for: 44 -> 29; matrix products, arithmetic and copies ran while one was open for 14% -> 22% of each run, Pallas kernels for 3% -> 3%
where the time goes in v4:
time: 272 us
  waiting for transfers between devices  112 us (41%)
  starting transfers between devices  50.4 us (19%)
  local copies, waits for them, and re-layouts  31.1 us (11%)
  other arithmetic  23.5 us (9%)
  matrix products  19.9 us (7%)
  Pallas kernels  19.8 us (7%)
  between operations  15.1 us (6%)
    ppermute x40, waiting for transfers between devices, swap(): lax.ppermute(values, 'ctx', [(i, i ^ 1 << bit) for i in range(count)])  110 us
    ppermute x40, starting transfers between devices, swap(): lax.ppermute(values, 'ctx', [(i, i ^ 1 << bit) for i in range(count)])  48.4 us
    pallas_call x1, Pallas kernels, attention_backward(): pl.pallas_call(backward_kernel, grid=(all_keys.shape[0] // keys,), in_spe...  10.6 us
    pallas_call x1, Pallas kernels, attention_forward(): pl.pallas_call(forward_kernel, grid=(all_keys.shape[0] // keys,), in_spec...  9.17 us
    dot_general x5, matrix products, times_transposed(): lax.dot_general(left, right, (((1,), (1,)), ((), ())), preferred_element_...  7.12 us
  transfers between devices with their start and end apart: 49, of which 29 were waited for; matrix products, arithmetic and copies ran while one was open for 22% of the time, Pallas kernels for 3%

profile of v4, /device:TPU:0, one launch (start us, length us, event | category | flops | bytes accessed | tf_op | source)
XLA Modules:
  0.0 271.7 jit_solution(12186731750787776961)
XLA Ops:
  12.2 1.9 maximum_select_fusion.2
  15.7 3.9 %collective-permute-start.2 = (bf16[128,192]{1,0:T(8,128)(2,1)S(1)}, bf16[128,192]{1,0:T(8,128)(2,1)S(1)}, u32[]{:S(2)}, u32[]{:S(2)}) collective-permute-start(bf16[128,192]{1,0:T(8,128)(2,1)S(1)} %copy.75), channel_id=1, source_target_pairs={{0,16},{2,18},{4,20},{6,22},{8,24},{10,26},{12,28},{14,30},{16,0},... | collective-permute-start | bytes 147464 | tf_op jit(solution)/shard_map/ppermute | solution.py:95
  20.1 3.6 %collective-permute-done.2 = bf16[128,192]{1,0:T(8,128)(2,1)S(1)} collective-permute-done((bf16[128,192]{1,0:T(8,128)(2,1)S(1)}, bf16[128,192]{1,0:T(8,128)(2,1)S(1)}, u32[]{:S(2)}, u32[]{:S(2)}) %collective-permute-start.2) | collective-permute-done | bytes 49184 | tf_op jit(solution)/shard_map/ppermute | solution.py:95
  23.7 2.1 collective-permute-start.3
  27.7 4.5 %collective-permute-done.7 = bf16[256,192]{1,0:T(8,128)(2,1)S(1)} collective-permute-done((bf16[256,192]{1,0:T(8,128)(2,1)S(1)}, bf16[256,192]{1,0:T(8,128)(2,1)S(1)}, u32[]{:S(2)}, u32[]{:S(2)}) %collective-permute-start.7) | collective-permute-done | bytes 98336 | tf_op jit(solution)/shard_map/ppermute | solution.py:95
  32.3 1.6 collective-permute-start.8
  33.9 1.6 collective-permute-start.4
  35.5 4.5 %collective-permute-done.8 = bf16[512,192]{1,0:T(8,128)(2,1)S(1)} collective-permute-done((bf16[512,192]{1,0:T(8,128)(2,1)S(1)}, bf16[512,192]{1,0:T(8,128)(2,1)S(1)}, u32[]{:S(2)}, u32[]{:S(2)}) %collective-permute-start.8) | collective-permute-done | bytes 196640 | tf_op jit(solution)/shard_map/ppermute | solution.py:95
  40.1 1.3 collective-permute-start.9
  41.5 1.6 collective-permute-start.5
  43.1 9.4 %collective-permute-done.9 = bf16[1024,192]{1,0:T(8,128)(2,1)S(1)} collective-permute-done((bf16[1024,192]{1,0:T(8,128)(2,1)S(1)}, bf16[1024,192]{1,0:T(8,128)(2,1)S(1)}, u32[]{:S(2)}, u32[]{:S(2)}) %collective-permute-start.9) | collective-permute-done | bytes 393248 | tf_op jit(solution)/shard_map/ppermute | solution.py:95
  53.5 9.2 %shard_map.194 = (f32[128,576]{1,0:T(8,128)S(1)}, f32[3,384]{1,0:T(4,128)S(1)}) custom-call(s32[1]{0:T(128)} %bitcast.1.first_ref, s32[2048,1]{1,0:T(8,128)S(1)} %copy.77.place_ref, bf16[128,576]{1,0:T(8,128)(2,1)S(1)} %copy.78.query_ref, bf16[2048,192]{1,0:T(8,128)(2,1)S(1)} %constant_dynamic-update-slice_fusion.key_ref, ...), custom_call_target="tpu_custom_call" | custom-call | flops 2013265920 | bytes 33554432 | tf_op jit(solution)/shard_map/pallas_call | solution.py:321
  62.7 1.8 multiply_reduce_fusion.2
  64.7 2.9 %fusion.36 = f32[128,1536]{1,0:T(8,128)} fusion(bf16[1536,576]{0,1:T(8,128)(2,1)} %all-gather.8.cloned.1.call-done, bf16[1,128,576]{1,2,0:T(8,128)(2,1)S(1)} %copy-done.25), kind=kOutput, calls=%fused_computation.126 | convolution fusion | flops 226492416 | bytes 2703360 | tf_op jit(solution)/shard_map/dot_general | solution.py:61
  67.6 2.9 %fusion.75 = f32[128,1536]{1,0:T(8,128)} fusion(bf16[128,576]{0,1:T(8,128)(2,1)S(1)} %multiply_convert_fusion.3, bf16[576,1536]{1,0:T(8,128)(2,1)} %all-gather.6.cloned.1.call-done), kind=kOutput, calls=%fused_computation.210 | convolution fusion | flops 226492416 | bytes 2703360 | tf_op jit(solution)/shard_map/dot_general | solution.py:443
  70.5 2.9 %multiply_convert_fusion = (bf16[128,1536]{1,0:T(8,128)(2,1)S(1)}, bf16[128,1536]{1,0:T(8,128)(2,1)S(1)}, bf16[128,1536]{1,0:T(8,128)(2,1)S(1)}) fusion(f32[128,1536]{1,0:T(8,128)} %fusion.36, f32[128,1536]{1,0:T(8,128)} %fusion.75, bf16[128,576]{0,1:T(8,128)(2,1)S(1)} %multiply_convert_fusion.3, bf16[576,1536]{1,0:T(8,128)(2,1)} %all-gather.4.cloned.1.call-done), kind=kOutput, calls=%fused_computation.29 | convolution fusion | flops 229441536 | bytes 4669440 | tf_op jit(solution)/shard_map/dot_general | solution.py:442
  82.8 1.3 fusion.3
  84.1 1.7 convolution_convert_fusion.grad_ref
  85.9 1.5 convert_add_fusion.2
  87.4 1.9 convert_add_fusion.1
  89.6 10.6 %shard_map.195 = (f32[128,576]{1,0:T(8,128)S(1)}, bf16[2048,192]{1,0:T(8,128)(2,1)S(1)}, bf16[2048,192]{1,0:T(8,128)(2,1)S(1)}) custom-call(s32[1]{0:T(128)} %bitcast.1.first_ref, s32[2048,1]{1,0:T(8,128)S(1)} %copy.77.place_ref, bf16[128,576]{1,0:T(8,128)(2,1)S(1)} %copy.78.query_ref, bf16[128,576]{1,0:T(8,128)(2,1)S(1)} %convolution_convert_fusion.grad_ref, ...), custom_call_target="tpu_custom_call" | custom-call | flops 2013265920 | bytes 33554432 | tf_op jit(solution)/shard_map/pallas_call | solution.py:355
  103.6 2.3 dynamic-slice_convert_fusion.2
  107.0 1.2 dynamic-slice_convert_fusion.4
  108.2 1.7 collective-permute-start.38
  112.1 3.2 %collective-permute-done.17 = bf16[1024,192]{1,0:T(8,128)(2,1)} collective-permute-done((bf16[1024,192]{1,0:T(8,128)(2,1)}, bf16[1024,192]{1,0:T(8,128)(2,1)}, u32[]{:S(2)}, u32[]{:S(2)}) %collective-permute-start.17) | collective-permute-done | bytes 393248 | tf_op jit(solution)/shard_map/ppermute | solution.py:95
  116.5 1.6 collective-permute-start.18
  120.1 4.0 %collective-permute-start.39 = (bf16[192,576]{0,1:T(8,128)(2,1)S(1)}, bf16[192,576]{0,1:T(8,128)(2,1)S(1)}, u32[]{:S(2)}, u32[]{:S(2)}) collective-permute-start(bf16[192,576]{0,1:T(8,128)(2,1)S(1)} %dynamic-slice_convert_fusion.9), channel_id=1, source_target_pairs={{0,16},{2,18},{4,20},{6,22},{8,24},{10,26},{12,28},{14,30},{16,0},... | collective-permute-start | bytes 663560 | tf_op jit(solution)/shard_map/ppermute | solution.py:95
  124.1 13.3 %collective-permute-done.18 = bf16[512,192]{1,0:T(8,128)(2,1)S(1)} collective-permute-done((bf16[512,192]{1,0:T(8,128)(2,1)S(1)}, bf16[512,192]{1,0:T(8,128)(2,1)S(1)}, u32[]{:S(2)}, u32[]{:S(2)}) %collective-permute-start.18) | collective-permute-done | bytes 196640 | tf_op jit(solution)/shard_map/ppermute | solution.py:95
  137.4 1.7 collective-permute-start.19
  143.2 4.5 %collective-permute-start.20 = (bf16[128,192]{1,0:T(8,128)(2,1)S(1)}, bf16[128,192]{1,0:T(8,128)(2,1)S(1)}, u32[]{:S(2)}, u32[]{:S(2)}) collective-permute-start(bf16[128,192]{1,0:T(8,128)(2,1)S(1)} %slice.291), channel_id=1, source_target_pairs={{0,16},{2,18},{4,20},{6,22},{8,24},{10,26},{12,28},{14,30},{16,0},... | collective-permute-start | bytes 147464 | tf_op jit(solution)/shard_map/ppermute | solution.py:95
  147.8 1.7 collective-permute-start.16
  150.8 2.9 %collective-permute-done.16 = bf16[128,192]{1,0:T(8,128)(2,1)S(1)} collective-permute-done((bf16[128,192]{1,0:T(8,128)(2,1)S(1)}, bf16[128,192]{1,0:T(8,128)(2,1)S(1)}, u32[]{:S(2)}, u32[]{:S(2)}) %collective-permute-start.16) | collective-permute-done | bytes 49184 | tf_op jit(solution)/shard_map/ppermute | solution.py:95
  153.8 1.2 fusion.23
  157.5 3.7 %concatenate.183 = bf16[288,2560]{1,0:T(8,128)(2,1)} concatenate(bf16[288,512]{1,0:T(8,128)(2,1)} %dynamic-slice_convert_fusion.10, bf16[288,576]{1,0:T(8,128)(2,1)} %dynamic-slice_convert_fusion.8, bf16[288,192]{1,0:T(8,128)(2,1)} %get-tuple-element.61, bf16[288,576]{1,0:T(8,128)(2,1)} %dynamic-slice_convert_fusion.7, bf16[288,192]{1,0:T(8,128)(2,1)S(1)} %get-tuple-element.60, ...), dimensions={1} | concatenate | bytes 2949120 | tf_op jit(solution)/shard_map/concatenate | solution.py:146
  161.2 2.5 convert_add_fusion.3
  167.1 2.9 %concatenate.182 = f32[288,2560]{1,0:T(8,128)S(1)} concatenate(f32[288,512]{1,0:T(8,128)} %constant_dynamic-slice_fusion.4, f32[288,576]{1,0:T(8,128)} %constant_dynamic-slice_fusion.3, f32[288,192]{1,0:T(8,128)} %get-tuple-element.63, f32[288,576]{1,0:T(8,128)} %constant_dynamic-slice_fusion.1, f32[288,192]{1,0:T(8,128)} %get-tuple-element.62, f32[288,512]{1,0:T(8,128)} %pad_dynamic-slice_fusion.1), dimensions={1} | concatenate | bytes 5898240 | tf_op jit(solution)/shard_map/concatenate | solution.py:143
  170.0 2.1 collective-permute-done.41
  173.7 1.7 convert_add_fusion
  175.5 1.7 collective-permute-start.22
  177.3 2.6 collective-permute-done.42
  180.1 2.4 collective-permute-start.31
  182.6 2.7 collective-permute-done.43
  186.3 9.4 %collective-permute-done.22 = bf16[144,2560]{1,0:T(8,128)(2,1)S(1)} collective-permute-done((bf16[144,2560]{1,0:T(8,128)(2,1)S(1)}, bf16[144,2560]{1,0:T(8,128)(2,1)S(1)}, u32[]{:S(2)}, u32[]{:S(2)}) %collective-permute-start.22) | collective-permute-done | bytes 737312 | tf_op jit(solution)/shard_map/ppermute | solution.py:95
  195.9 1.5 collective-permute-start.23
  197.3 5.0 %collective-permute-done.31 = bf16[72,2560]{1,0:T(8,128)(2,1)S(1)} collective-permute-done((bf16[72,2560]{1,0:T(8,128)(2,1)S(1)}, bf16[72,2560]{1,0:T(8,128)(2,1)S(1)}, u32[]{:S(2)}, u32[]{:S(2)}) %collective-permute-start.31) | collective-permute-done | bytes 368672 | tf_op jit(solution)/shard_map/ppermute | solution.py:95
  202.5 1.6 collective-permute-done.23
  204.7 6.2 %collective-permute-done.32 = bf16[72,1280]{1,0:T(8,128)(2,1)S(1)} collective-permute-done((bf16[72,1280]{1,0:T(8,128)(2,1)S(1)}, bf16[72,1280]{1,0:T(8,128)(2,1)S(1)}, u32[]{:S(2)}, u32[]{:S(2)}) %collective-permute-start.32) | collective-permute-done | bytes 184352 | tf_op jit(solution)/shard_map/ppermute | solution.py:95
  211.2 1.6 collective-permute-done.24
  212.9 1.5 collective-permute-start.25
  214.4 5.2 %collective-permute-done.33 = bf16[72,640]{1,0:T(8,128)(2,1)S(1)} collective-permute-done((bf16[72,640]{1,0:T(8,128)(2,1)S(1)}, bf16[72,640]{1,0:T(8,128)(2,1)S(1)}, u32[]{:S(2)}, u32[]{:S(2)}) %collective-permute-start.33) | collective-permute-done | bytes 92192 | tf_op jit(solution)/shard_map/ppermute | solution.py:95
  219.7 1.8 collective-permute-done.25
  221.5 1.2 collective-permute-start.26
  222.8 3.5 %collective-permute-done.34 = bf16[72,640]{1,0:T(8,128)(2,1)S(1)} collective-permute-done((bf16[72,640]{1,0:T(8,128)(2,1)S(1)}, bf16[72,640]{1,0:T(8,128)(2,1)S(1)}, u32[]{:S(2)}, u32[]{:S(2)}) %collective-permute-start.34) | collective-permute-done | bytes 92192 | tf_op jit(solution)/shard_map/ppermute | solution.py:95
  226.4 1.9 collective-permute-done.26
  228.5 4.1 %collective-permute-done.35 = bf16[72,1280]{1,0:T(8,128)(2,1)S(1)} collective-permute-done((bf16[72,1280]{1,0:T(8,128)(2,1)S(1)}, bf16[72,1280]{1,0:T(8,128)(2,1)S(1)}, u32[]{:S(2)}, u32[]{:S(2)}) %collective-permute-start.35) | collective-permute-done | bytes 184352 | tf_op jit(solution)/shard_map/ppermute | solution.py:95
  232.8 1.8 collective-permute-done.27
  234.7 1.4 collective-permute-start.28
  236.8 3.4 %collective-permute-done.36 = bf16[72,2560]{1,0:T(8,128)(2,1)S(1)} collective-permute-done((bf16[72,2560]{1,0:T(8,128)(2,1)S(1)}, bf16[72,2560]{1,0:T(8,128)(2,1)S(1)}, u32[]{:S(2)}, u32[]{:S(2)}) %collective-permute-start.36) | collective-permute-done | bytes 368672 | tf_op jit(solution)/shard_map/ppermute | solution.py:95
  241.6 4.7 %collective-permute-done.28 = bf16[72,2560]{1,0:T(8,128)(2,1)S(1)} collective-permute-done((bf16[72,2560]{1,0:T(8,128)(2,1)S(1)}, bf16[72,2560]{1,0:T(8,128)(2,1)S(1)}, u32[]{:S(2)}, u32[]{:S(2)}) %collective-permute-start.28) | collective-permute-done | bytes 368672 | tf_op jit(solution)/shard_map/ppermute | solution.py:95
  248.5 1.4 fusion.4
  249.8 8.0 %collective-permute-done.37 = bf16[144,2560]{1,0:T(8,128)(2,1)S(1)} collective-permute-done((bf16[144,2560]{1,0:T(8,128)(2,1)S(1)}, bf16[144,2560]{1,0:T(8,128)(2,1)S(1)}, u32[]{:S(2)}, u32[]{:S(2)}) %collective-permute-start.37) | collective-permute-done | bytes 737312 | tf_op jit(solution)/shard_map/ppermute | solution.py:95
  258.2 1.4 slice.237
  260.7 1.2 fusion.72
  263.9 1.3 pad_maximum_fusion
  (278 shorter events, 53.8 us)
Async XLA Ops:
  7.2 57.5 %all-gather.8.cloned.1.call-start = ((), (), s32[]{:S(2)}) async-start(), calls=%async_computation.2 | async-start | bytes 2654208 | tf_op jit(solution)/shard_map/all_gather | solution.py:399
  8.0 59.6 %all-gather.6.cloned.1.call-start = ((), (), s32[]{:S(2)}) async-start(), calls=%async_computation.1 | async-start | bytes 2654208 | tf_op jit(solution)/shard_map/all_gather | solution.py:398
  8.7 61.8 %all-gather.4.cloned.1.call-start = ((), (), s32[]{:S(2)}) async-start(), calls=%async_computation | async-start | bytes 2654208 | tf_op jit(solution)/shard_map/all_gather | solution.py:397
  8.8 53.9 %collective-permute-start.10 = (bf16[288,576]{1,0:T(8,128)(2,1)}, bf16[288,576]{1,0:T(8,128)(2,1)}, u32[]{:S(2)}, u32[]{:S(2)}) collective-permute-start(bf16[288,576]{1,0:T(8,128)(2,1)} %param.17), channel_id=1, source_target_pairs={{0,1},{1,0},{2,3},{3,2},{4,5},{5,4},{6,7},{7,6},{8,9},{9,8},{10,11... | collective-permute-start | bytes 995336 | tf_op jit(solution)/shard_map/ppermute | solution.py:187
  9.4 2.8 %collective-permute-start.1 = (bf16[288,960]{1,0:T(8,128)(2,1)S(1)}, bf16[288,960]{1,0:T(8,128)(2,1)}, u32[]{:S(2)}, u32[]{:S(2)}) collective-permute-start(bf16[288,960]{1,0:T(8,128)(2,1)S(1)} %pad_maximum_fusion.1), channel_id=1, source_target_pairs={{0,1},{1,0},{2,3},{3,2},{4,5},{5,4},{6,7},{7,6},{8,9},{9,8},{10,11... | collective-permute-start | bytes 1658888 | tf_op jit(solution)/shard_map/ppermute | solution.py:187
  9.6 1.9 collective-permute-start
  10.9 4.0 %copy-start.34 = (f32[128]{0:T(128)}, f32[128]{0:T(128)S(1)}, u32[]{:S(2)}) copy-start(f32[128]{0:T(128)S(1)} %add_rsqrt_fusion.1) | copy-start | bytes 1540
  15.7 7.9 %collective-permute-start.2 = (bf16[128,192]{1,0:T(8,128)(2,1)S(1)}, bf16[128,192]{1,0:T(8,128)(2,1)S(1)}, u32[]{:S(2)}, u32[]{:S(2)}) collective-permute-start(bf16[128,192]{1,0:T(8,128)(2,1)S(1)} %copy.75), channel_id=1, source_target_pairs={{0,16},{2,18},{4,20},{6,22},{8,24},{10,26},{12,28},{14,30},{16,0},... | collective-permute-start | bytes 147464 | tf_op jit(solution)/shard_map/ppermute | solution.py:95
  19.7 6.6 %collective-permute-start.6 = (bf16[128,192]{1,0:T(8,128)(2,1)S(1)}, bf16[128,192]{1,0:T(8,128)(2,1)S(1)}, u32[]{:S(2)}, u32[]{:S(2)}) collective-permute-start(bf16[128,192]{1,0:T(8,128)(2,1)S(1)} %copy.93), channel_id=1, source_target_pairs={{0,16},{2,18},{4,20},{6,22},{8,24},{10,26},{12,28},{14,30},{16,0},... | collective-permute-start | bytes 147464 | tf_op jit(solution)/shard_map/ppermute | solution.py:95
  23.7 10.1 %collective-permute-start.3 = (bf16[256,192]{1,0:T(8,128)(2,1)S(1)}, bf16[256,192]{1,0:T(8,128)(2,1)S(1)}, u32[]{:S(2)}, u32[]{:S(2)}) collective-permute-start(bf16[256,192]{1,0:T(8,128)(2,1)S(1)} %pad_maximum_fusion.7), channel_id=1, source_target_pairs={{0,8},{2,10},{4,12},{6,14},{8,0},{10,2},{12,4},{14,6},{16,24},{18,... | collective-permute-start | bytes 294920 | tf_op jit(solution)/shard_map/ppermute | solution.py:95
  26.4 5.8 %collective-permute-start.7 = (bf16[256,192]{1,0:T(8,128)(2,1)S(1)}, bf16[256,192]{1,0:T(8,128)(2,1)S(1)}, u32[]{:S(2)}, u32[]{:S(2)}) collective-permute-start(bf16[256,192]{1,0:T(8,128)(2,1)S(1)} %pad_maximum_fusion.8), channel_id=1, source_target_pairs={{0,8},{2,10},{4,12},{6,14},{8,0},{10,2},{12,4},{14,6},{16,24},{18,... | collective-permute-start | bytes 294920 | tf_op jit(solution)/shard_map/ppermute | solution.py:95
  27.7 13.7 %copy-start.2 = (bf16[2048,192]{1,0:T(8,128)(2,1)S(1)}, bf16[2048,192]{1,0:T(8,128)(2,1)}, u32[]{:S(2)}) copy-start(bf16[2048,192]{1,0:T(8,128)(2,1)} %constant_dynamic-update-slice_fusion.3) | copy-start | bytes 2359300
  32.3 7.7 %collective-permute-start.8 = (bf16[512,192]{1,0:T(8,128)(2,1)S(1)}, bf16[512,192]{1,0:T(8,128)(2,1)S(1)}, u32[]{:S(2)}, u32[]{:S(2)}) collective-permute-start(bf16[512,192]{1,0:T(8,128)(2,1)S(1)} %pad_maximum_fusion.6), channel_id=1, source_target_pairs={{0,2},{2,0},{4,6},{6,4},{8,10},{10,8},{12,14},{14,12},{16,18},{18,... | collective-permute-start | bytes 589832 | tf_op jit(solution)/shard_map/ppermute | solution.py:95
  33.9 7.6 %collective-permute-start.4 = (bf16[512,192]{1,0:T(8,128)(2,1)S(1)}, bf16[512,192]{1,0:T(8,128)(2,1)S(1)}, u32[]{:S(2)}, u32[]{:S(2)}) collective-permute-start(bf16[512,192]{1,0:T(8,128)(2,1)S(1)} %pad_maximum_fusion.5), channel_id=1, source_target_pairs={{0,4},{2,6},{4,0},{6,2},{8,12},{10,14},{12,8},{14,10},{16,20},{18,... | collective-permute-start | bytes 589832 | tf_op jit(solution)/shard_map/ppermute | solution.py:95
  40.1 12.4 %collective-permute-start.9 = (bf16[1024,192]{1,0:T(8,128)(2,1)S(1)}, bf16[1024,192]{1,0:T(8,128)(2,1)S(1)}, u32[]{:S(2)}, u32[]{:S(2)}) collective-permute-start(bf16[1024,192]{1,0:T(8,128)(2,1)S(1)} %pad_maximum_fusion.3), channel_id=1, source_target_pairs={{0,4},{2,6},{4,0},{6,2},{8,12},{10,14},{12,8},{14,10},{16,20},{18,... | collective-permute-start | bytes 1179656 | tf_op jit(solution)/shard_map/ppermute | solution.py:95
  41.5 11.9 %collective-permute-start.5 = (bf16[1024,192]{1,0:T(8,128)(2,1)S(1)}, bf16[1024,192]{1,0:T(8,128)(2,1)S(1)}, u32[]{:S(2)}, u32[]{:S(2)}) collective-permute-start(bf16[1024,192]{1,0:T(8,128)(2,1)S(1)} %pad_maximum_fusion.2), channel_id=1, source_target_pairs={{0,2},{2,0},{4,6},{6,4},{8,10},{10,8},{12,14},{14,12},{16,18},{18,... | collective-permute-start | bytes 1179656 | tf_op jit(solution)/shard_map/ppermute | solution.py:95
  52.6 10.1 %copy-start = (bf16[2048,192]{1,0:T(8,128)(2,1)}, bf16[2048,192]{1,0:T(8,128)(2,1)S(1)}, u32[]{:S(2)}) copy-start(bf16[2048,192]{1,0:T(8,128)(2,1)S(1)} %slice_dynamic-update-slice_fusion.value_ref) | copy-start | bytes 2359300
  53.5 9.2 %copy-start.3 = (bf16[2048,192]{1,0:T(8,128)(2,1)}, bf16[2048,192]{1,0:T(8,128)(2,1)S(1)}, u32[]{:S(2)}) copy-start(bf16[2048,192]{1,0:T(8,128)(2,1)S(1)} %constant_dynamic-update-slice_fusion.key_ref) | copy-start | bytes 2359300
  76.7 10.7 %collective-permute-start.11 = (bf16[288,2560]{1,0:T(8,128)(2,1)S(1)}, bf16[288,2560]{1,0:T(8,128)(2,1)S(1)}, u32[]{:S(2)}, u32[]{:S(2)}) collective-permute-start(bf16[288,2560]{1,0:T(8,128)(2,1)S(1)} %dynamic-slice_convert_fusion), channel_id=1, source_target_pairs={{0,1},{1,0},{2,3},{3,2},{4,5},{5,4},{6,7},{7,6},{8,9},{9,8},{10,11... | collective-permute-start | bytes 4423688 | tf_op jit(solution)/shard_map/ppermute | solution.py:148
  77.5 8.4 %collective-permute-start.12 = (bf16[768,576]{0,1:T(8,128)(2,1)S(1)}, bf16[768,576]{0,1:T(8,128)(2,1)S(1)}, u32[]{:S(2)}, u32[]{:S(2)}) collective-permute-start(bf16[768,576]{0,1:T(8,128)(2,1)S(1)} %dynamic-slice_convert_fusion.1), channel_id=1, source_target_pairs={{0,1},{1,0},{2,3},{3,2},{4,5},{5,4},{6,7},{7,6},{8,9},{9,8},{10,11... | collective-permute-start | bytes 2654216 | tf_op jit(solution)/shard_map/ppermute | solution.py:148
  101.2 14.1 %collective-permute-start.17 = (bf16[1024,192]{1,0:T(8,128)(2,1)}, bf16[1024,192]{1,0:T(8,128)(2,1)}, u32[]{:S(2)}, u32[]{:S(2)}) collective-permute-start(bf16[1024,192]{1,0:T(8,128)(2,1)} %pad_maximum_fusion.4), channel_id=1, source_target_pairs={{0,4},{2,6},{4,0},{6,2},{8,12},{10,14},{12,8},{14,10},{16,20},{18,... | collective-permute-start | bytes 1179656 | tf_op jit(solution)/shard_map/ppermute | solution.py:95
  102.4 15.7 %collective-permute-start.13 = (bf16[1024,192]{1,0:T(8,128)(2,1)S(1)}, bf16[1024,192]{1,0:T(8,128)(2,1)}, u32[]{:S(2)}, u32[]{:S(2)}) collective-permute-start(bf16[1024,192]{1,0:T(8,128)(2,1)S(1)} %slice.170), channel_id=1, source_target_pairs={{0,2},{2,0},{4,6},{6,4},{8,10},{10,8},{12,14},{14,12},{16,18},{18,... | collective-permute-start | bytes 1179656 | tf_op jit(solution)/shard_map/ppermute | solution.py:95
  103.5 6.5 %copy-start.30 = (f32[576]{0:T(1024)S(1)}, f32[576]{0:T(1024)}, u32[]{:S(2)}) copy-start(f32[576]{0:T(1024)} %copy-done.29) | copy-start | bytes 6916
  103.5 6.5 %copy-start.35 = (f32[128]{0:T(128)S(1)}, f32[128]{0:T(128)}, u32[]{:S(2)}) copy-start(f32[128]{0:T(128)} %copy-done.34) | copy-start | bytes 1540
  105.9 55.4 %collective-permute-start.30 = (bf16[144,2560]{1,0:T(8,128)(2,1)}, bf16[144,2560]{1,0:T(8,128)(2,1)}, u32[]{:S(2)}, u32[]{:S(2)}) collective-permute-start(bf16[144,2560]{1,0:T(8,128)(2,1)} %dynamic-slice_convert_fusion.2), channel_id=1, source_target_pairs={{0,2},{2,0},{4,6},{6,4},{8,10},{10,8},{12,14},{14,12},{16,18},{18,... | collective-permute-start | bytes 2211848 | tf_op jit(solution)/shard_map/ppermute | solution.py:95
  108.2 11.6 %collective-permute-start.38 = (bf16[384,576]{0,1:T(8,128)(2,1)S(1)}, bf16[384,576]{0,1:T(8,128)(2,1)S(1)}, u32[]{:S(2)}, u32[]{:S(2)}) collective-permute-start(bf16[384,576]{0,1:T(8,128)(2,1)S(1)} %dynamic-slice_convert_fusion.4), channel_id=1, source_target_pairs={{0,8},{2,10},{4,12},{6,14},{8,0},{10,2},{12,4},{14,6},{16,24},{18,... | collective-permute-start | bytes 1327112 | tf_op jit(solution)/shard_map/ppermute | solution.py:95
  116.5 3.4 %copy-start.9 = (f32[768,576]{0,1:T(8,128)S(1)}, f32[768,576]{0,1:T(8,128)}, u32[]{:S(2)}) copy-start(f32[768,576]{0,1:T(8,128)} %convert_add_fusion.2) | copy-start | bytes 5308420
  116.5 20.8 %collective-permute-start.18 = (bf16[512,192]{1,0:T(8,128)(2,1)S(1)}, bf16[512,192]{1,0:T(8,128)(2,1)S(1)}, u32[]{:S(2)}, u32[]{:S(2)}) collective-permute-start(bf16[512,192]{1,0:T(8,128)(2,1)S(1)} %slice.287), channel_id=1, source_target_pairs={{0,2},{2,0},{4,6},{6,4},{8,10},{10,8},{12,14},{14,12},{16,18},{18,... | collective-permute-start | bytes 589832 | tf_op jit(solution)/shard_map/ppermute | solution.py:95
  119.3 19.9 %collective-permute-start.14 = (bf16[512,192]{1,0:T(8,128)(2,1)S(1)}, bf16[512,192]{1,0:T(8,128)(2,1)S(1)}, u32[]{:S(2)}, u32[]{:S(2)}) collective-permute-start(bf16[512,192]{1,0:T(8,128)(2,1)S(1)} %slice.288), channel_id=1, source_target_pairs={{0,4},{2,6},{4,0},{6,2},{8,12},{10,14},{12,8},{14,10},{16,20},{18,... | collective-permute-start | bytes 589832 | tf_op jit(solution)/shard_map/ppermute | solution.py:95
  120.1 19.6 %collective-permute-start.39 = (bf16[192,576]{0,1:T(8,128)(2,1)S(1)}, bf16[192,576]{0,1:T(8,128)(2,1)S(1)}, u32[]{:S(2)}, u32[]{:S(2)}) collective-permute-start(bf16[192,576]{0,1:T(8,128)(2,1)S(1)} %dynamic-slice_convert_fusion.9), channel_id=1, source_target_pairs={{0,16},{2,18},{4,20},{6,22},{8,24},{10,26},{12,28},{14,30},{16,0},... | collective-permute-start | bytes 663560 | tf_op jit(solution)/shard_map/ppermute | solution.py:95
  137.4 5.7 %collective-permute-start.19 = (bf16[256,192]{1,0:T(8,128)(2,1)S(1)}, bf16[256,192]{1,0:T(8,128)(2,1)S(1)}, u32[]{:S(2)}, u32[]{:S(2)}) collective-permute-start(bf16[256,192]{1,0:T(8,128)(2,1)S(1)} %slice.289), channel_id=1, source_target_pairs={{0,8},{2,10},{4,12},{6,14},{8,0},{10,2},{12,4},{14,6},{16,24},{18,... | collective-permute-start | bytes 294920 | tf_op jit(solution)/shard_map/ppermute | solution.py:95
  139.2 8.6 %collective-permute-start.15 = (bf16[256,192]{1,0:T(8,128)(2,1)S(1)}, bf16[256,192]{1,0:T(8,128)(2,1)S(1)}, u32[]{:S(2)}, u32[]{:S(2)}) collective-permute-start(bf16[256,192]{1,0:T(8,128)(2,1)S(1)} %slice.290), channel_id=1, source_target_pairs={{0,8},{2,10},{4,12},{6,14},{8,0},{10,2},{12,4},{14,6},{16,24},{18,... | collective-permute-start | bytes 294920 | tf_op jit(solution)/shard_map/ppermute | solution.py:95
  140.7 13.1 %copy-start.12 = (bf16[576,960]{1,0:T(8,128)(2,1)S(1)}, bf16[576,960]{1,0:T(8,128)(2,1)}, u32[]{:S(2)}) copy-start(bf16[576,960]{1,0:T(8,128)(2,1)} %copy-done.11) | copy-start | bytes 3317764
  140.7 13.1 %copy-start.31 = (f32[576]{0:T(1024)S(1)}, f32[576]{0:T(1024)}, u32[]{:S(2)}) copy-start(f32[576]{0:T(1024)} %copy-done.29) | copy-start | bytes 6916
  140.7 13.1 %copy-start.36 = (f32[128]{0:T(128)S(1)}, f32[128]{0:T(128)}, u32[]{:S(2)}) copy-start(f32[128]{0:T(128)} %copy-done.34) | copy-start | bytes 1540
  141.5 23.1 %collective-permute-start.40 = (bf16[96,576]{0,1:T(8,128)(2,1)}, bf16[96,576]{0,1:T(8,128)(2,1)}, u32[]{:S(2)}, u32[]{:S(2)}) collective-permute-start(bf16[96,576]{0,1:T(8,128)(2,1)} %dynamic-slice_convert_fusion.14), channel_id=1, source_target_pairs={{0,2},{2,0},{4,6},{6,4},{8,10},{10,8},{12,14},{14,12},{16,18},{18,... | collective-permute-start | bytes 331784 | tf_op jit(solution)/shard_map/ppermute | solution.py:95
  143.2 7.4 %collective-permute-start.20 = (bf16[128,192]{1,0:T(8,128)(2,1)S(1)}, bf16[128,192]{1,0:T(8,128)(2,1)S(1)}, u32[]{:S(2)}, u32[]{:S(2)}) collective-permute-start(bf16[128,192]{1,0:T(8,128)(2,1)S(1)} %slice.291), channel_id=1, source_target_pairs={{0,16},{2,18},{4,20},{6,22},{8,24},{10,26},{12,28},{14,30},{16,0},... | collective-permute-start | bytes 147464 | tf_op jit(solution)/shard_map/ppermute | solution.py:95
  147.8 5.8 %collective-permute-start.16 = (bf16[128,192]{1,0:T(8,128)(2,1)S(1)}, bf16[128,192]{1,0:T(8,128)(2,1)S(1)}, u32[]{:S(2)}, u32[]{:S(2)}) collective-permute-start(bf16[128,192]{1,0:T(8,128)(2,1)S(1)} %slice.292), channel_id=1, source_target_pairs={{0,16},{2,18},{4,20},{6,22},{8,24},{10,26},{12,28},{14,30},{16,0},... | collective-permute-start | bytes 147464 | tf_op jit(solution)/shard_map/ppermute | solution.py:95
  157.5 3.8 %copy-start.6 = (f32[288,2560]{1,0:T(8,128)S(1)}, f32[288,2560]{1,0:T(8,128)}, u32[]{:S(2)}) copy-start(f32[288,2560]{1,0:T(8,128)} %convert_add_fusion.1) | copy-start | bytes 8847364
  161.1 3.5 %copy-start.18 = (f32[192,576]{0,1:T(8,128)S(1)}, f32[192,576]{0,1:T(8,128)}, u32[]{:S(2)}) copy-start(f32[192,576]{0,1:T(8,128)} %copy-done.17) | copy-start | bytes 1327108
  161.1 12.6 %collective-permute-start.21 = (bf16[288,2560]{1,0:T(8,128)(2,1)}, bf16[288,2560]{1,0:T(8,128)(2,1)}, u32[]{:S(2)}, u32[]{:S(2)}) collective-permute-start(bf16[288,2560]{1,0:T(8,128)(2,1)} %concatenate.183), channel_id=1, source_target_pairs={{0,1},{1,0},{2,3},{3,2},{4,5},{5,4},{6,7},{7,6},{8,9},{9,8},{10,11... | collective-permute-start | bytes 4423688 | tf_op jit(solution)/shard_map/ppermute | solution.py:148
  165.8 6.3 %collective-permute-start.41 = (bf16[48,576]{0,1:T(8,128)(2,1)S(1)}, bf16[48,576]{0,1:T(8,128)(2,1)}, u32[]{:S(2)}, u32[]{:S(2)}) collective-permute-start(bf16[48,576]{0,1:T(8,128)(2,1)S(1)} %dynamic-slice_convert_fusion.13), channel_id=1, source_target_pairs={{0,4},{2,6},{4,0},{6,2},{8,12},{10,14},{12,8},{14,10},{16,20},{18,... | collective-permute-start | bytes 165896 | tf_op jit(solution)/shard_map/ppermute | solution.py:95
  173.3 6.6 %collective-permute-start.42 = (bf16[48,576]{0,1:T(8,128)(2,1)S(1)}, bf16[48,576]{0,1:T(8,128)(2,1)S(1)}, u32[]{:S(2)}, u32[]{:S(2)}) collective-permute-start(bf16[48,576]{0,1:T(8,128)(2,1)S(1)} %add_convert_fusion), channel_id=1, source_target_pairs={{0,4},{2,6},{4,0},{6,2},{8,12},{10,14},{12,8},{14,10},{16,20},{18,... | collective-permute-start | bytes 165896 | tf_op jit(solution)/shard_map/ppermute | solution.py:95
  175.5 20.1 %collective-permute-start.22 = (bf16[144,2560]{1,0:T(8,128)(2,1)S(1)}, bf16[144,2560]{1,0:T(8,128)(2,1)S(1)}, u32[]{:S(2)}, u32[]{:S(2)}) collective-permute-start(bf16[144,2560]{1,0:T(8,128)(2,1)S(1)} %dynamic-slice_convert_fusion.3), channel_id=1, source_target_pairs={{0,4},{2,6},{4,0},{6,2},{8,12},{10,14},{12,8},{14,10},{16,20},{18,... | collective-permute-start | bytes 2211848 | tf_op jit(solution)/shard_map/ppermute | solution.py:95
  180.0 5.2 %collective-permute-start.43 = (bf16[96,576]{0,1:T(8,128)(2,1)S(1)}, bf16[96,576]{0,1:T(8,128)(2,1)S(1)}, u32[]{:S(2)}, u32[]{:S(2)}) collective-permute-start(bf16[96,576]{0,1:T(8,128)(2,1)S(1)} %maximum_select_fusion.13), channel_id=1, source_target_pairs={{0,2},{2,0},{4,6},{6,4},{8,10},{10,8},{12,14},{14,12},{16,18},{18,... | collective-permute-start | bytes 331784 | tf_op jit(solution)/shard_map/ppermute | solution.py:95
  180.1 22.2 %collective-permute-start.31 = (bf16[72,2560]{1,0:T(8,128)(2,1)S(1)}, bf16[72,2560]{1,0:T(8,128)(2,1)S(1)}, u32[]{:S(2)}, u32[]{:S(2)}) collective-permute-start(bf16[72,2560]{1,0:T(8,128)(2,1)S(1)} %dynamic-slice_convert_fusion.5), channel_id=1, source_target_pairs={{0,4},{2,6},{4,0},{6,2},{8,12},{10,14},{12,8},{14,10},{16,20},{18,... | collective-permute-start | bytes 1105928 | tf_op jit(solution)/shard_map/ppermute | solution.py:95
  185.5 50.5 %collective-permute-start.44 = (bf16[192,576]{0,1:T(8,128)(2,1)S(1)}, bf16[192,576]{0,1:T(8,128)(2,1)S(1)}, u32[]{:S(2)}, u32[]{:S(2)}) collective-permute-start(bf16[192,576]{0,1:T(8,128)(2,1)S(1)} %maximum_select_fusion.10), channel_id=1, source_target_pairs={{0,16},{2,18},{4,20},{6,22},{8,24},{10,26},{12,28},{14,30},{16,0},... | collective-permute-start | bytes 663560 | tf_op jit(solution)/shard_map/ppermute | solution.py:95
  195.9 8.2 %collective-permute-start.23 = (bf16[72,2560]{1,0:T(8,128)(2,1)S(1)}, bf16[72,2560]{1,0:T(8,128)(2,1)S(1)}, u32[]{:S(2)}, u32[]{:S(2)}) collective-permute-start(bf16[72,2560]{1,0:T(8,128)(2,1)S(1)} %dynamic-slice_convert_fusion.6), channel_id=1, source_target_pairs={{0,2},{2,0},{4,6},{6,4},{8,10},{10,8},{12,14},{14,12},{16,18},{18,... | collective-permute-start | bytes 1105928 | tf_op jit(solution)/shard_map/ppermute | solution.py:95
  202.4 8.5 %collective-permute-start.32 = (bf16[72,1280]{1,0:T(8,128)(2,1)S(1)}, bf16[72,1280]{1,0:T(8,128)(2,1)S(1)}, u32[]{:S(2)}, u32[]{:S(2)}) collective-permute-start(bf16[72,1280]{1,0:T(8,128)(2,1)S(1)} %dynamic-slice_convert_fusion.11), channel_id=1, source_target_pairs={{0,8},{2,10},{4,12},{6,14},{8,0},{10,2},{12,4},{14,6},{16,24},{18,... | collective-permute-start | bytes 552968 | tf_op jit(solution)/shard_map/ppermute | solution.py:95
  204.2 8.7 %collective-permute-start.24 = (bf16[72,1280]{1,0:T(8,128)(2,1)S(1)}, bf16[72,1280]{1,0:T(8,128)(2,1)S(1)}, u32[]{:S(2)}, u32[]{:S(2)}) collective-permute-start(bf16[72,1280]{1,0:T(8,128)(2,1)S(1)} %dynamic-slice_convert_fusion.12), channel_id=1, source_target_pairs={{0,8},{2,10},{4,12},{6,14},{8,0},{10,2},{12,4},{14,6},{16,24},{18,... | collective-permute-start | bytes 552968 | tf_op jit(solution)/shard_map/ppermute | solution.py:95
  211.0 8.7 %collective-permute-start.33 = (bf16[72,640]{1,0:T(8,128)(2,1)S(1)}, bf16[72,640]{1,0:T(8,128)(2,1)S(1)}, u32[]{:S(2)}, u32[]{:S(2)}) collective-permute-start(bf16[72,640]{1,0:T(8,128)(2,1)S(1)} %dynamic-slice_convert_fusion.17), channel_id=1, source_target_pairs={{0,16},{2,18},{4,20},{6,22},{8,24},{10,26},{12,28},{14,30},{16,0},... | collective-permute-start | bytes 276488 | tf_op jit(solution)/shard_map/ppermute | solution.py:95
  212.9 8.6 %collective-permute-start.25 = (bf16[72,640]{1,0:T(8,128)(2,1)S(1)}, bf16[72,640]{1,0:T(8,128)(2,1)S(1)}, u32[]{:S(2)}, u32[]{:S(2)}) collective-permute-start(bf16[72,640]{1,0:T(8,128)(2,1)S(1)} %dynamic-slice_convert_fusion.18), channel_id=1, source_target_pairs={{0,16},{2,18},{4,20},{6,22},{8,24},{10,26},{12,28},{14,30},{16,0},... | collective-permute-start | bytes 276488 | tf_op jit(solution)/shard_map/ppermute | solution.py:95
  219.7 6.6 %collective-permute-start.34 = (bf16[72,640]{1,0:T(8,128)(2,1)S(1)}, bf16[72,640]{1,0:T(8,128)(2,1)S(1)}, u32[]{:S(2)}, u32[]{:S(2)}) collective-permute-start(bf16[72,640]{1,0:T(8,128)(2,1)S(1)} %add_convert_fusion.1), channel_id=1, source_target_pairs={{0,16},{2,18},{4,20},{6,22},{8,24},{10,26},{12,28},{14,30},{16,0},... | collective-permute-start | bytes 276488 | tf_op jit(solution)/shard_map/ppermute | solution.py:95
  221.5 6.7 %collective-permute-start.26 = (bf16[72,640]{1,0:T(8,128)(2,1)S(1)}, bf16[72,640]{1,0:T(8,128)(2,1)S(1)}, u32[]{:S(2)}, u32[]{:S(2)}) collective-permute-start(bf16[72,640]{1,0:T(8,128)(2,1)S(1)} %add_convert_fusion.2), channel_id=1, source_target_pairs={{0,16},{2,18},{4,20},{6,22},{8,24},{10,26},{12,28},{14,30},{16,0},... | collective-permute-start | bytes 276488 | tf_op jit(solution)/shard_map/ppermute | solution.py:95
  226.3 6.3 %collective-permute-start.35 = (bf16[72,1280]{1,0:T(8,128)(2,1)S(1)}, bf16[72,1280]{1,0:T(8,128)(2,1)S(1)}, u32[]{:S(2)}, u32[]{:S(2)}) collective-permute-start(bf16[72,1280]{1,0:T(8,128)(2,1)S(1)} %maximum_select_fusion.12), channel_id=1, source_target_pairs={{0,8},{2,10},{4,12},{6,14},{8,0},{10,2},{12,4},{14,6},{16,24},{18,... | collective-permute-start | bytes 552968 | tf_op jit(solution)/shard_map/ppermute | solution.py:95
  228.3 6.2 %collective-permute-start.27 = (bf16[72,1280]{1,0:T(8,128)(2,1)S(1)}, bf16[72,1280]{1,0:T(8,128)(2,1)S(1)}, u32[]{:S(2)}, u32[]{:S(2)}) collective-permute-start(bf16[72,1280]{1,0:T(8,128)(2,1)S(1)} %maximum_select_fusion.11), channel_id=1, source_target_pairs={{0,8},{2,10},{4,12},{6,14},{8,0},{10,2},{12,4},{14,6},{16,24},{18,... | collective-permute-start | bytes 552968 | tf_op jit(solution)/shard_map/ppermute | solution.py:95
  232.7 7.6 %collective-permute-start.36 = (bf16[72,2560]{1,0:T(8,128)(2,1)S(1)}, bf16[72,2560]{1,0:T(8,128)(2,1)S(1)}, u32[]{:S(2)}, u32[]{:S(2)}) collective-permute-start(bf16[72,2560]{1,0:T(8,128)(2,1)S(1)} %maximum_select_fusion.9), channel_id=1, source_target_pairs={{0,4},{2,6},{4,0},{6,2},{8,12},{10,14},{12,8},{14,10},{16,20},{18,... | collective-permute-start | bytes 1105928 | tf_op jit(solution)/shard_map/ppermute | solution.py:95
  234.7 11.6 %collective-permute-start.28 = (bf16[72,2560]{1,0:T(8,128)(2,1)S(1)}, bf16[72,2560]{1,0:T(8,128)(2,1)S(1)}, u32[]{:S(2)}, u32[]{:S(2)}) collective-permute-start(bf16[72,2560]{1,0:T(8,128)(2,1)S(1)} %maximum_select_fusion.8), channel_id=1, source_target_pairs={{0,2},{2,0},{4,6},{6,4},{8,10},{10,8},{12,14},{14,12},{16,18},{18,... | collective-permute-start | bytes 1105928 | tf_op jit(solution)/shard_map/ppermute | solution.py:95
  236.4 11.1 %copy-start.28 = (f32[128,576]{0,1:T(8,128)S(1)}, f32[128,576]{0,1:T(8,128)}, u32[]{:S(2)}) copy-start(f32[128,576]{0,1:T(8,128)} %get-tuple-element.59) | copy-start | bytes 884740
  236.5 11.1 %copy-start.32 = (f32[576]{0:T(1024)S(1)}, f32[576]{0:T(1024)}, u32[]{:S(2)}) copy-start(f32[576]{0:T(1024)} %copy-done.29) | copy-start | bytes 6916
  236.5 11.1 %copy-start.37 = (f32[128]{0:T(128)S(1)}, f32[128]{0:T(128)}, u32[]{:S(2)}) copy-start(f32[128]{0:T(128)} %copy-done.34) | copy-start | bytes 1540
  236.5 12.0 %collective-permute-start.45 = (bf16[384,576]{0,1:T(8,128)(2,1)S(1)}, bf16[384,576]{0,1:T(8,128)(2,1)S(1)}, u32[]{:S(2)}, u32[]{:S(2)}) collective-permute-start(bf16[384,576]{0,1:T(8,128)(2,1)S(1)} %maximum_select_fusion.7), channel_id=1, source_target_pairs={{0,8},{2,10},{4,12},{6,14},{8,0},{10,2},{12,4},{14,6},{16,24},{18,... | collective-permute-start | bytes 1327112 | tf_op jit(solution)/shard_map/ppermute | solution.py:95
  240.4 17.4 %collective-permute-start.37 = (bf16[144,2560]{1,0:T(8,128)(2,1)S(1)}, bf16[144,2560]{1,0:T(8,128)(2,1)S(1)}, u32[]{:S(2)}, u32[]{:S(2)}) collective-permute-start(bf16[144,2560]{1,0:T(8,128)(2,1)S(1)} %maximum_select_fusion.6), channel_id=1, source_target_pairs={{0,2},{2,0},{4,6},{6,4},{8,10},{10,8},{12,14},{14,12},{16,18},{18,... | collective-permute-start | bytes 2211848 | tf_op jit(solution)/shard_map/ppermute | solution.py:95
  246.4 13.9 %collective-permute-start.29 = (bf16[144,2560]{1,0:T(8,128)(2,1)S(1)}, bf16[144,2560]{1,0:T(8,128)(2,1)S(1)}, u32[]{:S(2)}, u32[]{:S(2)}) collective-permute-start(bf16[144,2560]{1,0:T(8,128)(2,1)S(1)} %maximum_select_fusion.5), channel_id=1, source_target_pairs={{0,4},{2,6},{4,0},{6,2},{8,12},{10,14},{12,8},{14,10},{16,20},{18,... | collective-permute-start | bytes 2211848 | tf_op jit(solution)/shard_map/ppermute | solution.py:95
  (27 other events, 52.3 us)
Sparse Core Ops, SparseCore 0:
  9.6 12.7 all-gather.7
  24.0 11.2 all-gather.5
  36.8 11.2 all-gather.3

commit v5 on v2

--- a/solution.py
+++ b/solution.py
@@ -165,6 +165,17 @@
             jnp.concatenate([other, held], axis),
         )
     return held.astype(jnp.float32)
+
+
+def core_gather(block, axis):
+    if lax.axis_size("fsdp") != 2:
+        return lax.all_gather(block, "fsdp", axis=axis, tiled=True)
+    other = lax.ppermute(block, "fsdp", [(0, 1), (1, 0)])
+    return jnp.where(
+        lax.axis_index("fsdp") == 0,
+        jnp.concatenate([block, other], axis),
+        jnp.concatenate([other, block], axis),
+    )
 
 
 def sum_tree(partial, order):
@@ -362,22 +373,18 @@
 def body(
     tokens, cotangent, norm_attn, w_query, w_key, w_value, w_out, norm_ffn, w_gate, w_up, w_down
 ):
-    gathered = (
-        lax.all_gather(norm_attn, "fsdp", axis=0, tiled=True),
-        lax.all_gather(w_query, "fsdp", axis=0, tiled=True),
-        lax.all_gather(w_key, "fsdp", axis=0, tiled=True),
-        lax.all_gather(w_value, "fsdp", axis=0, tiled=True),
-        lax.all_gather(w_out, "fsdp", axis=0, tiled=True),
-        lax.all_gather(norm_ffn, "fsdp", axis=0, tiled=True),
-        lax.all_gather(w_gate, "fsdp", axis=0, tiled=True),
-        lax.all_gather(w_up, "fsdp", axis=0, tiled=True),
-        lax.all_gather(w_down, "fsdp", axis=0, tiled=True),
-    )
-    gain_attn, query_w, key_w, value_w, out_w, gain_ffn, gate_w, up_w, down_w = gathered
+    model_width = tokens.shape[2]
+    kv_width = KV_HEADS * HEAD_DIM
+    gains = core_gather(jnp.stack([norm_attn, norm_ffn]), 1)
+    gain_attn, gain_ffn = gains[0], gains[1]
+    joined_w = core_gather(jnp.concatenate([w_query, w_key, w_value], 1), 0)
+    out_w = core_gather(w_out, 0)
+    gate_w = lax.all_gather(w_gate, "fsdp", axis=0, tiled=True)
+    up_w = lax.all_gather(w_up, "fsdp", axis=0, tiled=True)
+    down_w = lax.all_gather(w_down, "fsdp", axis=0, tiled=True)
     gain_attn = gain_attn.astype(jnp.float32)
     gain_ffn = gain_ffn.astype(jnp.float32)
     local_rows = tokens.shape[1]
-    model_width = tokens.shape[2]
     groups = KV_HEADS
     repeat = HEADS // KV_HEADS
     kv_width = KV_HEADS * HEAD_DIM
@@ -388,9 +395,10 @@
     attn_in, normed_one, factor_one = norm_forward(inputs, gain_attn)
     act_one = attn_in.astype(jnp.bfloat16)
     cosine_table, sine_table = rope_tables(first_pos, local_rows, HEAD_DIM)
-    query_pre = jnp.dot(act_one, query_w, preferred_element_type=jnp.float32)
-    key_pre = jnp.dot(act_one, key_w, preferred_element_type=jnp.float32)
-    value_pre = jnp.dot(act_one, value_w, preferred_element_type=jnp.float32)
+    joined_pre = jnp.dot(act_one, joined_w, preferred_element_type=jnp.float32)
+    query_pre = joined_pre[:, :model_width]
+    key_pre = joined_pre[:, model_width : model_width + kv_width]
+    value_pre = joined_pre[:, model_width + kv_width :]
     query_matrix = rotate(
         query_pre.reshape(local_rows, HEADS, HEAD_DIM), cosine_table, sine_table
     ).astype(jnp.bfloat16)
@@ -462,11 +470,8 @@
     grad_query_w = transposed_times(act_one, grad_query_pre)
     grad_key_w = transposed_times(act_one, grad_key_pre)
     grad_value_w = transposed_times(act_one, grad_value_pre)
-    grad_act_one = (
-        times_transposed(grad_query_pre, query_w)
-        + times_transposed(grad_key_pre, key_w)
-        + times_transposed(grad_value_pre, value_w)
-    )
+    grad_joined_pre = jnp.concatenate([grad_query_pre, grad_key_pre, grad_value_pre], 1)
+    grad_act_one = times_transposed(grad_joined_pre, joined_w)
     back_one, grad_gain_attn = norm_backward(grad_act_one, gain_attn, normed_one, factor_one)
     grad_input = grad_residual + back_one
     shard_one = reduce_tree(

time: 271 us -> 273 us (level)
  blocking collectives: 12.1 us -> 0 us
  other arithmetic: 16.7 us -> 28.2 us
    all_gather x4 -> x0, blocking collectives: 8.98 us -> none  [the longest x1 2.5 us: body(): lax.all_gather(w_query, 'fsdp', axis=0, tiled=True)]
    concatenate x6, other arithmetic: 0.3 us -> 5.43 us  [gather_tree(): held = jnp.concatenate([held, swap(held, bit)], 0)]
    add x7, other arithmetic: 0.44 us -> 4.13 us  [scatter_tree(): held[:half]]
    unnamed x1 -> x0, blocking collectives: 3.13 us -> none
    dot_general x7 -> x5, matrix products: 6.89 us -> 8.09 us  [times_transposed(): lax.dot_general(left, right, (((1,), (1,)), ((), ())), preferred_element_...]
    unnamed x114 -> x92, local copies, waits for them, and re-layouts: 8.92 us -> 9.19 us
  transfers between devices with their start and end apart: 69 -> 72, of which waited for: 30 -> 36; matrix products, arithmetic and copies ran while one was open for 16% -> 22% of each run, Pallas kernels for 3% -> 3%
where the time goes in v5:
time: 273 us; the launch traced here: 271 us
  starting transfers between devices  82.9 us (30%)
  waiting for transfers between devices  70.4 us (26%)
  local copies, waits for them, and re-layouts  28.7 us (11%)
  other arithmetic  28.2 us (10%)
  matrix products  26.2 us (10%)
  Pallas kernels  19.8 us (7%)
  between operations  15.2 us (6%)
    ppermute x60, starting transfers between devices, swap(): lax.ppermute(values, 'ctx', [(i, i ^ 1 << bit) for i in range(count)])  80.9 us
    ppermute x60, waiting for transfers between devices, swap(): lax.ppermute(values, 'ctx', [(i, i ^ 1 << bit) for i in range(count)])  67.6 us
    pallas_call x1, Pallas kernels, attention_backward(): pl.pallas_call(backward_kernel, grid=(all_keys.shape[0] // keys,), in_spe...  10.7 us
    unnamed x92, local copies, waits for them, and re-layouts  9.19 us
    pallas_call x1, Pallas kernels, attention_forward(): pl.pallas_call(forward_kernel, grid=(all_keys.shape[0] // keys,), in_spec...  9.15 us
    dot_general x5, matrix products, times_transposed(): lax.dot_general(left, right, (((1,), (1,)), ((), ())), preferred_element_...  8.09 us
    dot_general x7, matrix products, transposed_times(): lax.dot_general(left, right, (((0,), (0,)), ((), ())), preferred_element_...  7.88 us
    convert_element_type x3, local copies, waits for them, and re-layouts, core_half(): lax.dynamic_slice_in_dim(partial, other * rows, rows, 0)  6.08 us
  transfers between devices with their start and end apart: 72, of which 36 were waited for; matrix products, arithmetic and copies ran while one was open for 22% of the time, Pallas kernels for 3%

profile of v5, /device:TPU:0, one launch (start us, length us, event | category | flops | bytes accessed | tf_op | source)
XLA Modules:
  0.0 271.4 jit_solution(1826676855128809100)
XLA Ops:
  11.7 1.9 maximum_select_fusion
  15.3 4.0 %collective-permute-start.2 = (bf16[128,192]{1,0:T(8,128)(2,1)S(1)}, bf16[128,192]{1,0:T(8,128)(2,1)}, u32[]{:S(2)}, u32[]{:S(2)}) collective-permute-start(bf16[128,192]{1,0:T(8,128)(2,1)S(1)} %copy.50), channel_id=1, source_target_pairs={{0,16},{2,18},{4,20},{6,22},{8,24},{10,26},{12,28},{14,30},{16,0},... | collective-permute-start | bytes 147464 | tf_op jit(solution)/shard_map/ppermute | solution.py:95
  24.5 2.0 collective-permute-start.3
  29.7 4.0 %collective-permute-done.7 = bf16[256,192]{1,0:T(8,128)(2,1)S(1)} collective-permute-done((bf16[256,192]{1,0:T(8,128)(2,1)S(1)}, bf16[256,192]{1,0:T(8,128)(2,1)S(1)}, u32[]{:S(2)}, u32[]{:S(2)}) %collective-permute-start.7) | collective-permute-done | bytes 98336 | tf_op jit(solution)/shard_map/ppermute | solution.py:95
  34.6 1.5 collective-permute-start.8
  37.9 1.6 collective-permute-start.4
  39.4 1.6 collective-permute-done.8
  42.0 1.5 collective-permute-start.9
  43.6 3.6 %collective-permute-done.4 = bf16[512,192]{1,0:T(8,128)(2,1)S(1)} collective-permute-done((bf16[512,192]{1,0:T(8,128)(2,1)S(1)}, bf16[512,192]{1,0:T(8,128)(2,1)S(1)}, u32[]{:S(2)}, u32[]{:S(2)}) %collective-permute-start.4) | collective-permute-done | bytes 196640 | tf_op jit(solution)/shard_map/ppermute | solution.py:95
  48.2 7.2 %collective-permute-done.9 = bf16[1024,192]{1,0:T(8,128)(2,1)S(1)} collective-permute-done((bf16[1024,192]{1,0:T(8,128)(2,1)S(1)}, bf16[1024,192]{1,0:T(8,128)(2,1)S(1)}, u32[]{:S(2)}, u32[]{:S(2)}) %collective-permute-start.9) | collective-permute-done | bytes 393248 | tf_op jit(solution)/shard_map/ppermute | solution.py:95
  55.4 1.9 collective-permute-done.5
  57.4 9.2 %shard_map.194 = (f32[128,576]{1,0:T(8,128)S(1)}, f32[3,384]{1,0:T(4,128)S(1)}) custom-call(s32[1]{0:T(128)} %bitcast.1.first_ref, s32[2048,1]{1,0:T(8,128)S(1)} %copy.52.place_ref, bf16[128,576]{1,0:T(8,128)(2,1)S(1)} %copy.53.query_ref, bf16[2048,192]{1,0:T(8,128)(2,1)S(1)} %constant_dynamic-update-slice_fusion.key_ref, ...), custom_call_target="tpu_custom_call" | custom-call | tf_op jit(solution)/shard_map/pallas_call | solution.py:316
  67.3 1.9 multiply_reduce_fusion.2
  70.0 2.9 %fusion.41 = f32[128,1536]{1,0:T(8,128)} fusion(bf16[1536,576]{0,1:T(8,128)(2,1)} %all-gather.8.cloned.1.call-done, bf16[1,128,576]{1,2,0:T(8,128)(2,1)} %param.12), kind=kOutput, calls=%fused_computation.135 | convolution fusion | flops 226492416 | bytes 2703360 | tf_op jit(solution)/shard_map/dot_general | solution.py:61
  73.0 2.9 %fusion.77 = f32[128,1536]{1,0:T(8,128)} fusion(bf16[128,576]{0,1:T(8,128)(2,1)S(1)} %multiply_convert_fusion.3, bf16[576,1536]{1,0:T(8,128)(2,1)} %all-gather.6.cloned.1.call-done), kind=kOutput, calls=%fused_computation.233 | convolution fusion | flops 226492416 | bytes 2703360 | tf_op jit(solution)/shard_map/dot_general | solution.py:428
  75.8 3.5 %multiply_convert_fusion = (bf16[128,1536]{1,0:T(8,128)(2,1)S(1)}, bf16[128,1536]{1,0:T(8,128)(2,1)S(1)}, bf16[128,1536]{1,0:T(8,128)(2,1)}) fusion(f32[128,1536]{1,0:T(8,128)} %fusion.41, f32[128,1536]{1,0:T(8,128)} %fusion.77, bf16[128,576]{0,1:T(8,128)(2,1)S(1)} %multiply_convert_fusion.3, bf16[576,1536]{1,0:T(8,128)(2,1)} %all-gather.4.cloned.1.call-done), kind=kOutput, calls=%fused_computation.43 | convolution fusion | flops 229441536 | bytes 4669440 | tf_op jit(solution)/shard_map/dot_general | solution.py:427
  79.3 2.4 fusion.79
  81.7 2.4 fusion.80
  86.7 1.5 fusion.44
  88.2 2.4 convolution_convert_fusion
  92.7 10.7 %shard_map.195 = (f32[128,576]{1,0:T(8,128)S(1)}, bf16[2048,192]{1,0:T(8,128)(2,1)S(1)}, bf16[2048,192]{1,0:T(8,128)(2,1)S(1)}) custom-call(s32[1]{0:T(128)} %bitcast.1.first_ref, s32[2048,1]{1,0:T(8,128)S(1)} %copy.52.place_ref, bf16[128,576]{1,0:T(8,128)(2,1)S(1)} %copy.53.query_ref, bf16[128,576]{1,0:T(8,128)(2,1)S(1)} %copy.56.grad_ref, ...), custom_call_target="tpu_custom_call" | custom-call | tf_op jit(solution)/shard_map/pallas_call | solution.py:345
  103.5 1.6 collective-permute-start.15
  106.1 2.5 dynamic-slice_convert_fusion.2
  108.6 2.5 dynamic-slice_convert_fusion.1
  118.0 2.1 collective-permute-start.16
  121.9 4.6 %collective-permute-done.16 = bf16[512,192]{1,0:T(8,128)(2,1)S(1)} collective-permute-done((bf16[512,192]{1,0:T(8,128)(2,1)S(1)}, bf16[512,192]{1,0:T(8,128)(2,1)S(1)}, u32[]{:S(2)}, u32[]{:S(2)}) %collective-permute-start.16) | collective-permute-done | bytes 196640 | tf_op jit(solution)/shard_map/ppermute | solution.py:95
  127.6 1.6 collective-permute-done.12
  130.1 2.4 collective-permute-done.17
  132.5 3.6 %collective-permute-start.18 = (bf16[128,192]{1,0:T(8,128)(2,1)S(1)}, bf16[128,192]{1,0:T(8,128)(2,1)S(1)}, u32[]{:S(2)}, u32[]{:S(2)}) collective-permute-start(bf16[128,192]{1,0:T(8,128)(2,1)S(1)} %slice.258), channel_id=1, source_target_pairs={{0,16},{2,18},{4,20},{6,22},{8,24},{10,26},{12,28},{14,30},{16,0},... | collective-permute-start | bytes 147464 | tf_op jit(solution)/shard_map/ppermute | solution.py:95
  136.9 2.3 collective-permute-start.14
  140.2 1.6 copy.59
  142.4 1.6 slice_add_fusion.5
  144.0 1.6 copy.58
  148.0 2.1 collective-permute-start.19
  150.1 1.6 collective-permute-done.19
  151.7 1.9 collective-permute-start.20
  153.7 1.6 collective-permute-done.20
  155.4 1.7 collective-permute-start.21
  159.1 3.0 %collective-permute-start.22 = (f32[2,576]{1,0:T(2,128)S(1)}, f32[2,576]{1,0:T(2,128)S(1)}, u32[]{:S(2)}, u32[]{:S(2)}) collective-permute-start(f32[2,576]{1,0:T(2,128)S(1)} %add.361), channel_id=1, source_target_pairs={{0,16},{2,18},{4,20},{6,22},{8,24},{10,26},{12,28},{14,30},{16,0},... | collective-permute-start | bytes 13832 | tf_op jit(solution)/shard_map/ppermute | solution.py:95
  165.6 1.6 convert_add_fusion.2
  167.3 2.1 collective-permute-start.43
  171.9 1.4 convert_add_fusion
  177.1 3.2 %collective-permute-done.43 = bf16[144,1536]{1,0:T(8,128)(2,1)S(1)} collective-permute-done((bf16[144,1536]{1,0:T(8,128)(2,1)S(1)}, bf16[144,1536]{1,0:T(8,128)(2,1)S(1)}, u32[]{:S(2)}, u32[]{:S(2)}) %collective-permute-start.43) | collective-permute-done | bytes 442400 | tf_op jit(solution)/shard_map/ppermute | solution.py:95
  180.4 1.9 collective-permute-start.44
  182.3 1.6 collective-permute-done.52
  185.6 2.7 collective-permute-start.62
  190.8 2.8 %collective-permute-done.26 = bf16[72,768]{1,0:T(8,128)(2,1)S(1)} collective-permute-done((bf16[72,768]{1,0:T(8,128)(2,1)S(1)}, bf16[72,768]{1,0:T(8,128)(2,1)S(1)}, u32[]{:S(2)}, u32[]{:S(2)}) %collective-permute-start.26) | collective-permute-done | bytes 110624 | tf_op jit(solution)/shard_map/ppermute | solution.py:95
  198.6 2.7 %collective-permute-done.62 = bf16[192,576]{0,1:T(8,128)(2,1)S(1)} collective-permute-done((bf16[192,576]{0,1:T(8,128)(2,1)S(1)}, bf16[192,576]{0,1:T(8,128)(2,1)S(1)}, u32[]{:S(2)}, u32[]{:S(2)}) %collective-permute-start.62) | collective-permute-done | bytes 221216 | tf_op jit(solution)/shard_map/ppermute | solution.py:95
  202.6 1.5 collective-permute-start.28
  204.3 1.5 collective-permute-start.37
  205.8 1.9 collective-permute-done.28
  207.7 1.5 collective-permute-start.29
  210.9 1.8 collective-permute-done.29
  214.9 2.4 collective-permute-start.39
  218.2 2.3 collective-permute-start.55
  222.0 1.6 collective-permute-start.31
  225.4 2.3 collective-permute-start.56
  232.3 2.2 collective-permute-done.65
  234.7 1.7 collective-permute-start.66
  239.3 1.7 collective-permute-start.58
  243.7 4.7 %collective-permute-done.49 = bf16[72,1536]{1,0:T(8,128)(2,1)S(1)} collective-permute-done((bf16[72,1536]{1,0:T(8,128)(2,1)S(1)}, bf16[72,1536]{1,0:T(8,128)(2,1)S(1)}, u32[]{:S(2)}, u32[]{:S(2)}) %collective-permute-start.49) | collective-permute-done | bytes 221216 | tf_op jit(solution)/shard_map/ppermute | solution.py:95
  256.8 1.4 fusion.10
  258.3 1.4 fusion.11
  259.7 3.8 %collective-permute-done.68 = bf16[384,576]{0,1:T(8,128)(2,1)S(1)} collective-permute-done((bf16[384,576]{0,1:T(8,128)(2,1)S(1)}, bf16[384,576]{0,1:T(8,128)(2,1)S(1)}, u32[]{:S(2)}, u32[]{:S(2)}) %collective-permute-start.68) | collective-permute-done | bytes 442400 | tf_op jit(solution)/shard_map/ppermute | solution.py:95
  (341 shorter events, 92.3 us)
Async XLA Ops:
  7.2 62.8 %all-gather.8.cloned.1.call-start = ((), (), s32[]{:S(2)}) async-start(), calls=%async_computation.2 | async-start | bytes 2654208 | tf_op jit(solution)/shard_map/all_gather | solution.py:384
  8.0 65.0 %all-gather.6.cloned.1.call-start = ((), (), s32[]{:S(2)}) async-start(), calls=%async_computation.1 | async-start | bytes 2654208 | tf_op jit(solution)/shard_map/all_gather | solution.py:383
  8.7 67.1 %all-gather.4.cloned.1.call-start = ((), (), s32[]{:S(2)}) async-start(), calls=%async_computation | async-start | bytes 2654208 | tf_op jit(solution)/shard_map/all_gather | solution.py:382
  8.8 57.8 %collective-permute-start.10 = (bf16[288,576]{1,0:T(8,128)(2,1)}, bf16[288,576]{1,0:T(8,128)(2,1)}, u32[]{:S(2)}, u32[]{:S(2)}) collective-permute-start(bf16[288,576]{1,0:T(8,128)(2,1)} %param.17), channel_id=1, source_target_pairs={{0,1},{1,0},{2,3},{3,2},{4,5},{5,4},{6,7},{7,6},{8,9},{9,8},{10,11... | collective-permute-start | bytes 995336 | tf_op jit(solution)/shard_map/ppermute | solution.py:173
  15.3 8.4 %collective-permute-start.2 = (bf16[128,192]{1,0:T(8,128)(2,1)S(1)}, bf16[128,192]{1,0:T(8,128)(2,1)}, u32[]{:S(2)}, u32[]{:S(2)}) collective-permute-start(bf16[128,192]{1,0:T(8,128)(2,1)S(1)} %copy.50), channel_id=1, source_target_pairs={{0,16},{2,18},{4,20},{6,22},{8,24},{10,26},{12,28},{14,30},{16,0},... | collective-permute-start | bytes 147464 | tf_op jit(solution)/shard_map/ppermute | solution.py:95
  20.8 7.0 %collective-permute-start.6 = (bf16[128,192]{1,0:T(8,128)(2,1)}, bf16[128,192]{1,0:T(8,128)(2,1)}, u32[]{:S(2)}, u32[]{:S(2)}) collective-permute-start(bf16[128,192]{1,0:T(8,128)(2,1)} %copy.64), channel_id=1, source_target_pairs={{0,16},{2,18},{4,20},{6,22},{8,24},{10,26},{12,28},{14,30},{16,0},... | collective-permute-start | bytes 147464 | tf_op jit(solution)/shard_map/ppermute | solution.py:95
  24.5 12.5 %collective-permute-start.3 = (bf16[256,192]{1,0:T(8,128)(2,1)S(1)}, bf16[256,192]{1,0:T(8,128)(2,1)S(1)}, u32[]{:S(2)}, u32[]{:S(2)}) collective-permute-start(bf16[256,192]{1,0:T(8,128)(2,1)S(1)} %pad_maximum_fusion.6), channel_id=1, source_target_pairs={{0,8},{2,10},{4,12},{6,14},{8,0},{10,2},{12,4},{14,6},{16,24},{18,... | collective-permute-start | bytes 294920 | tf_op jit(solution)/shard_map/ppermute | solution.py:95
  28.7 5.0 %collective-permute-start.7 = (bf16[256,192]{1,0:T(8,128)(2,1)S(1)}, bf16[256,192]{1,0:T(8,128)(2,1)S(1)}, u32[]{:S(2)}, u32[]{:S(2)}) collective-permute-start(bf16[256,192]{1,0:T(8,128)(2,1)S(1)} %pad_maximum_fusion.7), channel_id=1, source_target_pairs={{0,8},{2,10},{4,12},{6,14},{8,0},{10,2},{12,4},{14,6},{16,24},{18,... | collective-permute-start | bytes 294920 | tf_op jit(solution)/shard_map/ppermute | solution.py:95
  34.6 6.4 %collective-permute-start.8 = (bf16[512,192]{1,0:T(8,128)(2,1)S(1)}, bf16[512,192]{1,0:T(8,128)(2,1)S(1)}, u32[]{:S(2)}, u32[]{:S(2)}) collective-permute-start(bf16[512,192]{1,0:T(8,128)(2,1)S(1)} %pad_maximum_fusion.5), channel_id=1, source_target_pairs={{0,2},{2,0},{4,6},{6,4},{8,10},{10,8},{12,14},{14,12},{16,18},{18,... | collective-permute-start | bytes 589832 | tf_op jit(solution)/shard_map/ppermute | solution.py:95
  37.9 9.2 %collective-permute-start.4 = (bf16[512,192]{1,0:T(8,128)(2,1)S(1)}, bf16[512,192]{1,0:T(8,128)(2,1)S(1)}, u32[]{:S(2)}, u32[]{:S(2)}) collective-permute-start(bf16[512,192]{1,0:T(8,128)(2,1)S(1)} %pad_maximum_fusion.4), channel_id=1, source_target_pairs={{0,4},{2,6},{4,0},{6,2},{8,12},{10,14},{12,8},{14,10},{16,20},{18,... | collective-permute-start | bytes 589832 | tf_op jit(solution)/shard_map/ppermute | solution.py:95
  42.0 13.4 %collective-permute-start.9 = (bf16[1024,192]{1,0:T(8,128)(2,1)S(1)}, bf16[1024,192]{1,0:T(8,128)(2,1)S(1)}, u32[]{:S(2)}, u32[]{:S(2)}) collective-permute-start(bf16[1024,192]{1,0:T(8,128)(2,1)S(1)} %pad_maximum_fusion.2), channel_id=1, source_target_pairs={{0,4},{2,6},{4,0},{6,2},{8,12},{10,14},{12,8},{14,10},{16,20},{18,... | collective-permute-start | bytes 1179656 | tf_op jit(solution)/shard_map/ppermute | solution.py:95
  48.0 9.2 %collective-permute-start.5 = (bf16[1024,192]{1,0:T(8,128)(2,1)S(1)}, bf16[1024,192]{1,0:T(8,128)(2,1)S(1)}, u32[]{:S(2)}, u32[]{:S(2)}) collective-permute-start(bf16[1024,192]{1,0:T(8,128)(2,1)S(1)} %pad_maximum_fusion.1), channel_id=1, source_target_pairs={{0,2},{2,0},{4,6},{6,4},{8,10},{10,8},{12,14},{14,12},{16,18},{18,... | collective-permute-start | bytes 1179656 | tf_op jit(solution)/shard_map/ppermute | solution.py:95
  103.5 13.1 %collective-permute-start.15 = (bf16[1024,192]{1,0:T(8,128)(2,1)S(1)}, bf16[1024,192]{1,0:T(8,128)(2,1)}, u32[]{:S(2)}, u32[]{:S(2)}) collective-permute-start(bf16[1024,192]{1,0:T(8,128)(2,1)S(1)} %pad_maximum_fusion.3), channel_id=1, source_target_pairs={{0,4},{2,6},{4,0},{6,2},{8,12},{10,14},{12,8},{14,10},{16,20},{18,... | collective-permute-start | bytes 1179656 | tf_op jit(solution)/shard_map/ppermute | solution.py:95
  105.1 14.9 %collective-permute-start.11 = (bf16[1024,192]{1,0:T(8,128)(2,1)S(1)}, bf16[1024,192]{1,0:T(8,128)(2,1)}, u32[]{:S(2)}, u32[]{:S(2)}) collective-permute-start(bf16[1024,192]{1,0:T(8,128)(2,1)S(1)} %slice.151), channel_id=1, source_target_pairs={{0,2},{2,0},{4,6},{6,4},{8,10},{10,8},{12,14},{14,12},{16,18},{18,... | collective-permute-start | bytes 1179656 | tf_op jit(solution)/shard_map/ppermute | solution.py:95
  108.6 57.1 %collective-permute-start.42 = (bf16[288,1536]{1,0:T(8,128)(2,1)}, bf16[288,1536]{1,0:T(8,128)(2,1)}, u32[]{:S(2)}, u32[]{:S(2)}) collective-permute-start(bf16[288,1536]{1,0:T(8,128)(2,1)} %dynamic-slice_convert_fusion.2), channel_id=1, source_target_pairs={{0,1},{1,0},{2,3},{3,2},{4,5},{5,4},{6,7},{7,6},{8,9},{9,8},{10,11... | collective-permute-start | bytes 2654216 | tf_op jit(solution)/shard_map/ppermute | solution.py:144
  111.1 58.3 %collective-permute-start.51 = (bf16[288,1536]{1,0:T(8,128)(2,1)}, bf16[288,1536]{1,0:T(8,128)(2,1)}, u32[]{:S(2)}, u32[]{:S(2)}) collective-permute-start(bf16[288,1536]{1,0:T(8,128)(2,1)} %dynamic-slice_convert_fusion.1), channel_id=1, source_target_pairs={{0,1},{1,0},{2,3},{3,2},{4,5},{5,4},{6,7},{7,6},{8,9},{9,8},{10,11... | collective-permute-start | bytes 2654216 | tf_op jit(solution)/shard_map/ppermute | solution.py:144
  113.3 58.5 %collective-permute-start.60 = (bf16[768,576]{0,1:T(8,128)(2,1)}, bf16[768,576]{0,1:T(8,128)(2,1)}, u32[]{:S(2)}, u32[]{:S(2)}) collective-permute-start(bf16[768,576]{0,1:T(8,128)(2,1)} %dynamic-slice_convert_fusion), channel_id=1, source_target_pairs={{0,1},{1,0},{2,3},{3,2},{4,5},{5,4},{6,7},{7,6},{8,9},{9,8},{10,11... | collective-permute-start | bytes 2654216 | tf_op jit(solution)/shard_map/ppermute | solution.py:144
  118.0 8.6 %collective-permute-start.16 = (bf16[512,192]{1,0:T(8,128)(2,1)S(1)}, bf16[512,192]{1,0:T(8,128)(2,1)S(1)}, u32[]{:S(2)}, u32[]{:S(2)}) collective-permute-start(bf16[512,192]{1,0:T(8,128)(2,1)S(1)} %slice.254), channel_id=1, source_target_pairs={{0,2},{2,0},{4,6},{6,4},{8,10},{10,8},{12,14},{14,12},{16,18},{18,... | collective-permute-start | bytes 589832 | tf_op jit(solution)/shard_map/ppermute | solution.py:95
  121.3 8.0 %collective-permute-start.12 = (bf16[512,192]{1,0:T(8,128)(2,1)S(1)}, bf16[512,192]{1,0:T(8,128)(2,1)S(1)}, u32[]{:S(2)}, u32[]{:S(2)}) collective-permute-start(bf16[512,192]{1,0:T(8,128)(2,1)S(1)} %slice.255), channel_id=1, source_target_pairs={{0,4},{2,6},{4,0},{6,2},{8,12},{10,14},{12,8},{14,10},{16,20},{18,... | collective-permute-start | bytes 589832 | tf_op jit(solution)/shard_map/ppermute | solution.py:95
  126.6 5.9 %collective-permute-start.17 = (bf16[256,192]{1,0:T(8,128)(2,1)S(1)}, bf16[256,192]{1,0:T(8,128)(2,1)S(1)}, u32[]{:S(2)}, u32[]{:S(2)}) collective-permute-start(bf16[256,192]{1,0:T(8,128)(2,1)S(1)} %slice.256), channel_id=1, source_target_pairs={{0,8},{2,10},{4,12},{6,14},{8,0},{10,2},{12,4},{14,6},{16,24},{18,... | collective-permute-start | bytes 294920 | tf_op jit(solution)/shard_map/ppermute | solution.py:95
  129.4 6.8 %collective-permute-start.13 = (bf16[256,192]{1,0:T(8,128)(2,1)S(1)}, bf16[256,192]{1,0:T(8,128)(2,1)S(1)}, u32[]{:S(2)}, u32[]{:S(2)}) collective-permute-start(bf16[256,192]{1,0:T(8,128)(2,1)S(1)} %slice.257), channel_id=1, source_target_pairs={{0,8},{2,10},{4,12},{6,14},{8,0},{10,2},{12,4},{14,6},{16,24},{18,... | collective-permute-start | bytes 294920 | tf_op jit(solution)/shard_map/ppermute | solution.py:95
  132.5 6.7 %collective-permute-start.18 = (bf16[128,192]{1,0:T(8,128)(2,1)S(1)}, bf16[128,192]{1,0:T(8,128)(2,1)S(1)}, u32[]{:S(2)}, u32[]{:S(2)}) collective-permute-start(bf16[128,192]{1,0:T(8,128)(2,1)S(1)} %slice.258), channel_id=1, source_target_pairs={{0,16},{2,18},{4,20},{6,22},{8,24},{10,26},{12,28},{14,30},{16,0},... | collective-permute-start | bytes 147464 | tf_op jit(solution)/shard_map/ppermute | solution.py:95
  136.9 5.5 %collective-permute-start.14 = (bf16[128,192]{1,0:T(8,128)(2,1)}, bf16[128,192]{1,0:T(8,128)(2,1)}, u32[]{:S(2)}, u32[]{:S(2)}) collective-permute-start(bf16[128,192]{1,0:T(8,128)(2,1)} %slice.259), channel_id=1, source_target_pairs={{0,16},{2,18},{4,20},{6,22},{8,24},{10,26},{12,28},{14,30},{16,0},... | collective-permute-start | bytes 147464 | tf_op jit(solution)/shard_map/ppermute | solution.py:95
  153.7 21.0 %collective-permute-start.24 = (bf16[288,768]{1,0:T(8,128)(2,1)S(1)}, bf16[288,768]{1,0:T(8,128)(2,1)S(1)}, u32[]{:S(2)}, u32[]{:S(2)}) collective-permute-start(bf16[288,768]{1,0:T(8,128)(2,1)S(1)} %fusion.7), channel_id=1, source_target_pairs={{0,1},{1,0},{2,3},{3,2},{4,5},{5,4},{6,7},{7,6},{8,9},{9,8},{10,11... | collective-permute-start | bytes 1327112 | tf_op jit(solution)/shard_map/ppermute | solution.py:144
  164.8 11.1 %collective-permute-start.33 = (bf16[288,768]{1,0:T(8,128)(2,1)S(1)}, bf16[288,768]{1,0:T(8,128)(2,1)S(1)}, u32[]{:S(2)}, u32[]{:S(2)}) collective-permute-start(bf16[288,768]{1,0:T(8,128)(2,1)S(1)} %fusion.3), channel_id=1, source_target_pairs={{0,1},{1,0},{2,3},{3,2},{4,5},{5,4},{6,7},{7,6},{8,9},{9,8},{10,11... | collective-permute-start | bytes 1327112 | tf_op jit(solution)/shard_map/ppermute | solution.py:144
  167.3 13.0 %collective-permute-start.43 = (bf16[144,1536]{1,0:T(8,128)(2,1)S(1)}, bf16[144,1536]{1,0:T(8,128)(2,1)S(1)}, u32[]{:S(2)}, u32[]{:S(2)}) collective-permute-start(bf16[144,1536]{1,0:T(8,128)(2,1)S(1)} %dynamic-slice_convert_fusion.5), channel_id=1, source_target_pairs={{0,2},{2,0},{4,6},{6,4},{8,10},{10,8},{12,14},{14,12},{16,18},{18,... | collective-permute-start | bytes 1327112 | tf_op jit(solution)/shard_map/ppermute | solution.py:95
  170.8 13.1 %collective-permute-start.52 = (bf16[144,1536]{1,0:T(8,128)(2,1)S(1)}, bf16[144,1536]{1,0:T(8,128)(2,1)S(1)}, u32[]{:S(2)}, u32[]{:S(2)}) collective-permute-start(bf16[144,1536]{1,0:T(8,128)(2,1)S(1)} %dynamic-slice_convert_fusion.4), channel_id=1, source_target_pairs={{0,4},{2,6},{4,0},{6,2},{8,12},{10,14},{12,8},{14,10},{16,20},{18,... | collective-permute-start | bytes 1327112 | tf_op jit(solution)/shard_map/ppermute | solution.py:95
  173.3 12.0 %collective-permute-start.61 = (bf16[384,576]{0,1:T(8,128)(2,1)S(1)}, bf16[384,576]{0,1:T(8,128)(2,1)S(1)}, u32[]{:S(2)}, u32[]{:S(2)}) collective-permute-start(bf16[384,576]{0,1:T(8,128)(2,1)S(1)} %dynamic-slice_convert_fusion.3), channel_id=1, source_target_pairs={{0,8},{2,10},{4,12},{6,14},{8,0},{10,2},{12,4},{14,6},{16,24},{18,... | collective-permute-start | bytes 1327112 | tf_op jit(solution)/shard_map/ppermute | solution.py:95
  174.9 13.8 %collective-permute-start.25 = (bf16[144,768]{1,0:T(8,128)(2,1)S(1)}, bf16[144,768]{1,0:T(8,128)(2,1)S(1)}, u32[]{:S(2)}, u32[]{:S(2)}) collective-permute-start(bf16[144,768]{1,0:T(8,128)(2,1)S(1)} %dynamic-slice_convert_fusion.10), channel_id=1, source_target_pairs={{0,4},{2,6},{4,0},{6,2},{8,12},{10,14},{12,8},{14,10},{16,20},{18,... | collective-permute-start | bytes 663560 | tf_op jit(solution)/shard_map/ppermute | solution.py:95
  176.1 13.5 %collective-permute-start.34 = (bf16[144,768]{1,0:T(8,128)(2,1)S(1)}, bf16[144,768]{1,0:T(8,128)(2,1)S(1)}, u32[]{:S(2)}, u32[]{:S(2)}) collective-permute-start(bf16[144,768]{1,0:T(8,128)(2,1)S(1)} %dynamic-slice_convert_fusion.9), channel_id=1, source_target_pairs={{0,2},{2,0},{4,6},{6,4},{8,10},{10,8},{12,14},{14,12},{16,18},{18,... | collective-permute-start | bytes 663560 | tf_op jit(solution)/shard_map/ppermute | solution.py:95
  180.4 15.8 %collective-permute-start.44 = (bf16[72,1536]{1,0:T(8,128)(2,1)S(1)}, bf16[72,1536]{1,0:T(8,128)(2,1)S(1)}, u32[]{:S(2)}, u32[]{:S(2)}) collective-permute-start(bf16[72,1536]{1,0:T(8,128)(2,1)S(1)} %dynamic-slice_convert_fusion.8), channel_id=1, source_target_pairs={{0,4},{2,6},{4,0},{6,2},{8,12},{10,14},{12,8},{14,10},{16,20},{18,... | collective-permute-start | bytes 663560 | tf_op jit(solution)/shard_map/ppermute | solution.py:95
  184.1 13.2 %collective-permute-start.53 = (bf16[72,1536]{1,0:T(8,128)(2,1)S(1)}, bf16[72,1536]{1,0:T(8,128)(2,1)S(1)}, u32[]{:S(2)}, u32[]{:S(2)}) collective-permute-start(bf16[72,1536]{1,0:T(8,128)(2,1)S(1)} %dynamic-slice_convert_fusion.7), channel_id=1, source_target_pairs={{0,2},{2,0},{4,6},{6,4},{8,10},{10,8},{12,14},{14,12},{16,18},{18,... | collective-permute-start | bytes 663560 | tf_op jit(solution)/shard_map/ppermute | solution.py:95
  185.6 15.7 %collective-permute-start.62 = (bf16[192,576]{0,1:T(8,128)(2,1)S(1)}, bf16[192,576]{0,1:T(8,128)(2,1)S(1)}, u32[]{:S(2)}, u32[]{:S(2)}) collective-permute-start(bf16[192,576]{0,1:T(8,128)(2,1)S(1)} %dynamic-slice_convert_fusion.6), channel_id=1, source_target_pairs={{0,16},{2,18},{4,20},{6,22},{8,24},{10,26},{12,28},{14,30},{16,0},... | collective-permute-start | bytes 663560 | tf_op jit(solution)/shard_map/ppermute | solution.py:95
  189.6 5.4 %collective-permute-start.35 = (bf16[72,768]{1,0:T(8,128)(2,1)S(1)}, bf16[72,768]{1,0:T(8,128)(2,1)S(1)}, u32[]{:S(2)}, u32[]{:S(2)}) collective-permute-start(bf16[72,768]{1,0:T(8,128)(2,1)S(1)} %dynamic-slice_convert_fusion.15), channel_id=1, source_target_pairs={{0,4},{2,6},{4,0},{6,2},{8,12},{10,14},{12,8},{14,10},{16,20},{18,... | collective-permute-start | bytes 331784 | tf_op jit(solution)/shard_map/ppermute | solution.py:95
  193.6 8.9 %collective-permute-start.27 = (bf16[72,384]{1,0:T(8,128)(2,1)S(1)}, bf16[72,384]{1,0:T(8,128)(2,1)S(1)}, u32[]{:S(2)}, u32[]{:S(2)}) collective-permute-start(bf16[72,384]{1,0:T(8,128)(2,1)S(1)} %dynamic-slice_convert_fusion.20), channel_id=1, source_target_pairs={{0,8},{2,10},{4,12},{6,14},{8,0},{10,2},{12,4},{14,6},{16,24},{18,... | collective-permute-start | bytes 165896 | tf_op jit(solution)/shard_map/ppermute | solution.py:95
  195.1 9.1 %collective-permute-start.36 = (bf16[72,384]{1,0:T(8,128)(2,1)S(1)}, bf16[72,384]{1,0:T(8,128)(2,1)S(1)}, u32[]{:S(2)}, u32[]{:S(2)}) collective-permute-start(bf16[72,384]{1,0:T(8,128)(2,1)S(1)} %dynamic-slice_convert_fusion.19), channel_id=1, source_target_pairs={{0,8},{2,10},{4,12},{6,14},{8,0},{10,2},{12,4},{14,6},{16,24},{18,... | collective-permute-start | bytes 165896 | tf_op jit(solution)/shard_map/ppermute | solution.py:95
  196.3 21.0 %collective-permute-start.45 = (bf16[72,768]{1,0:T(8,128)(2,1)S(1)}, bf16[72,768]{1,0:T(8,128)(2,1)S(1)}, u32[]{:S(2)}, u32[]{:S(2)}) collective-permute-start(bf16[72,768]{1,0:T(8,128)(2,1)S(1)} %dynamic-slice_convert_fusion.14), channel_id=1, source_target_pairs={{0,8},{2,10},{4,12},{6,14},{8,0},{10,2},{12,4},{14,6},{16,24},{18,... | collective-permute-start | bytes 331784 | tf_op jit(solution)/shard_map/ppermute | solution.py:95
  197.4 20.7 %collective-permute-start.54 = (bf16[72,768]{1,0:T(8,128)(2,1)S(1)}, bf16[72,768]{1,0:T(8,128)(2,1)S(1)}, u32[]{:S(2)}, u32[]{:S(2)}) collective-permute-start(bf16[72,768]{1,0:T(8,128)(2,1)S(1)} %dynamic-slice_convert_fusion.13), channel_id=1, source_target_pairs={{0,8},{2,10},{4,12},{6,14},{8,0},{10,2},{12,4},{14,6},{16,24},{18,... | collective-permute-start | bytes 331784 | tf_op jit(solution)/shard_map/ppermute | solution.py:95
  201.7 18.8 %collective-permute-start.63 = (bf16[96,576]{0,1:T(8,128)(2,1)S(1)}, bf16[96,576]{0,1:T(8,128)(2,1)S(1)}, u32[]{:S(2)}, u32[]{:S(2)}) collective-permute-start(bf16[96,576]{0,1:T(8,128)(2,1)S(1)} %dynamic-slice_convert_fusion.12), channel_id=1, source_target_pairs={{0,2},{2,0},{4,6},{6,4},{8,10},{10,8},{12,14},{14,12},{16,18},{18,... | collective-permute-start | bytes 331784 | tf_op jit(solution)/shard_map/ppermute | solution.py:95
  202.6 5.0 %collective-permute-start.28 = (bf16[72,192]{1,0:T(8,128)(2,1)S(1)}, bf16[72,192]{1,0:T(8,128)(2,1)S(1)}, u32[]{:S(2)}, u32[]{:S(2)}) collective-permute-start(bf16[72,192]{1,0:T(8,128)(2,1)S(1)} %dynamic-slice_convert_fusion.22), channel_id=1, source_target_pairs={{0,16},{2,18},{4,20},{6,22},{8,24},{10,26},{12,28},{14,30},{16,0},... | collective-permute-start | bytes 82952 | tf_op jit(solution)/shard_map/ppermute | solution.py:95
  204.3 5.6 %collective-permute-start.37 = (bf16[72,192]{1,0:T(8,128)(2,1)S(1)}, bf16[72,192]{1,0:T(8,128)(2,1)S(1)}, u32[]{:S(2)}, u32[]{:S(2)}) collective-permute-start(bf16[72,192]{1,0:T(8,128)(2,1)S(1)} %dynamic-slice_convert_fusion.21), channel_id=1, source_target_pairs={{0,16},{2,18},{4,20},{6,22},{8,24},{10,26},{12,28},{14,30},{16,0},... | collective-permute-start | bytes 82952 | tf_op jit(solution)/shard_map/ppermute | solution.py:95
  207.7 4.9 %collective-permute-start.29 = (bf16[72,192]{1,0:T(8,128)(2,1)S(1)}, bf16[72,192]{1,0:T(8,128)(2,1)S(1)}, u32[]{:S(2)}, u32[]{:S(2)}) collective-permute-start(bf16[72,192]{1,0:T(8,128)(2,1)S(1)} %add_convert_fusion.5), channel_id=1, source_target_pairs={{0,16},{2,18},{4,20},{6,22},{8,24},{10,26},{12,28},{14,30},{16,0},... | collective-permute-start | bytes 82952 | tf_op jit(solution)/shard_map/ppermute | solution.py:95
  209.9 4.9 %collective-permute-start.38 = (bf16[72,192]{1,0:T(8,128)(2,1)S(1)}, bf16[72,192]{1,0:T(8,128)(2,1)S(1)}, u32[]{:S(2)}, u32[]{:S(2)}) collective-permute-start(bf16[72,192]{1,0:T(8,128)(2,1)S(1)} %add_convert_fusion.4), channel_id=1, source_target_pairs={{0,16},{2,18},{4,20},{6,22},{8,24},{10,26},{12,28},{14,30},{16,0},... | collective-permute-start | bytes 82952 | tf_op jit(solution)/shard_map/ppermute | solution.py:95
  212.8 9.3 %collective-permute-start.30 = (bf16[72,384]{1,0:T(8,128)(2,1)S(1)}, bf16[72,384]{1,0:T(8,128)(2,1)S(1)}, u32[]{:S(2)}, u32[]{:S(2)}) collective-permute-start(bf16[72,384]{1,0:T(8,128)(2,1)S(1)} %maximum_select_fusion.22), channel_id=1, source_target_pairs={{0,8},{2,10},{4,12},{6,14},{8,0},{10,2},{12,4},{14,6},{16,24},{18,... | collective-permute-start | bytes 165896 | tf_op jit(solution)/shard_map/ppermute | solution.py:95
  214.9 8.7 %collective-permute-start.39 = (bf16[72,384]{1,0:T(8,128)(2,1)S(1)}, bf16[72,384]{1,0:T(8,128)(2,1)S(1)}, u32[]{:S(2)}, u32[]{:S(2)}) collective-permute-start(bf16[72,384]{1,0:T(8,128)(2,1)S(1)} %maximum_select_fusion.23), channel_id=1, source_target_pairs={{0,8},{2,10},{4,12},{6,14},{8,0},{10,2},{12,4},{14,6},{16,24},{18,... | collective-permute-start | bytes 165896 | tf_op jit(solution)/shard_map/ppermute | solution.py:95
  217.4 7.2 %collective-permute-start.46 = (bf16[72,384]{1,0:T(8,128)(2,1)S(1)}, bf16[72,384]{1,0:T(8,128)(2,1)S(1)}, u32[]{:S(2)}, u32[]{:S(2)}) collective-permute-start(bf16[72,384]{1,0:T(8,128)(2,1)S(1)} %dynamic-slice_convert_fusion.18), channel_id=1, source_target_pairs={{0,16},{2,18},{4,20},{6,22},{8,24},{10,26},{12,28},{14,30},{16,0},... | collective-permute-start | bytes 165896 | tf_op jit(solution)/shard_map/ppermute | solution.py:95
  218.2 7.2 %collective-permute-start.55 = (bf16[72,384]{1,0:T(8,128)(2,1)S(1)}, bf16[72,384]{1,0:T(8,128)(2,1)S(1)}, u32[]{:S(2)}, u32[]{:S(2)}) collective-permute-start(bf16[72,384]{1,0:T(8,128)(2,1)S(1)} %dynamic-slice_convert_fusion.17), channel_id=1, source_target_pairs={{0,16},{2,18},{4,20},{6,22},{8,24},{10,26},{12,28},{14,30},{16,0},... | collective-permute-start | bytes 165896 | tf_op jit(solution)/shard_map/ppermute | solution.py:95
  220.8 6.9 %collective-permute-start.64 = (bf16[48,576]{0,1:T(8,128)(2,1)S(1)}, bf16[48,576]{0,1:T(8,128)(2,1)S(1)}, u32[]{:S(2)}, u32[]{:S(2)}) collective-permute-start(bf16[48,576]{0,1:T(8,128)(2,1)S(1)} %dynamic-slice_convert_fusion.11), channel_id=1, source_target_pairs={{0,4},{2,6},{4,0},{6,2},{8,12},{10,14},{12,8},{14,10},{16,20},{18,... | collective-permute-start | bytes 165896 | tf_op jit(solution)/shard_map/ppermute | solution.py:95
  222.0 14.4 %collective-permute-start.31 = (bf16[72,768]{1,0:T(8,128)(2,1)S(1)}, bf16[72,768]{1,0:T(8,128)(2,1)S(1)}, u32[]{:S(2)}, u32[]{:S(2)}) collective-permute-start(bf16[72,768]{1,0:T(8,128)(2,1)S(1)} %maximum_select_fusion.18), channel_id=1, source_target_pairs={{0,2},{2,0},{4,6},{6,4},{8,10},{10,8},{12,14},{14,12},{16,18},{18,... | collective-permute-start | bytes 331784 | tf_op jit(solution)/shard_map/ppermute | solution.py:95
  223.6 13.6 %collective-permute-start.40 = (bf16[72,768]{1,0:T(8,128)(2,1)S(1)}, bf16[72,768]{1,0:T(8,128)(2,1)S(1)}, u32[]{:S(2)}, u32[]{:S(2)}) collective-permute-start(bf16[72,768]{1,0:T(8,128)(2,1)S(1)} %maximum_select_fusion.19), channel_id=1, source_target_pairs={{0,4},{2,6},{4,0},{6,2},{8,12},{10,14},{12,8},{14,10},{16,20},{18,... | collective-permute-start | bytes 331784 | tf_op jit(solution)/shard_map/ppermute | solution.py:95
  224.6 5.5 %collective-permute-start.47 = (bf16[72,384]{1,0:T(8,128)(2,1)S(1)}, bf16[72,384]{1,0:T(8,128)(2,1)S(1)}, u32[]{:S(2)}, u32[]{:S(2)}) collective-permute-start(bf16[72,384]{1,0:T(8,128)(2,1)S(1)} %add_convert_fusion.3), channel_id=1, source_target_pairs={{0,16},{2,18},{4,20},{6,22},{8,24},{10,26},{12,28},{14,30},{16,0},... | collective-permute-start | bytes 165896 | tf_op jit(solution)/shard_map/ppermute | solution.py:95
  225.4 5.7 %collective-permute-start.56 = (bf16[72,384]{1,0:T(8,128)(2,1)S(1)}, bf16[72,384]{1,0:T(8,128)(2,1)S(1)}, u32[]{:S(2)}, u32[]{:S(2)}) collective-permute-start(bf16[72,384]{1,0:T(8,128)(2,1)S(1)} %add_convert_fusion.2), channel_id=1, source_target_pairs={{0,16},{2,18},{4,20},{6,22},{8,24},{10,26},{12,28},{14,30},{16,0},... | collective-permute-start | bytes 165896 | tf_op jit(solution)/shard_map/ppermute | solution.py:95
  227.8 6.7 %collective-permute-start.65 = (bf16[48,576]{0,1:T(8,128)(2,1)S(1)}, bf16[48,576]{0,1:T(8,128)(2,1)S(1)}, u32[]{:S(2)}, u32[]{:S(2)}) collective-permute-start(bf16[48,576]{0,1:T(8,128)(2,1)S(1)} %add_convert_fusion), channel_id=1, source_target_pairs={{0,4},{2,6},{4,0},{6,2},{8,12},{10,14},{12,8},{14,10},{16,20},{18,... | collective-permute-start | bytes 165896 | tf_op jit(solution)/shard_map/ppermute | solution.py:95
  230.1 8.0 %collective-permute-start.48 = (bf16[72,768]{1,0:T(8,128)(2,1)S(1)}, bf16[72,768]{1,0:T(8,128)(2,1)S(1)}, u32[]{:S(2)}, u32[]{:S(2)}) collective-permute-start(bf16[72,768]{1,0:T(8,128)(2,1)S(1)} %maximum_select_fusion.20), channel_id=1, source_target_pairs={{0,8},{2,10},{4,12},{6,14},{8,0},{10,2},{12,4},{14,6},{16,24},{18,... | collective-permute-start | bytes 331784 | tf_op jit(solution)/shard_map/ppermute | solution.py:95
  231.1 8.1 %collective-permute-start.57 = (bf16[72,768]{1,0:T(8,128)(2,1)S(1)}, bf16[72,768]{1,0:T(8,128)(2,1)S(1)}, u32[]{:S(2)}, u32[]{:S(2)}) collective-permute-start(bf16[72,768]{1,0:T(8,128)(2,1)S(1)} %maximum_select_fusion.21), channel_id=1, source_target_pairs={{0,8},{2,10},{4,12},{6,14},{8,0},{10,2},{12,4},{14,6},{16,24},{18,... | collective-permute-start | bytes 331784 | tf_op jit(solution)/shard_map/ppermute | solution.py:95
  234.7 6.3 %collective-permute-start.66 = (bf16[96,576]{0,1:T(8,128)(2,1)S(1)}, bf16[96,576]{0,1:T(8,128)(2,1)S(1)}, u32[]{:S(2)}, u32[]{:S(2)}) collective-permute-start(bf16[96,576]{0,1:T(8,128)(2,1)S(1)} %maximum_select_fusion.15), channel_id=1, source_target_pairs={{0,2},{2,0},{4,6},{6,4},{8,10},{10,8},{12,14},{14,12},{16,18},{18,... | collective-permute-start | bytes 331784 | tf_op jit(solution)/shard_map/ppermute | solution.py:95
  236.5 7.1 %collective-permute-start.32 = (bf16[144,768]{1,0:T(8,128)(2,1)S(1)}, bf16[144,768]{1,0:T(8,128)(2,1)S(1)}, u32[]{:S(2)}, u32[]{:S(2)}) collective-permute-start(bf16[144,768]{1,0:T(8,128)(2,1)S(1)} %maximum_select_fusion.11), channel_id=1, source_target_pairs={{0,4},{2,6},{4,0},{6,2},{8,12},{10,14},{12,8},{14,10},{16,20},{18,... | collective-permute-start | bytes 663560 | tf_op jit(solution)/shard_map/ppermute | solution.py:95
  237.3 13.8 %collective-permute-start.41 = (bf16[144,768]{1,0:T(8,128)(2,1)S(1)}, bf16[144,768]{1,0:T(8,128)(2,1)S(1)}, u32[]{:S(2)}, u32[]{:S(2)}) collective-permute-start(bf16[144,768]{1,0:T(8,128)(2,1)S(1)} %maximum_select_fusion.12), channel_id=1, source_target_pairs={{0,2},{2,0},{4,6},{6,4},{8,10},{10,8},{12,14},{14,12},{16,18},{18,... | collective-permute-start | bytes 663560 | tf_op jit(solution)/shard_map/ppermute | solution.py:95
  238.2 10.1 %collective-permute-start.49 = (bf16[72,1536]{1,0:T(8,128)(2,1)S(1)}, bf16[72,1536]{1,0:T(8,128)(2,1)S(1)}, u32[]{:S(2)}, u32[]{:S(2)}) collective-permute-start(bf16[72,1536]{1,0:T(8,128)(2,1)S(1)} %maximum_select_fusion.13), channel_id=1, source_target_pairs={{0,4},{2,6},{4,0},{6,2},{8,12},{10,14},{12,8},{14,10},{16,20},{18,... | collective-permute-start | bytes 663560 | tf_op jit(solution)/shard_map/ppermute | solution.py:95
  239.3 10.6 %collective-permute-start.58 = (bf16[72,1536]{1,0:T(8,128)(2,1)S(1)}, bf16[72,1536]{1,0:T(8,128)(2,1)S(1)}, u32[]{:S(2)}, u32[]{:S(2)}) collective-permute-start(bf16[72,1536]{1,0:T(8,128)(2,1)S(1)} %maximum_select_fusion.14), channel_id=1, source_target_pairs={{0,2},{2,0},{4,6},{6,4},{8,10},{10,8},{12,14},{14,12},{16,18},{18,... | collective-permute-start | bytes 663560 | tf_op jit(solution)/shard_map/ppermute | solution.py:95
  241.2 13.5 %collective-permute-start.67 = (bf16[192,576]{0,1:T(8,128)(2,1)S(1)}, bf16[192,576]{0,1:T(8,128)(2,1)S(1)}, u32[]{:S(2)}, u32[]{:S(2)}) collective-permute-start(bf16[192,576]{0,1:T(8,128)(2,1)S(1)} %maximum_select_fusion.10), channel_id=1, source_target_pairs={{0,16},{2,18},{4,20},{6,22},{8,24},{10,26},{12,28},{14,30},{16,0},... | collective-permute-start | bytes 663560 | tf_op jit(solution)/shard_map/ppermute | solution.py:95
  248.4 8.4 %collective-permute-start.50 = (bf16[144,1536]{1,0:T(8,128)(2,1)S(1)}, bf16[144,1536]{1,0:T(8,128)(2,1)S(1)}, u32[]{:S(2)}, u32[]{:S(2)}) collective-permute-start(bf16[144,1536]{1,0:T(8,128)(2,1)S(1)} %maximum_select_fusion.7), channel_id=1, source_target_pairs={{0,2},{2,0},{4,6},{6,4},{8,10},{10,8},{12,14},{14,12},{16,18},{18,... | collective-permute-start | bytes 1327112 | tf_op jit(solution)/shard_map/ppermute | solution.py:95
  249.9 8.4 %collective-permute-start.59 = (bf16[144,1536]{1,0:T(8,128)(2,1)S(1)}, bf16[144,1536]{1,0:T(8,128)(2,1)S(1)}, u32[]{:S(2)}, u32[]{:S(2)}) collective-permute-start(bf16[144,1536]{1,0:T(8,128)(2,1)S(1)} %maximum_select_fusion.8), channel_id=1, source_target_pairs={{0,4},{2,6},{4,0},{6,2},{8,12},{10,14},{12,8},{14,10},{16,20},{18,... | collective-permute-start | bytes 1327112 | tf_op jit(solution)/shard_map/ppermute | solution.py:95
  255.1 8.4 %collective-permute-start.68 = (bf16[384,576]{0,1:T(8,128)(2,1)S(1)}, bf16[384,576]{0,1:T(8,128)(2,1)S(1)}, u32[]{:S(2)}, u32[]{:S(2)}) collective-permute-start(bf16[384,576]{0,1:T(8,128)(2,1)S(1)} %maximum_select_fusion.9), channel_id=1, source_target_pairs={{0,8},{2,10},{4,12},{6,14},{8,0},{10,2},{12,4},{14,6},{16,24},{18,... | collective-permute-start | bytes 1327112 | tf_op jit(solution)/shard_map/ppermute | solution.py:95
  (49 other events, 178.5 us)
Sparse Core Ops, SparseCore 0:
  9.6 12.7 all-gather.7
  24.0 11.2 all-gather.5
  36.8 11.2 all-gather.3
